TPU v7x, 128 devices: a whole 4x4x4 slice. The times are simulated.
128 devices in a mesh: slot: 16 (over y, z), shard: 8 (over x, core).
Axes of the slice: x: 4, y: 4, z: 4, core: 2. Of those that a mesh axis runs over, the one named last changes fastest.
Arguments:
- acts: bfloat16 [16, 3072, 1024], P('slot'), may hold values from -6 to 6
- out_grads: bfloat16 [16, 3072, 7168], P('slot', None, 'shard'), may hold values from -6 to 6
- counts: int32 [16], P('slot'), may hold values from 128 to 3072, as said below
- replica_map: int32 [16], replicated, may hold values from 0 to 3, as said below
- next_map: int32 [16], replicated, may hold values from 0 to 3, as said below
- slot_weights: bfloat16 [16, 1024, 7168], P('slot', None, 'shard'), may hold values from -6 to 6
- master: float32 [4096, 7168], P('slot', 'shard'), may hold values from -6 to 6
- moment1: float32 [4096, 7168], P('slot', 'shard'), may hold values from -1.75 to 1.75
- moment2: float32 [4096, 7168], P('slot', 'shard'), may hold values from 0.05 to 2
Outputs:
- new_weights: bfloat16 [16, 1024, 7168], P('slot', None, 'shard')
- new_master: float32 [4096, 7168], P('slot', 'shard')
- new_moment1: float32 [4096, 7168], P('slot', 'shard')
- new_moment2: float32 [4096, 7168], P('slot', 'shard')
- act_grads: bfloat16 [16, 3072, 1024], P('slot', None, 'shard')
Inputs may be any that keep to these rules, and one draw needn't show every extreme that they name: `counts`: every entry is a multiple of 128; some slot has exactly 3072 and some exactly 128. `replica_map`: every expert is held by at least 2 slots and at most 8; one expert by exactly 8. `next_map`: every expert is held by at least 2 slots and at most 8; one expert by exactly 8.
All inputs are finite; a program needn't handle non-finite values.
Results may differ from a plain program's by a relative error of at most 0.017.
Values may be sent and summed in bfloat16 or wider, within the bound.
No kernel may reach another device: no remote copies, remote signals or barrier semaphores. Data moves between devices by JAX's collectives and lax.ppermute only.
A program may use at most 128 MiB of HBM per device.

v0:
```python
import jax
import jax.numpy as jnp
from jax import lax
from jax.sharding import PartitionSpec as P

beta_one = 0.9
beta_two = 0.95
learn_rate = 0.5
weight_decay = 0.1
epsilon = 1e-08
adam_step = 20


def adam_update(grad_total, master, moment1, moment2):
    new_first = beta_one * moment1 + (1.0 - beta_one) * grad_total
    new_second = beta_two * moment2 + (1.0 - beta_two) * grad_total * grad_total
    first_hat = new_first / (1.0 - beta_one**adam_step)
    second_hat = new_second / (1.0 - beta_two**adam_step)
    update = first_hat / (jnp.sqrt(second_hat) + epsilon)
    master_new = master - learn_rate * (update + weight_decay * master)
    return (master_new, new_first, new_second)


def local(acts, out_grads, counts, replica_map, next_map, slot_weights, master, moment1, moment2):
    hidden = acts[0]
    grad_out = out_grads[0]
    weight = slot_weights[0]
    tokens_here, width_ff = hidden.shape
    width_sh = grad_out.shape[1]
    unit_scale = width_ff ** (-0.5)
    index_here = lax.axis_index("slot")
    slot_count = lax.axis_size("slot")
    rows_here = master.shape[0]
    per_expert = width_ff // rows_here
    expert_count = slot_count // per_expert
    expert_here = replica_map[index_here]
    next_here = next_map[index_here]
    positions = jnp.arange(tokens_here, dtype=jnp.int32)
    masked = jnp.where((positions < counts[0])[:, None], grad_out, jnp.zeros_like(grad_out))
    grad_sum = jnp.einsum("tf,td->fd", hidden, masked, preferred_element_type=jnp.float32)
    partial_value = jnp.einsum("td,fd->tf", masked, weight, preferred_element_type=jnp.float32)
    act_grads = lax.psum_scatter(
        (partial_value * unit_scale).astype(jnp.bfloat16), "shard", scatter_dimension=1, tiled=True
    )
    slot_grad = grad_sum * unit_scale
    onehot = (jnp.arange(expert_count, dtype=jnp.int32) == expert_here).astype(jnp.float32)
    dense_term = (onehot[:, None, None] * slot_grad[None]).reshape(
        expert_count * width_ff, width_sh
    )
    summed = lax.psum_scatter(
        dense_term.astype(jnp.bfloat16), "slot", scatter_dimension=0, tiled=True
    ).astype(jnp.float32)
    master_new, new_first, new_second = adam_update(summed, master, moment1, moment2)
    fresh_rows = master_new.astype(jnp.bfloat16)
    gathered = lax.all_gather(fresh_rows, "slot", axis=0, tiled=True)
    new_weight = lax.dynamic_slice_in_dim(gathered, next_here * width_ff, width_ff, 0)
    return (new_weight[None], master_new, new_first, new_second, act_grads[None])


def solution(mesh):
    placed = (
        P("slot", None, None),
        P("slot", None, "shard"),
        P("slot"),
        P(),
        P(),
        P("slot", None, "shard"),
        P("slot", "shard"),
        P("slot", "shard"),
        P("slot", "shard"),
    )
    return jax.shard_map(
        local,
        mesh=mesh,
        in_specs=placed,
        out_specs=(
            P("slot", None, "shard"),
            P("slot", "shard"),
            P("slot", "shard"),
            P("slot", "shard"),
            P("slot", None, "shard"),
        ),
        check_vma=False,
    )
```

profile of v0, /device:TPU:0, one launch (start us, length us, event | category | flops | bytes accessed | tf_op | source)
XLA Modules:
  0.0 241.8 jit_solution(6078999625996409742)
XLA Ops:
  7.2 0.0 copy-start
  7.2 0.0 reduce-scatter.5.cloned.1.call-start
  8.0 1.2 dynamic_slice.9
  9.2 0.6 compare_convert_fusion
  9.9 0.1 broadcast_bitcast_fusion
  10.0 12.2 %multiply_bitcast_fusion = f32[1024,896]{0,1:T(8,128)} fusion(bf16[1,3072,1024]{2,1,0:T(8,128)(2,1)} %param.9, bf16[1,3072,896]{2,1,0:T(8,128)(2,1)} %param.10, pred[3072]{0:T(1024)(128)(4,1)S(1)} %iota_compare_fusion), kind=kOutput, calls=%fused_computation.8 | convolution fusion | flops 5640814592 | bytes 15469568 | tf_op jit(solution)/shard_map/tf,td->fd/dot_general | solution.py:40
  22.2 5.0 %copy.15 = f32[1024,896]{1,0:T(8,128)} copy(f32[1024,896]{0,1:T(8,128)} %multiply_bitcast_fusion) | data formatting | bytes 7340032 | tf_op jit(solution)/shard_map/mul | solution.py:45
  27.3 6.0 %fusion = bf16[4096,896]{1,0:T(8,128)(2,1)} fusion(f32[1024,896]{1,0:T(8,128)} %copy.15, f32[4096]{0:T(1024)S(1)} %bitcast.38), kind=kLoop, calls=%fused_computation.1 | loop fusion | flops 7340032 | bytes 11026432 | tf_op jit(solution)/shard_map/convert_element_type | solution.py:51
  33.2 0.0 reduce-scatter.5.cloned.1.call-update
  33.2 0.0 reduce-scatter.7.cloned.1.call-start
  33.3 0.0 copy-done
  33.3 11.1 %multiply_convert_fusion = bf16[3072,1024]{1,0:T(8,128)(2,1)} fusion(bf16[1,3072,896]{2,1,0:T(8,128)(2,1)} %param.10, pred[3072]{0:T(1024)(128)(4,1)S(1)} %iota_compare_fusion, bf16[1,1024,896]{2,1,0:T(8,128)(2,1)S(1)} %copy-done), kind=kOutput, calls=%fused_computation.2 | convolution fusion | flops 5646188544 | bytes 13634560 | tf_op jit(solution)/shard_map/td,fd->tf/dot_general | solution.py:41
  44.4 8.9 %copy.16 = bf16[3072,1024]{0,1:T(8,128)(2,1)} copy(bf16[3072,1024]{1,0:T(8,128)(2,1)} %multiply_convert_fusion) | data formatting | bytes 12582912
  53.3 0.0 reduce-scatter.7.cloned.1.call-update
  53.3 0.0 all-gather.2.cloned.1.call-start
  53.4 65.7 %reduce-scatter.5.cloned.1.call-done = bf16[256,896]{1,0:T(8,128)(2,1)} async-done(((bf16[4096,896]{1,0:T(8,128)(2,1)}), bf16[256,896]{1,0:T(8,128)(2,1)}) %reduce-scatter.5.cloned.1.call-update) | async-done | bytes 458768 | tf_op jit(solution)/shard_map/reduce_scatter | solution.py:50
  119.1 0.0 copy-done.1
  119.1 3.7 %fusion.14 = (bf16[256,896]{1,0:T(8,128)(2,1)}, f32[256,896]{1,0:T(8,128)}, f32[256,896]{1,0:T(8,128)}, f32[256,896]{1,0:T(8,128)}) fusion(f32[256,896]{1,0:T(8,128)S(1)} %copy-done.1, bf16[256,896]{1,0:T(8,128)(2,1)} %reduce-scatter.5.cloned.1.call-done, f32[256,896]{1,0:T(8,128)} %param.16, f32[256,896]{1,0:T(8,128)} %param.17), kind=kLoop, calls=%fused_computation.22 | loop fusion | flops 3899392 | bytes 6422528 | tf_op jit(solution)/shard_map/convert_element_type | solution.py:54
  122.9 0.0 all-gather.2.cloned.1.call-update
  122.9 0.6 dynamic_slice.10
  124.1 39.2 %reduce-scatter.7.cloned.1.call-done = bf16[128,3072]{1,0:T(8,128)(2,1)} async-done(((bf16[1024,3072]{1,0:T(8,128)(2,1)}), bf16[128,3072]{1,0:T(8,128)(2,1)}) %reduce-scatter.7.cloned.1.call-update) | async-done | bytes 786448
  163.4 2.3 copy.17
  165.7 66.7 %all-gather.2.cloned.1.call-done = bf16[4096,896]{1,0:T(8,128)(2,1)} async-done(((bf16[256,896]{1,0:T(8,128)(2,1)}), bf16[4096,896]{1,0:T(8,128)(2,1)}) %all-gather.2.cloned.1.call-update) | async-done | bytes 7340048 | tf_op jit(solution)/shard_map/all_gather | solution.py:55
  232.4 2.9 %dynamic-slice_bitcast_fusion = bf16[1,1024,896]{2,1,0:T(8,128)(2,1)} fusion(bf16[4096,896]{1,0:T(8,128)(2,1)} %all-gather.2.cloned.1.call-done, s32[]{:T(128)S(6)} %select_n.18), kind=kLoop, calls=%fused_computation.10 | loop fusion | bytes 3670020 | tf_op jit(solution)/shard_map/broadcast_in_dim | solution.py:57
  (5 shorter events, 0.0 us)
Async XLA Ops:
  7.2 26.1 %copy-start = (bf16[1,1024,896]{2,1,0:T(8,128)(2,1)S(1)}, bf16[1,1024,896]{2,1,0:T(8,128)(2,1)}, u32[]{:S(2)}) copy-start(bf16[1,1024,896]{2,1,0:T(8,128)(2,1)} %param.14) | copy-start | bytes 5505028
  7.2 111.9 %reduce-scatter.5.cloned.1.call-start = ((), (), s32[]{:S(2)}) async-start(), calls=%async_computation.2 | async-start | bytes 7798784 | tf_op jit(solution)/shard_map/reduce_scatter | solution.py:50
  33.2 130.1 %reduce-scatter.7.cloned.1.call-start = ((), (), s32[]{:S(2)}) async-start(), calls=%async_computation.4 | async-start | bytes 7077888
  53.3 65.8 %copy-start.1 = (f32[256,896]{1,0:T(8,128)S(1)}, f32[256,896]{1,0:T(8,128)}, u32[]{:S(2)}) copy-start(f32[256,896]{1,0:T(8,128)} %param.15) | copy-start | bytes 2752516
  53.3 69.6 %copy-start.2 = (s32[16]{0:T(128)S(1)}, s32[16]{0:T(128)}, u32[]{:S(2)}) copy-start(s32[16]{0:T(128)} %param.13) | copy-start | bytes 196
  53.3 179.1 %all-gather.2.cloned.1.call-start = ((), (), s32[]{:S(2)}) async-start(), calls=%async_computation.3 | async-start | bytes 7798784 | tf_op jit(solution)/shard_map/all_gather | solution.py:55
Sparse Core Ops, SparseCore 0:
  33.4 85.7 reduce-scatter.4
  121.7 41.6 reduce-scatter.6
  166.4 65.9 all-gather.1
where the time goes:
time: 243 us; the launch traced here: 242 us
  waiting for transfers between devices  172 us (71%)
  matrix products  23.3 us (10%)
  local copies, waits for them, and re-layouts  21 us (9%)
  between operations  15.2 us (6%)
  other arithmetic  10.3 us (4%)
    all_gather x1, waiting for transfers between devices, local(): gathered = lax.all_gather(fresh_rows, 'slot', axis=0, tiled=True)  66.7 us
    reduce_scatter x1, waiting for transfers between devices, local(): lax.psum_scatter(dense_term.astype(jnp.bfloat16), 'slot', scatter_dimensi...  65.7 us
    unnamed x4, waiting for transfers between devices  39.3 us
    dot_general x1, matrix products, local(): jnp.einsum('tf,td->fd', hidden, masked, preferred_element_type=jnp.float32)  12.2 us
    unnamed x10, local copies, waits for them, and re-layouts  11.3 us
    dot_general x1, matrix products, local(): jnp.einsum('td,fd->tf', masked, weight, preferred_element_type=jnp.float32)  11.1 us
    convert_element_type x1, other arithmetic, local(): dense_term.astype(jnp.bfloat16)  5.95 us
    mul x1, local copies, waits for them, and re-layouts, local(): slot_grad = grad_sum * unit_scale  5.04 us
  transfers between devices with their start and end apart: 3, of which 3 were waited for; matrix products, arithmetic and copies ran while one was open for 11% of the time, Pallas kernels for 0%

commit v1 on v0

v1 whole, which is shorter than its diff:
```python
import functools

import jax
import jax.numpy as jnp
from jax import lax
from jax.experimental import pallas as pl
from jax.experimental.pallas import tpu as pltpu
from jax.sharding import PartitionSpec as P

beta_one = 0.9
beta_two = 0.95
learn_rate = 0.5
weight_decay = 0.1
epsilon = 1e-08
adam_step = 20

RING = 4
CHUNKS = 2
bf16 = jnp.bfloat16
f32 = jnp.float32


def params(*semantics):
    return pltpu.CompilerParams(vmem_limit_bytes=56 << 20, dimension_semantics=semantics or None)


def shift_z(value, step):
    return lax.ppermute(value, "slot", [(RING * y + z, RING * y + (z + step) % RING) for y in range(RING) for z in range(RING)])


def shift_y(value, step):
    return lax.ppermute(value, "slot", [(RING * y + z, RING * ((y + step) % RING) + z) for y in range(RING) for z in range(RING)])


def shift_x(value, step):
    return lax.ppermute(value, "shard", [(2 * x + c, 2 * ((x + step) % RING) + c) for x in range(RING) for c in range(2)])


def swap_core(value):
    return lax.ppermute(value, "shard", [(i, i ^ 1) for i in range(2 * RING)])


def exchange(shift, pieces):
    ahead, behind, across = shift(pieces[1], 1), shift(pieces[3], -1), shift(pieces[2], 2)
    return [pieces[0], behind, across, ahead]


def slot_grads(counts, acts, out_grads, scale):
    tokens, ff = acts.shape
    width = out_grads.shape[1]
    block = 1024
    steps = tokens // block
    quarter = ff // RING
    part = quarter // CHUNKS

    def kernel(count_ref, acts_ref, grads_ref, *rest):
        outs, total = rest[:-1], rest[-1]
        step = pl.program_id(0)
        here = lax.axis_index("slot") % RING
        live = count_ref[0] - step * block
        rows = lax.broadcasted_iota(jnp.int32, (block, width), 0)
        grads = grads_ref[...]
        masked = jnp.where(rows < live, grads, jnp.zeros_like(grads))
        term = lax.dot_general(masked, acts_ref[...], (((0,), (0,)), ((), ())), preferred_element_type=f32)

        @pl.when(step == 0)
        def _():
            total[...] = term

        @pl.when(step > 0)
        def _():
            total[...] += term

        @pl.when(step == steps - 1)
        def _():
            for chunk in range(CHUNKS):
                for distance in range(RING):
                    start = ((here + distance) % RING) * quarter + chunk * part
                    columns = total[:, pl.ds(pl.multiple_of(start, part), part)]
                    outs[chunk * RING + distance][...] = (columns * scale).astype(bf16)

    pieces = pl.pallas_call(
        kernel,
        grid_spec=pltpu.PrefetchScalarGridSpec(
            num_scalar_prefetch=1,
            grid=(steps,),
            in_specs=[
                pl.BlockSpec((block, ff), lambda i, c: (i, 0)),
                pl.BlockSpec((block, width), lambda i, c: (i, 0)),
            ],
            out_specs=[pl.BlockSpec((width, part), lambda i, c: (0, 0))] * (CHUNKS * RING),
            scratch_shapes=[pltpu.VMEM((width, ff), f32)],
        ),
        out_shape=[jax.ShapeDtypeStruct((width, part), bf16)] * (CHUNKS * RING),
        compiler_params=params("arbitrary"),
        cost_estimate=pl.CostEstimate(flops=2 * tokens * ff * width, bytes_accessed=14_000_000, transcendentals=0),
        name="slot_grads",
    )(counts, acts, out_grads)
    return [pieces[chunk * RING : (chunk + 1) * RING] for chunk in range(CHUNKS)]


def act_terms(place, half, halves, out_grads, other_grads, weight, other_weight, scale):
    tokens, width = out_grads.shape
    ff = weight.shape[0]
    block = 512
    here_tokens = tokens // halves
    steps = here_tokens // block
    columns = ff // (2 * RING)
    first = half * steps

    def kernel(place_ref, grads_ref, other_ref, *rest):
        weights, outs = rest[: 2 * RING], rest[2 * RING :]
        live = place_ref[2] - (first + pl.program_id(0)) * block
        both = jnp.concatenate([grads_ref[...], other_ref[...]], axis=1)
        own = jnp.concatenate([w[...].reshape(columns, width) for w in weights[:RING]], axis=0)
        other = jnp.concatenate([w[...].reshape(columns, width) for w in weights[RING:]], axis=0)
        matrix = jnp.concatenate([own, other], axis=1)
        term = lax.dot_general(both, matrix, (((1,), (1,)), ((), ())), preferred_element_type=f32) * scale
        rows = lax.broadcasted_iota(jnp.int32, term.shape, 0)
        term = jnp.where(rows < live, term, 0.0).astype(bf16)
        for distance in range(RING):
            outs[distance][...] = term[:, distance * columns : (distance + 1) * columns]

    def rows_of(distance):
        return pl.BlockSpec((1, 1, columns, width), lambda i, p: ((p[0] + distance) % RING, p[1], 0, 0))

    split = (RING, 2, columns, width)
    return pl.pallas_call(
        kernel,
        grid_spec=pltpu.PrefetchScalarGridSpec(
            num_scalar_prefetch=1,
            grid=(steps,),
            in_specs=[pl.BlockSpec((block, width), lambda i, p: (first + i, 0))] * 2
            + [rows_of(distance) for distance in range(RING)] * 2,
            out_specs=[pl.BlockSpec((block, columns), lambda i, p: (i, 0))] * RING,
        ),
        out_shape=[jax.ShapeDtypeStruct((here_tokens, columns), bf16)] * RING,
        compiler_params=params("arbitrary"),
        cost_estimate=pl.CostEstimate(flops=2 * here_tokens * ff * width, bytes_accessed=9_000_000, transcendentals=0),
        name="act_terms",
    )(place, out_grads, other_grads, *([weight.reshape(split)] * RING), *([other_weight.reshape(split)] * RING))


def act_sum(halves):
    rows, columns = halves[0][0].shape
    count = len(halves)

    def kernel(*refs):
        ins, out = refs[:-1], refs[-1]
        for half in range(count):

            @pl.when(pl.program_id(0) == half)
            def _(half=half):
                terms = [ref[...].astype(f32) for ref in ins[half * RING : (half + 1) * RING]]
                out[...] = ((terms[0] + terms[1]) + (terms[2] + terms[3])).astype(bf16)

    return pl.pallas_call(
        kernel,
        grid=(count,),
        in_specs=[pl.BlockSpec((rows, columns), lambda i: (0, 0))] * (count * RING),
        out_specs=pl.BlockSpec((rows, columns), lambda i: (i, 0)),
        out_shape=jax.ShapeDtypeStruct((count * rows, columns), bf16),
        compiler_params=params("arbitrary"),
        cost_estimate=pl.CostEstimate(flops=4 * count * rows * columns, bytes_accessed=8_000_000, transcendentals=0),
        name="act_sum",
    )(*[piece for half in halves for piece in half])


def by_expert(replica_map, pieces):
    def kernel(map_ref, *refs):
        ins, outs = refs[:RING], refs[RING:]
        slot = lax.axis_index("slot")
        y, z = slot // RING, slot % RING
        values = [ref[...].astype(f32) for ref in ins]
        held = [map_ref[RING * y + (z + distance) % RING] for distance in range(RING)]
        for step in range(RING):
            expert = (y + step) % RING
            total = jnp.where(held[0] == expert, values[0], 0.0)
            for value, one in zip(values[1:], held[1:]):
                total = total + jnp.where(one == expert, value, 0.0)
            outs[step][...] = total.astype(bf16)

    shape = pieces[0].shape
    return pl.pallas_call(
        kernel,
        grid_spec=pltpu.PrefetchScalarGridSpec(
            num_scalar_prefetch=1,
            grid=(1,),
            in_specs=[pl.BlockSpec(shape, lambda i, m: (0, 0))] * RING,
            out_specs=[pl.BlockSpec(shape, lambda i, m: (0, 0))] * RING,
        ),
        out_shape=[jax.ShapeDtypeStruct(shape, bf16)] * RING,
        compiler_params=params("arbitrary"),
        cost_estimate=pl.CostEstimate(flops=1_000_000, bytes_accessed=2_000_000, transcendentals=0),
        name="by_expert",
    )(replica_map, *pieces)


def adam_update(grad_total, master, moment1, moment2):
    new_first = beta_one * moment1 + (1.0 - beta_one) * grad_total
    new_second = beta_two * moment2 + (1.0 - beta_two) * grad_total * grad_total
    first_hat = new_first / (1.0 - beta_one**adam_step)
    second_hat = new_second / (1.0 - beta_two**adam_step)
    update = first_hat / (jnp.sqrt(second_hat) + epsilon)
    master_new = master - learn_rate * (update + weight_decay * master)
    return (master_new, new_first, new_second)


def adam(chunk, pieces, state, earlier):
    rows, width = state[0].shape
    part = rows // CHUNKS

    def kernel(*refs):
        terms = [ref[...].astype(f32) for ref in refs[:RING]]
        master, moment1, moment2 = refs[RING : RING + 3]
        outs = refs[-4:]
        grad = ((terms[0] + terms[1]) + (terms[2] + terms[3])).T
        master_new, new_first, new_second = adam_update(grad, master[...], moment1[...], moment2[...])
        outs[0][...] = master_new
        outs[1][...] = new_first
        outs[2][...] = new_second
        outs[3][...] = master_new.astype(bf16)

    whole = jax.ShapeDtypeStruct((rows, width), f32)
    mine = pl.BlockSpec((part, width), lambda i: (chunk, 0))
    return pl.pallas_call(
        kernel,
        grid=(1,),
        in_specs=[pl.BlockSpec((width, part), lambda i: (0, 0))] * RING
        + [mine] * 3
        + [pl.BlockSpec(memory_space=pl.ANY)] * len(earlier),
        out_specs=[mine] * 3 + [pl.BlockSpec((part, width), lambda i: (0, 0))],
        out_shape=[whole] * 3 + [jax.ShapeDtypeStruct((part, width), bf16)],
        input_output_aliases={RING + 3 + i: i for i in range(len(earlier))},
        compiler_params=params("arbitrary"),
        cost_estimate=pl.CostEstimate(flops=2_000_000, bytes_accessed=4_000_000, transcendentals=rows * width),
        name="adam",
    )(*pieces, *state, *earlier)


def by_slot(next_map, pieces):
    def kernel(map_ref, *refs):
        ins, outs = refs[:RING], refs[RING:]
        slot = lax.axis_index("slot")
        y, z = slot // RING, slot % RING
        for distance in range(RING):
            wanted = (map_ref[RING * y + (z + distance) % RING] - y + RING) % RING
            for step in range(RING):

                @pl.when(wanted == step)
                def _(step=step, distance=distance):
                    outs[distance][...] = ins[step][...]

    shape = pieces[0].shape
    return pl.pallas_call(
        kernel,
        grid_spec=pltpu.PrefetchScalarGridSpec(
            num_scalar_prefetch=1,
            grid=(1,),
            in_specs=[pl.BlockSpec(shape, lambda i, m: (0, 0))] * RING,
            out_specs=[pl.BlockSpec(shape, lambda i, m: (0, 0))] * RING,
        ),
        out_shape=[jax.ShapeDtypeStruct(shape, bf16)] * RING,
        compiler_params=params("arbitrary"),
        cost_estimate=pl.CostEstimate(flops=0, bytes_accessed=2_000_000, transcendentals=0),
        name="by_slot",
    )(next_map, *pieces)


def put_rows(place, chunk, pieces, ff, earlier):
    part, width = pieces[0].shape

    def kernel(place_ref, *refs):
        out = refs[-1]
        for distance in range(RING):

            @pl.when(pl.program_id(0) == distance)
            def _(distance=distance):
                out[...] = refs[distance][...]

    return pl.pallas_call(
        kernel,
        grid_spec=pltpu.PrefetchScalarGridSpec(
            num_scalar_prefetch=1,
            grid=(RING,),
            in_specs=[pl.BlockSpec((part, width), lambda i, p: (0, 0))] * RING
            + [pl.BlockSpec(memory_space=pl.ANY)] * len(earlier),
            out_specs=pl.BlockSpec((part, width), lambda i, p: (((p[3] + i) % RING) * CHUNKS + chunk, 0)),
        ),
        out_shape=jax.ShapeDtypeStruct((ff, width), bf16),
        input_output_aliases={1 + RING: 0} if earlier else {},
        compiler_params=params("arbitrary"),
        cost_estimate=pl.CostEstimate(flops=0, bytes_accessed=2_000_000, transcendentals=0),
        name="put_rows",
    )(place, *pieces, *earlier)


def local(acts, out_grads, counts, replica_map, next_map, slot_weights, master, moment1, moment2):
    hidden, grads, weight = acts[0], out_grads[0], slot_weights[0]
    ff = hidden.shape[1]
    scale = ff**-0.5
    slot, shard = lax.axis_index("slot"), lax.axis_index("shard")
    place = jnp.stack([shard // 2, shard % 2, counts[0], slot % RING]).astype(jnp.int32)

    other_weight, other_grads = swap_core(weight), swap_core(grads)
    by_chunk = slot_grads(counts, hidden, grads, scale)
    along_z = [exchange(shift_z, pieces) for pieces in by_chunk]

    halves = []
    for half in range(2):
        terms = act_terms(place, half, 2, grads, other_grads, weight, other_weight, scale)
        halves.append(exchange(shift_x, terms))

    along_y = [exchange(shift_y, by_expert(replica_map, pieces)) for pieces in along_z]
    state = ()
    fresh = []
    for chunk, pieces in enumerate(along_y):
        *state, rows = adam(chunk, pieces, (master, moment1, moment2), tuple(state))
        fresh.append(exchange(shift_y, [rows] * RING))
    wanted = [exchange(shift_z, by_slot(next_map, pieces)) for pieces in fresh]
    new_weight = ()
    for chunk, pieces in enumerate(wanted):
        new_weight = (put_rows(place, chunk, pieces, ff, new_weight),)
    act_grads = act_sum(halves)
    return (new_weight[0][None], *state, act_grads[None])


def solution(mesh):
    placed = (
        P("slot", None, None),
        P("slot", None, "shard"),
        P("slot"),
        P(),
        P(),
        P("slot", None, "shard"),
        P("slot", "shard"),
        P("slot", "shard"),
        P("slot", "shard"),
    )
    return jax.shard_map(
        local,
        mesh=mesh,
        in_specs=placed,
        out_specs=(
            P("slot", None, "shard"),
            P("slot", "shard"),
            P("slot", "shard"),
            P("slot", "shard"),
            P("slot", None, "shard"),
        ),
        check_vma=False,
    )
```

time: 243 us -> 151 us (0.62)
  waiting for transfers between devices: 172 us -> 40.8 us
  Pallas kernels: 0 us -> 55.4 us
  starting transfers between devices: 0.12 us -> 48.9 us
  matrix products: 23.3 us -> 0 us
  local copies, waits for them, and re-layouts: 21 us -> 2.89 us
  between operations: 15.2 us -> 1.51 us
  other arithmetic: 10.3 us -> 0.61 us
    all_gather x1 -> x0, waiting for transfers between devices: 66.7 us -> none  [local(): gathered = lax.all_gather(fresh_rows, 'slot', axis=0, tiled=True)]
    reduce_scatter x1 -> x0, waiting for transfers between devices: 65.7 us -> none  [local(): lax.psum_scatter(dense_term.astype(jnp.bfloat16), 'slot', scatter_dimensi...]
    pallas_call x0 -> x12, Pallas kernels: none -> 55.4 us  [the longest x2 15.1 us: act_terms(): pl.pallas_call(kernel, grid_spec=pltpu.PrefetchScalarGridSpec(num_scalar_...]
    ppermute x0 -> x32, starting transfers between devices: none -> 48.9 us  [the longest x12 21.2 us: shift_y(): lax.ppermute(value, 'slot', [(RING * y + z, RING * ((y + step) % RING) +...]
    ppermute x0 -> x32, waiting for transfers between devices: none -> 40.8 us  [the longest x6 19.4 us: shift_x(): lax.ppermute(value, 'shard', [(2 * x + c, 2 * ((x + step) % RING) + c) fo...]
    unnamed x4 -> x0, waiting for transfers between devices: 39.3 us -> none
    dot_general x2 -> x0, matrix products: 23.3 us -> none  [the longest x1 12.2 us: local(): jnp.einsum('tf,td->fd', hidden, masked, preferred_element_type=jnp.float32)]
    convert_element_type x3 -> x0, other arithmetic: 10.3 us -> none  [the longest x1 5.95 us: local(): dense_term.astype(jnp.bfloat16)]
  transfers between devices with their start and end apart: 3 -> 32, of which waited for: 3 -> 12; matrix products, arithmetic and copies ran while one was open for 11% -> 0% of each run, Pallas kernels for 0% -> 35%
where the time goes in v1:
time: 151 us; the launch traced here: 150 us
  Pallas kernels  55.4 us (37%)
  starting transfers between devices  48.9 us (32%)
  waiting for transfers between devices  40.8 us (27%)
  local copies, waits for them, and re-layouts  2.89 us (2%)
  between operations  1.51 us (1%)
    ppermute x12, starting transfers between devices, shift_y(): lax.ppermute(value, 'slot', [(RING * y + z, RING * ((y + step) % RING) +...  21.2 us
    ppermute x6, waiting for transfers between devices, shift_x(): lax.ppermute(value, 'shard', [(2 * x + c, 2 * ((x + step) % RING) + c) fo...  19.4 us
    ppermute x12, starting transfers between devices, shift_z(): lax.ppermute(value, 'slot', [(RING * y + z, RING * y + (z + step) % RING)...  18.5 us
    pallas_call x2, Pallas kernels, act_terms(): pl.pallas_call(kernel, grid_spec=pltpu.PrefetchScalarGridSpec(num_scalar_...  15.1 us
    ppermute x12, waiting for transfers between devices, shift_z(): lax.ppermute(value, 'slot', [(RING * y + z, RING * y + (z + step) % RING)...  14.5 us
    pallas_call x1, Pallas kernels, slot_grads(): pl.pallas_call(kernel, grid_spec=pltpu.PrefetchScalarGridSpec(num_scalar_...  11.2 us
    ppermute x6, starting transfers between devices, shift_x(): lax.ppermute(value, 'shard', [(2 * x + c, 2 * ((x + step) % RING) + c) fo...  8.53 us
    pallas_call x2, Pallas kernels, put_rows(): pl.pallas_call(kernel, grid_spec=pltpu.PrefetchScalarGridSpec(num_scalar_...  7 us
  transfers between devices with their start and end apart: 32, of which 12 were waited for; matrix products, arithmetic and copies ran while one was open for 0% of the time, Pallas kernels for 35%

profile of v1, /device:TPU:0, one launch (start us, length us, event | category | flops | bytes accessed | tf_op | source)
XLA Modules:
  0.0 150.1 jit_solution(13346562051763079241)
XLA Ops:
  1.9 11.2 %slot_grads.1 = (bf16[896,128]{1,0:T(8,128)(2,1)}, bf16[896,128]{1,0:T(8,128)(2,1)}, bf16[896,128]{1,0:T(8,128)(2,1)}, bf16[896,128]{1,0:T(8,128)(2,1)}, bf16[89...) custom-call(s32[1]{0:T(128)S(6)} %copy.22.count_ref, ...), custom_call_target="tpu_custom_call" | custom-call | flops 5637144576 | bytes 14000000 | tf_op jit(solution)/shard_map/slot_grads/pallas_call | solution.py:82
  13.0 4.1 %collective-permute-start.6 = (bf16[896,128]{1,0:T(8,128)(2,1)}, bf16[896,128]{1,0:T(8,128)(2,1)S(1)}, u32[]{:S(2)}, u32[]{:S(2)}) collective-permute-start(bf16[896,128]{1,0:T(8,128)(2,1)} %get-tuple-element.54), channel_id=1, source_target_pairs={{0,24},{8,0},{16,8},{24,16},{32,56},{40,32},{48,40},{56,48},{64,88... | collective-permute-start | bytes 688136 | tf_op jit(solution)/shard_map/ppermute | solution.py:28
  18.4 9.1 %collective-permute-done.6.refs_1_ = bf16[896,128]{1,0:T(8,128)(2,1)S(1)} collective-permute-done((bf16[896,128]{1,0:T(8,128)(2,1)}, bf16[896,128]{1,0:T(8,128)(2,1)S(1)}, u32[]{:S(2)}, u32[]{:S(2)}) %collective-permute-start.6) | collective-permute-done | bytes 229408 | tf_op jit(solution)/shard_map/ppermute | solution.py:28
  27.5 3.6 %collective-permute-start = (bf16[896,128]{1,0:T(8,128)(2,1)}, bf16[896,128]{1,0:T(8,128)(2,1)S(1)}, u32[]{:S(2)}, u32[]{:S(2)}) collective-permute-start(bf16[896,128]{1,0:T(8,128)(2,1)} %get-tuple-element.46), channel_id=1, source_target_pairs={{0,24},{8,0},{16,8},{24,16},{32,56},{40,32},{48,40},{56,48},{64,88... | collective-permute-start | bytes 688136 | tf_op jit(solution)/shard_map/ppermute | solution.py:28
  32.1 3.2 %by_expert.3 = (bf16[896,128]{1,0:T(8,128)(2,1)}, bf16[896,128]{1,0:T(8,128)(2,1)}, bf16[896,128]{1,0:T(8,128)(2,1)}, bf16[896,128]{1,0:T(8,128)(2,1)}) custom-call(s32[16]{0:T(128)} %map_ref.5, bf16[896,128]{1,0:T(8,128)(2,1)} %get-tuple-element.53.refs_0_, bf16[896,128]{1,0:T(8,128)(2,1)} %copy-done.22, bf16[896,128]{1,0:T(8,128)(2,1)} %copy-done.23, ...), custom_call_target="tpu_custom_call" | custom-call | flops 1000000 | bytes 2000000 | tf_op jit(solution)/shard_map/by_expert/pallas_call | solution.py:184
  35.3 5.4 %collective-permute-done.refs_1_ = bf16[896,128]{1,0:T(8,128)(2,1)S(1)} collective-permute-done((bf16[896,128]{1,0:T(8,128)(2,1)}, bf16[896,128]{1,0:T(8,128)(2,1)S(1)}, u32[]{:S(2)}, u32[]{:S(2)}) %collective-permute-start) | collective-permute-done | bytes 229408 | tf_op jit(solution)/shard_map/ppermute | solution.py:28
  40.6 3.2 %collective-permute-start.10 = (bf16[896,128]{1,0:T(8,128)(2,1)}, bf16[896,128]{1,0:T(8,128)(2,1)S(1)}, u32[]{:S(2)}, u32[]{:S(2)}) collective-permute-start(bf16[896,128]{1,0:T(8,128)(2,1)} %get-tuple-element.59), channel_id=1, source_target_pairs={{0,64},{8,72},{16,80},{24,88},{32,96},{40,104},{48,112},{56,120},{... | collective-permute-start | bytes 688136 | tf_op jit(solution)/shard_map/ppermute | solution.py:32
  47.2 3.2 %by_expert.2 = (bf16[896,128]{1,0:T(8,128)(2,1)}, bf16[896,128]{1,0:T(8,128)(2,1)}, bf16[896,128]{1,0:T(8,128)(2,1)}, bf16[896,128]{1,0:T(8,128)(2,1)}) custom-call(s32[16]{0:T(128)} %map_ref.5, bf16[896,128]{1,0:T(8,128)(2,1)} %get-tuple-element.45.refs_0_, bf16[896,128]{1,0:T(8,128)(2,1)} %copy-done.18, bf16[896,128]{1,0:T(8,128)(2,1)} %copy-done.20, ...), custom_call_target="tpu_custom_call" | custom-call | flops 1000000 | bytes 2000000 | tf_op jit(solution)/shard_map/by_expert/pallas_call | solution.py:184
  56.4 3.3 %adam.2 = (f32[256,896]{1,0:T(8,128)}, f32[256,896]{1,0:T(8,128)}, f32[256,896]{1,0:T(8,128)}, bf16[128,896]{1,0:T(8,128)(2,1)}) custom-call(bf16[896,128]{1,0:T(8,128)(2,1)} %get-tuple-element.57.refs_0_, bf16[896,128]{1,0:T(8,128)(2,1)} %copy-done.9, bf16[896,128]{1,0:T(8,128)(2,1)} %copy-done.7, bf16[896,128]{1,0:T(8,128)(2,1)} %copy-done.8, ...), custom_call_target="tpu_custom_call" | custom-call | flops 2000000 | bytes 4000000 | tf_op jit(solution)/shard_map/adam/pallas_call | solution.py:226
  59.7 3.1 %collective-permute-done.3.refs_1_ = bf16[896,128]{1,0:T(8,128)(2,1)S(1)} collective-permute-done((bf16[896,128]{1,0:T(8,128)(2,1)}, bf16[896,128]{1,0:T(8,128)(2,1)S(1)}, u32[]{:S(2)}, u32[]{:S(2)}) %collective-permute-start.3) | collective-permute-done | bytes 229408 | tf_op jit(solution)/shard_map/ppermute | solution.py:32
  62.8 4.1 %collective-permute-start.18 = (bf16[128,896]{1,0:T(8,128)(2,1)}, bf16[128,896]{1,0:T(8,128)(2,1)S(1)}, u32[]{:S(2)}, u32[]{:S(2)}) collective-permute-start(bf16[128,896]{1,0:T(8,128)(2,1)} %get-tuple-element.69.refs_0_), channel_id=1, source_target_pairs={{0,96},{8,104},{16,112},{24,120},{32,0},{40,8},{48,16},{56,24},{64... | collective-permute-start | bytes 688136 | tf_op jit(solution)/shard_map/ppermute | solution.py:32
  70.0 3.3 %adam.3 = (f32[256,896]{1,0:T(8,128)}, f32[256,896]{1,0:T(8,128)}, f32[256,896]{1,0:T(8,128)}, bf16[128,896]{1,0:T(8,128)(2,1)}) custom-call(bf16[896,128]{1,0:T(8,128)(2,1)} %get-tuple-element.49.refs_0_, bf16[896,128]{1,0:T(8,128)(2,1)} %copy-done.25, bf16[896,128]{1,0:T(8,128)(2,1)} %copy-done.26, ...), custom_call_target="tpu_custom_call", output_to_operand_aliasing={{0}: (7, {}), {1}: (8, {}), {2}: (9, {})} | custom-call | flops 2000000 | bytes 4000000 | tf_op jit(solution)/shard_map/adam/pallas_call | solution.py:226
  75.0 3.7 %collective-permute-start.12 = (bf16[128,896]{1,0:T(8,128)(2,1)}, bf16[128,896]{1,0:T(8,128)(2,1)S(1)}, u32[]{:S(2)}, u32[]{:S(2)}) collective-permute-start(bf16[128,896]{1,0:T(8,128)(2,1)} %get-tuple-element.64.refs_0_), channel_id=1, source_target_pairs={{0,96},{8,104},{16,112},{24,120},{32,0},{40,8},{48,16},{56,24},{64... | collective-permute-start | bytes 688136 | tf_op jit(solution)/shard_map/ppermute | solution.py:32
  80.5 3.2 %by_slot.3 = (bf16[128,896]{1,0:T(8,128)(2,1)}, bf16[128,896]{1,0:T(8,128)(2,1)}, bf16[128,896]{1,0:T(8,128)(2,1)}, bf16[128,896]{1,0:T(8,128)(2,1)}) custom-call(s32[16]{0:T(128)} %map_ref.7, bf16[128,896]{1,0:T(8,128)(2,1)} %get-tuple-element.69.refs_0_, bf16[128,896]{1,0:T(8,128)(2,1)} %copy-done.13, bf16[128,896]{1,0:T(8,128)(2,1)} %copy-done.14, ...), custom_call_target="tpu_custom_call" | custom-call | bytes 2000000 | tf_op jit(solution)/shard_map/by_slot/pallas_call | solution.py:255
  83.8 3.0 %collective-permute-start.21 = (bf16[128,896]{1,0:T(8,128)(2,1)}, bf16[128,896]{1,0:T(8,128)(2,1)S(1)}, u32[]{:S(2)}, u32[]{:S(2)}) collective-permute-start(bf16[128,896]{1,0:T(8,128)(2,1)} %get-tuple-element.71), channel_id=1, source_target_pairs={{0,24},{8,0},{16,8},{24,16},{32,56},{40,32},{48,40},{56,48},{64,88... | collective-permute-start | bytes 688136 | tf_op jit(solution)/shard_map/ppermute | solution.py:28
  86.7 7.6 %act_terms.2 = (bf16[1536,128]{1,0:T(8,128)(2,1)}, bf16[1536,128]{1,0:T(8,128)(2,1)}, bf16[1536,128]{1,0:T(8,128)(2,1)}, bf16[1536,128]{1,0:T(8,128)(2,1)}) custom-call(s32[4]{0:T(128)} %pad_add_fusion.place_ref, bf16[3072,896]{1,0:T(8,128)(2,1)} %bitcast.29, bf16[3072,896]{1,0:T(8,128)(2,1)} %collective-permute-done.24.other_ref, ...), custom_call_target="tpu_custom_call" | custom-call | flops 2818572288 | bytes 9000000 | tf_op jit(solution)/shard_map/act_terms/pallas_call | solution.py:128
  98.8 3.0 %by_slot.2 = (bf16[128,896]{1,0:T(8,128)(2,1)}, bf16[128,896]{1,0:T(8,128)(2,1)}, bf16[128,896]{1,0:T(8,128)(2,1)}, bf16[128,896]{1,0:T(8,128)(2,1)}) custom-call(s32[16]{0:T(128)} %map_ref.7, bf16[128,896]{1,0:T(8,128)(2,1)} %get-tuple-element.64.refs_0_, bf16[128,896]{1,0:T(8,128)(2,1)} %copy-done.16, bf16[128,896]{1,0:T(8,128)(2,1)} %copy-done.17, ...), custom_call_target="tpu_custom_call" | custom-call | bytes 2000000 | tf_op jit(solution)/shard_map/by_slot/pallas_call | solution.py:255
  106.6 7.6 %act_terms.3 = (bf16[1536,128]{1,0:T(8,128)(2,1)}, bf16[1536,128]{1,0:T(8,128)(2,1)}, bf16[1536,128]{1,0:T(8,128)(2,1)}, bf16[1536,128]{1,0:T(8,128)(2,1)}) custom-call(s32[4]{0:T(128)} %pad_add_fusion.place_ref, bf16[3072,896]{1,0:T(8,128)(2,1)} %bitcast.30, bf16[3072,896]{1,0:T(8,128)(2,1)} %collective-permute-done.24.other_ref, ...), custom_call_target="tpu_custom_call" | custom-call | flops 2818572288 | bytes 9000000 | tf_op jit(solution)/shard_map/act_terms/pallas_call | solution.py:128
  119.9 3.5 %put_rows.2.refs_4_ = bf16[1024,896]{1,0:T(8,128)(2,1)} custom-call(s32[4]{0:T(128)} %pad_add_fusion.place_ref, bf16[128,896]{1,0:T(8,128)(2,1)} %get-tuple-element.70.refs_0_, bf16[128,896]{1,0:T(8,128)(2,1)} %copy-done.10, bf16[128,896]{1,0:T(8,128)(2,1)} %copy-done.11, bf16[128,896]{1,0:T(8,128)(2,1)} %copy-done.12), custom_call_target="tpu_custom_call" | custom-call | bytes 2000000 | tf_op jit(solution)/shard_map/put_rows/pallas_call | solution.py:281
  123.5 3.5 %put_rows.3 = bf16[1024,896]{1,0:T(8,128)(2,1)} custom-call(s32[4]{0:T(128)} %pad_add_fusion.place_ref, bf16[128,896]{1,0:T(8,128)(2,1)} %get-tuple-element.65.refs_0_, bf16[128,896]{1,0:T(8,128)(2,1)} %copy-done.28, bf16[128,896]{1,0:T(8,128)(2,1)} %copy-done.29, bf16[128,896]{1,0:T(8,128)(2,1)} %copy-done.30, ...), custom_call_target="tpu_custom_call", output_to_operand_aliasing={{}: (5, {})} | custom-call | bytes 2000000 | tf_op jit(solution)/shard_map/put_rows/pallas_call | solution.py:281
  127.9 8.9 %collective-permute-done.28.refs_3_ = bf16[1536,128]{1,0:T(8,128)(2,1)S(1)} collective-permute-done((bf16[1536,128]{1,0:T(8,128)(2,1)S(1)}, bf16[1536,128]{1,0:T(8,128)(2,1)S(1)}, u32[]{:S(2)}, u32[]{:S(2)}) %collective-permute-start.28) | collective-permute-done | bytes 393248 | tf_op jit(solution)/shard_map/ppermute | solution.py:36
  136.9 5.4 %collective-permute-done.30.refs_6_ = bf16[1536,128]{1,0:T(8,128)(2,1)S(1)} collective-permute-done((bf16[1536,128]{1,0:T(8,128)(2,1)}, bf16[1536,128]{1,0:T(8,128)(2,1)S(1)}, u32[]{:S(2)}, u32[]{:S(2)}) %collective-permute-start.30) | collective-permute-done | bytes 393248 | tf_op jit(solution)/shard_map/ppermute | solution.py:36
  142.3 4.0 %collective-permute-done.31.refs_7_ = bf16[1536,128]{1,0:T(8,128)(2,1)S(1)} collective-permute-done((bf16[1536,128]{1,0:T(8,128)(2,1)}, bf16[1536,128]{1,0:T(8,128)(2,1)S(1)}, u32[]{:S(2)}, u32[]{:S(2)}) %collective-permute-start.31) | collective-permute-done | bytes 393248 | tf_op jit(solution)/shard_map/ppermute | solution.py:36
  147.1 3.0 %act_sum.1 = bf16[3072,128]{1,0:T(8,128)(2,1)} custom-call(bf16[1536,128]{1,0:T(8,128)(2,1)} %get-tuple-element.77.refs_0_, bf16[1536,128]{1,0:T(8,128)(2,1)} %copy-done.1, bf16[1536,128]{1,0:T(8,128)(2,1)} %copy-done.2, bf16[1536,128]{1,0:T(8,128)(2,1)} %copy-done.3, bf16[1536,128]{1,0:T(8,128)(2,1)} %get-tuple-element.81.refs_4_, ...), custom_call_target="tpu_custom_call" | custom-call | flops 1572864 | bytes 8000000 | tf_op jit(solution)/shard_map/act_sum/pallas_call | solution.py:157
  (121 shorter events, 35.5 us)
Async XLA Ops:
  0.6 86.1 %collective-permute-start.24 = (bf16[3072,896]{1,0:T(8,128)(2,1)}, bf16[3072,896]{1,0:T(8,128)(2,1)}, u32[]{:S(2)}, u32[]{:S(2)}) collective-permute-start(bf16[3072,896]{1,0:T(8,128)(2,1)} %bitcast.27), channel_id=1, source_target_pairs={{0,1},{1,0},{2,3},{3,2},{4,5},{5,4},{6,7},{7,6},{8,9},{9,8},{10,11... | collective-permute-start | bytes 16515080 | tf_op jit(solution)/shard_map/ppermute | solution.py:40
  0.7 83.0 %collective-permute-start.25 = (bf16[1024,896]{1,0:T(8,128)(2,1)}, bf16[1024,896]{1,0:T(8,128)(2,1)S(1)}, u32[]{:S(2)}, u32[]{:S(2)}) collective-permute-start(bf16[1024,896]{1,0:T(8,128)(2,1)} %bitcast.10), channel_id=1, source_target_pairs={{0,1},{1,0},{2,3},{3,2},{4,5},{5,4},{6,7},{7,6},{8,9},{9,8},{10,11... | collective-permute-start | bytes 5505032 | tf_op jit(solution)/shard_map/ppermute | solution.py:40
  13.0 14.5 %collective-permute-start.6 = (bf16[896,128]{1,0:T(8,128)(2,1)}, bf16[896,128]{1,0:T(8,128)(2,1)S(1)}, u32[]{:S(2)}, u32[]{:S(2)}) collective-permute-start(bf16[896,128]{1,0:T(8,128)(2,1)} %get-tuple-element.54), channel_id=1, source_target_pairs={{0,24},{8,0},{16,8},{24,16},{32,56},{40,32},{48,40},{56,48},{64,88... | collective-permute-start | bytes 688136 | tf_op jit(solution)/shard_map/ppermute | solution.py:28
  17.2 13.9 %collective-permute-start.7 = (bf16[896,128]{1,0:T(8,128)(2,1)}, bf16[896,128]{1,0:T(8,128)(2,1)S(1)}, u32[]{:S(2)}, u32[]{:S(2)}) collective-permute-start(bf16[896,128]{1,0:T(8,128)(2,1)} %get-tuple-element.55), channel_id=1, source_target_pairs={{0,16},{8,24},{16,0},{24,8},{32,48},{40,56},{48,32},{56,40},{64,80... | collective-permute-start | bytes 688136 | tf_op jit(solution)/shard_map/ppermute | solution.py:28
  17.2 14.0 %collective-permute-start.8 = (bf16[896,128]{1,0:T(8,128)(2,1)}, bf16[896,128]{1,0:T(8,128)(2,1)S(1)}, u32[]{:S(2)}, u32[]{:S(2)}) collective-permute-start(bf16[896,128]{1,0:T(8,128)(2,1)} %get-tuple-element.56), channel_id=1, source_target_pairs={{0,8},{8,16},{16,24},{24,0},{32,40},{40,48},{48,56},{56,32},{64,72... | collective-permute-start | bytes 688136 | tf_op jit(solution)/shard_map/ppermute | solution.py:28
  27.5 13.1 %collective-permute-start = (bf16[896,128]{1,0:T(8,128)(2,1)}, bf16[896,128]{1,0:T(8,128)(2,1)S(1)}, u32[]{:S(2)}, u32[]{:S(2)}) collective-permute-start(bf16[896,128]{1,0:T(8,128)(2,1)} %get-tuple-element.46), channel_id=1, source_target_pairs={{0,24},{8,0},{16,8},{24,16},{32,56},{40,32},{48,40},{56,48},{64,88... | collective-permute-start | bytes 688136 | tf_op jit(solution)/shard_map/ppermute | solution.py:28
  31.1 12.7 %collective-permute-start.1 = (bf16[896,128]{1,0:T(8,128)(2,1)}, bf16[896,128]{1,0:T(8,128)(2,1)S(1)}, u32[]{:S(2)}, u32[]{:S(2)}) collective-permute-start(bf16[896,128]{1,0:T(8,128)(2,1)} %get-tuple-element.47), channel_id=1, source_target_pairs={{0,16},{8,24},{16,0},{24,8},{32,48},{40,56},{48,32},{56,40},{64,80... | collective-permute-start | bytes 688136 | tf_op jit(solution)/shard_map/ppermute | solution.py:28
  31.1 13.4 %collective-permute-start.2 = (bf16[896,128]{1,0:T(8,128)(2,1)}, bf16[896,128]{1,0:T(8,128)(2,1)S(1)}, u32[]{:S(2)}, u32[]{:S(2)}) collective-permute-start(bf16[896,128]{1,0:T(8,128)(2,1)} %get-tuple-element.48), channel_id=1, source_target_pairs={{0,8},{8,16},{16,24},{24,0},{32,40},{40,48},{48,56},{56,32},{64,72... | collective-permute-start | bytes 688136 | tf_op jit(solution)/shard_map/ppermute | solution.py:28
  53.4 13.5 %collective-permute-start.4 = (bf16[896,128]{1,0:T(8,128)(2,1)}, bf16[896,128]{1,0:T(8,128)(2,1)S(1)}, u32[]{:S(2)}, u32[]{:S(2)}) collective-permute-start(bf16[896,128]{1,0:T(8,128)(2,1)} %get-tuple-element.51), channel_id=1, source_target_pairs={{0,64},{8,72},{16,80},{24,88},{32,96},{40,104},{48,112},{56,120},{... | collective-permute-start | bytes 688136 | tf_op jit(solution)/shard_map/ppermute | solution.py:32
  62.8 12.1 %collective-permute-start.18 = (bf16[128,896]{1,0:T(8,128)(2,1)}, bf16[128,896]{1,0:T(8,128)(2,1)S(1)}, u32[]{:S(2)}, u32[]{:S(2)}) collective-permute-start(bf16[128,896]{1,0:T(8,128)(2,1)} %get-tuple-element.69.refs_0_), channel_id=1, source_target_pairs={{0,96},{8,104},{16,112},{24,120},{32,0},{40,8},{48,16},{56,24},{64... | collective-permute-start | bytes 688136 | tf_op jit(solution)/shard_map/ppermute | solution.py:32
  67.0 12.8 %collective-permute-start.20 = (bf16[128,896]{1,0:T(8,128)(2,1)}, bf16[128,896]{1,0:T(8,128)(2,1)S(1)}, u32[]{:S(2)}, u32[]{:S(2)}) collective-permute-start(bf16[128,896]{1,0:T(8,128)(2,1)} %get-tuple-element.69.refs_0_), channel_id=1, source_target_pairs={{0,32},{8,40},{16,48},{24,56},{32,64},{40,72},{48,80},{56,88},{64,... | collective-permute-start | bytes 688136 | tf_op jit(solution)/shard_map/ppermute | solution.py:32
  75.0 19.3 %collective-permute-start.12 = (bf16[128,896]{1,0:T(8,128)(2,1)}, bf16[128,896]{1,0:T(8,128)(2,1)S(1)}, u32[]{:S(2)}, u32[]{:S(2)}) collective-permute-start(bf16[128,896]{1,0:T(8,128)(2,1)} %get-tuple-element.64.refs_0_), channel_id=1, source_target_pairs={{0,96},{8,104},{16,112},{24,120},{32,0},{40,8},{48,16},{56,24},{64... | collective-permute-start | bytes 688136 | tf_op jit(solution)/shard_map/ppermute | solution.py:32
  78.7 18.5 %collective-permute-start.13 = (bf16[128,896]{1,0:T(8,128)(2,1)}, bf16[128,896]{1,0:T(8,128)(2,1)S(1)}, u32[]{:S(2)}, u32[]{:S(2)}) collective-permute-start(bf16[128,896]{1,0:T(8,128)(2,1)} %get-tuple-element.64.refs_0_), channel_id=1, source_target_pairs={{0,64},{8,72},{16,80},{24,88},{32,96},{40,104},{48,112},{56,120},{... | collective-permute-start | bytes 688136 | tf_op jit(solution)/shard_map/ppermute | solution.py:32
  79.8 18.3 %collective-permute-start.14 = (bf16[128,896]{1,0:T(8,128)(2,1)}, bf16[128,896]{1,0:T(8,128)(2,1)S(1)}, u32[]{:S(2)}, u32[]{:S(2)}) collective-permute-start(bf16[128,896]{1,0:T(8,128)(2,1)} %get-tuple-element.64.refs_0_), channel_id=1, source_target_pairs={{0,32},{8,40},{16,48},{24,56},{32,64},{40,72},{48,80},{56,88},{64,... | collective-permute-start | bytes 688136 | tf_op jit(solution)/shard_map/ppermute | solution.py:32
  83.8 20.4 %collective-permute-start.21 = (bf16[128,896]{1,0:T(8,128)(2,1)}, bf16[128,896]{1,0:T(8,128)(2,1)S(1)}, u32[]{:S(2)}, u32[]{:S(2)}) collective-permute-start(bf16[128,896]{1,0:T(8,128)(2,1)} %get-tuple-element.71), channel_id=1, source_target_pairs={{0,24},{8,0},{16,8},{24,16},{32,56},{40,32},{48,40},{56,48},{64,88... | collective-permute-start | bytes 688136 | tf_op jit(solution)/shard_map/ppermute | solution.py:28
  86.7 19.8 %collective-permute-start.22 = (bf16[128,896]{1,0:T(8,128)(2,1)}, bf16[128,896]{1,0:T(8,128)(2,1)S(1)}, u32[]{:S(2)}, u32[]{:S(2)}) collective-permute-start(bf16[128,896]{1,0:T(8,128)(2,1)} %get-tuple-element.72), channel_id=1, source_target_pairs={{0,16},{8,24},{16,0},{24,8},{32,48},{40,56},{48,32},{56,40},{64,80... | collective-permute-start | bytes 688136 | tf_op jit(solution)/shard_map/ppermute | solution.py:28
  94.3 25.6 %collective-permute-start.26 = (bf16[1536,128]{1,0:T(8,128)(2,1)}, bf16[1536,128]{1,0:T(8,128)(2,1)S(1)}, u32[]{:S(2)}, u32[]{:S(2)}) collective-permute-start(bf16[1536,128]{1,0:T(8,128)(2,1)} %get-tuple-element.78), channel_id=1, source_target_pairs={{0,6},{1,7},{2,0},{3,1},{4,2},{5,3},{6,4},{7,5},{8,14},{9,15},{10,... | collective-permute-start | bytes 1179656 | tf_op jit(solution)/shard_map/ppermute | solution.py:36
  97.2 17.0 %collective-permute-start.23 = (bf16[128,896]{1,0:T(8,128)(2,1)S(1)}, bf16[128,896]{1,0:T(8,128)(2,1)S(1)}, u32[]{:S(2)}, u32[]{:S(2)}) collective-permute-start(bf16[128,896]{1,0:T(8,128)(2,1)S(1)} %copy-done.33), channel_id=1, source_target_pairs={{0,8},{8,16},{16,24},{24,0},{32,40},{40,48},{48,56},{56,32},{64,72... | collective-permute-start | bytes 688136 | tf_op jit(solution)/shard_map/ppermute | solution.py:28
  101.9 13.2 %collective-permute-start.15 = (bf16[128,896]{1,0:T(8,128)(2,1)}, bf16[128,896]{1,0:T(8,128)(2,1)S(1)}, u32[]{:S(2)}, u32[]{:S(2)}) collective-permute-start(bf16[128,896]{1,0:T(8,128)(2,1)} %get-tuple-element.66), channel_id=1, source_target_pairs={{0,24},{8,0},{16,8},{24,16},{32,56},{40,32},{48,40},{56,48},{64,88... | collective-permute-start | bytes 688136 | tf_op jit(solution)/shard_map/ppermute | solution.py:28
  114.2 13.7 %collective-permute-start.27 = (bf16[1536,128]{1,0:T(8,128)(2,1)S(1)}, bf16[1536,128]{1,0:T(8,128)(2,1)S(1)}, u32[]{:S(2)}, u32[]{:S(2)}) collective-permute-start(bf16[1536,128]{1,0:T(8,128)(2,1)S(1)} %copy-done.32), channel_id=1, source_target_pairs={{0,4},{1,5},{2,6},{3,7},{4,0},{5,1},{6,2},{7,3},{8,12},{9,13},{10,... | collective-permute-start | bytes 1179656 | tf_op jit(solution)/shard_map/ppermute | solution.py:36
  115.1 21.8 %collective-permute-start.28 = (bf16[1536,128]{1,0:T(8,128)(2,1)S(1)}, bf16[1536,128]{1,0:T(8,128)(2,1)S(1)}, u32[]{:S(2)}, u32[]{:S(2)}) collective-permute-start(bf16[1536,128]{1,0:T(8,128)(2,1)S(1)} %copy-done.31), channel_id=1, source_target_pairs={{0,2},{1,3},{2,4},{3,5},{4,6},{5,7},{6,0},{7,1},{8,10},{9,11},{10,... | collective-permute-start | bytes 1179656 | tf_op jit(solution)/shard_map/ppermute | solution.py:36
  116.1 20.8 %collective-permute-start.29 = (bf16[1536,128]{1,0:T(8,128)(2,1)}, bf16[1536,128]{1,0:T(8,128)(2,1)S(1)}, u32[]{:S(2)}, u32[]{:S(2)}) collective-permute-start(bf16[1536,128]{1,0:T(8,128)(2,1)} %get-tuple-element.82), channel_id=1, source_target_pairs={{0,6},{1,7},{2,0},{3,1},{4,2},{5,3},{6,4},{7,5},{8,14},{9,15},{10,... | collective-permute-start | bytes 1179656 | tf_op jit(solution)/shard_map/ppermute | solution.py:36
  118.4 23.9 %collective-permute-start.30 = (bf16[1536,128]{1,0:T(8,128)(2,1)}, bf16[1536,128]{1,0:T(8,128)(2,1)S(1)}, u32[]{:S(2)}, u32[]{:S(2)}) collective-permute-start(bf16[1536,128]{1,0:T(8,128)(2,1)} %get-tuple-element.83), channel_id=1, source_target_pairs={{0,4},{1,5},{2,6},{3,7},{4,0},{5,1},{6,2},{7,3},{8,12},{9,13},{10,... | collective-permute-start | bytes 1179656 | tf_op jit(solution)/shard_map/ppermute | solution.py:36
  119.9 26.4 %collective-permute-start.31 = (bf16[1536,128]{1,0:T(8,128)(2,1)}, bf16[1536,128]{1,0:T(8,128)(2,1)S(1)}, u32[]{:S(2)}, u32[]{:S(2)}) collective-permute-start(bf16[1536,128]{1,0:T(8,128)(2,1)} %get-tuple-element.84), channel_id=1, source_target_pairs={{0,2},{1,3},{2,4},{3,5},{4,6},{5,7},{6,0},{7,1},{8,10},{9,11},{10,... | collective-permute-start | bytes 1179656 | tf_op jit(solution)/shard_map/ppermute | solution.py:36
  (42 other events, 265.6 us)

commit v2 on v0

v2 whole, which is shorter than its diff:
```python
import functools

import jax
import jax.numpy as jnp
from jax import lax
from jax.experimental import pallas as pl
from jax.experimental.pallas import tpu as pltpu
from jax.sharding import PartitionSpec as P

beta_one = 0.9
beta_two = 0.95
learn_rate = 0.5
weight_decay = 0.1
epsilon = 1e-08
adam_step = 20

RING = 4
CHUNKS = 2
bf16 = jnp.bfloat16
f32 = jnp.float32


def params(limit, *semantics):
    return pltpu.CompilerParams(vmem_limit_bytes=int(limit * 2**20), dimension_semantics=semantics or None)


VMEM = pl.BlockSpec(memory_space=pltpu.VMEM)
SMEM = pl.BlockSpec(memory_space=pltpu.SMEM)
ANY = pl.BlockSpec(memory_space=pl.ANY)
HBM = pl.BlockSpec(memory_space=pltpu.HBM)


def turned(distance, core):
    return distance ^ ((distance & 1) * 2 * core)


def along(stride):
    def move(value, distance):
        pairs = [
            (slot * 2 * RING + shard, (slot ^ (turned(distance, shard % 2) * stride)) * 2 * RING + shard)
            for slot in range(RING * RING)
            for shard in range(2 * RING)
        ]
        return lax.ppermute(value, ("slot", "shard"), pairs)

    return move


move_z = along(1)
move_y = along(RING)


def exchange(move, pieces):
    return [pieces[0]] + [move(pieces[distance], distance) for distance in range(1, RING)]


def my_place():
    slot = lax.axis_index("slot")
    return slot // RING, slot % RING, lax.axis_index("shard") % 2


def slot_grads(counts, acts, out_grads, scale):
    tokens, ff = acts.shape
    width = out_grads.shape[1]
    quarter = ff // RING
    part = quarter // CHUNKS
    blocks = [256, 512, 768, 768, 768]
    starts = [sum(blocks[:i]) for i in range(len(blocks))]
    assert sum(blocks) == tokens

    def kernel(count_ref, acts_hbm, grads_hbm, *rest):
        outs, (acts_ref, grads_ref, total, sems) = rest[:-4], rest[-4:]
        _, z, core = my_place()
        copies = []
        for i, (start, block) in enumerate(zip(starts, blocks)):
            rows = pl.ds(start, block)
            copies.append(
                (
                    pltpu.make_async_copy(grads_hbm.at[rows, :], grads_ref.at[rows, :], sems.at[2 * i]),
                    pltpu.make_async_copy(acts_hbm.at[rows, :], acts_ref.at[rows, :], sems.at[2 * i + 1]),
                )
            )
        for pair in copies:
            for copy in pair:
                copy.start()
        for i, (start, block) in enumerate(zip(starts, blocks)):
            for copy in copies[i]:
                copy.wait()
            rows = lax.broadcasted_iota(jnp.int32, (block, width), 0)
            grads = grads_ref[start : start + block, :]
            masked = jnp.where(rows < count_ref[0] - start, grads, jnp.zeros_like(grads))
            term = lax.dot_general(
                masked, acts_ref[start : start + block, :], (((0,), (0,)), ((), ())), preferred_element_type=f32
            )
            total[...] = term if i == 0 else total[...] + term
        for chunk in range(CHUNKS):
            for distance in range(RING):
                start = (z ^ turned(distance, core)) * quarter + chunk * part
                columns = total[:, pl.ds(pl.multiple_of(start, part), part)]
                outs[chunk * RING + distance][...] = (columns * scale).astype(bf16)

    pieces = pl.pallas_call(
        kernel,
        in_specs=[SMEM, HBM, HBM],
        out_specs=[VMEM] * (CHUNKS * RING),
        out_shape=[jax.ShapeDtypeStruct((width, part), bf16)] * (CHUNKS * RING),
        scratch_shapes=[
            pltpu.VMEM((tokens, ff), bf16),
            pltpu.VMEM((tokens, width), bf16),
            pltpu.VMEM((width, ff), f32),
            pltpu.SemaphoreType.DMA((2 * len(blocks),)),
        ],
        compiler_params=params(57.5),
        cost_estimate=pl.CostEstimate(flops=2 * tokens * ff * width, bytes_accessed=14_000_000, transcendentals=0),
        name="slot_grads",
    )(counts, acts, out_grads)
    return [pieces[chunk * RING : (chunk + 1) * RING] for chunk in range(CHUNKS)]


def act_terms(counts, out_grads, weight, scale, after):
    tokens, width = out_grads.shape
    ff = weight.shape[0]
    block = 512
    steps = tokens // block
    columns = ff // (2 * RING)

    def kernel(count_ref, grads_ref, weight_ref, after_ref, out_ref, done_ref):
        live = count_ref[0] - pl.program_id(0) * block
        term = lax.dot_general(grads_ref[...], weight_ref[...], (((1,), (1,)), ((), ())), preferred_element_type=f32)
        rows = lax.broadcasted_iota(jnp.int32, term.shape, 0)
        term = jnp.where(rows < live, term * scale, 0.0).astype(bf16)
        for piece in range(2 * RING):
            out_ref[piece] = term[:, piece * columns : (piece + 1) * columns]
        done_ref[0] = 0

    return pl.pallas_call(
        kernel,
        grid_spec=pltpu.PrefetchScalarGridSpec(
            num_scalar_prefetch=1,
            grid=(steps,),
            in_specs=[
                pl.BlockSpec((block, width), lambda i, c: (i, 0)),
                pl.BlockSpec((ff, width), lambda i, c: (0, 0)),
                ANY,
            ],
            out_specs=[
                pl.BlockSpec((2 * RING, block, columns), lambda i, c: (0, i, 0)),
                SMEM,
            ],
        ),
        out_shape=[jax.ShapeDtypeStruct((2 * RING, tokens, columns), bf16), jax.ShapeDtypeStruct((1,), jnp.int32)],
        compiler_params=params(50, "arbitrary"),
        cost_estimate=pl.CostEstimate(flops=2 * tokens * ff * width, bytes_accessed=14_000_000, transcendentals=0),
        name="act_terms",
    )(counts, out_grads, weight, after)


def by_expert(replica_map, pieces, after):
    def kernel(map_ref, after_ref, *refs):
        ins, outs = refs[:RING], refs[RING:]
        y, z, core = my_place()
        values = [ref[...].astype(f32) for ref in ins]
        held = [map_ref[RING * y + (z ^ turned(distance, core))] for distance in range(RING)]
        for step in range(RING):
            expert = y ^ turned(step, core)
            total = jnp.where(held[0] == expert, values[0], 0.0)
            for value, one in zip(values[1:], held[1:]):
                total = total + jnp.where(one == expert, value, 0.0)
            outs[step][...] = total.astype(bf16)

    shape = pieces[0].shape
    return pl.pallas_call(
        kernel,
        in_specs=[SMEM, SMEM] + [VMEM] * RING,
        out_specs=[VMEM] * RING,
        out_shape=[jax.ShapeDtypeStruct(shape, bf16)] * RING,
        compiler_params=params(16),
        cost_estimate=pl.CostEstimate(flops=1_000_000, bytes_accessed=2_000_000, transcendentals=0),
        name="by_expert",
    )(replica_map, after, *pieces)


def adam_update(grad_total, master, moment1, moment2):
    new_first = beta_one * moment1 + (1.0 - beta_one) * grad_total
    new_second = beta_two * moment2 + (1.0 - beta_two) * grad_total * grad_total
    first_hat = new_first / (1.0 - beta_one**adam_step)
    second_hat = new_second / (1.0 - beta_two**adam_step)
    update = first_hat / (jnp.sqrt(second_hat) + epsilon)
    master_new = master - learn_rate * (update + weight_decay * master)
    return (master_new, new_first, new_second)


def adam(chunk, pieces, state, earlier):
    rows, width = state[0].shape
    part = rows // CHUNKS

    def kernel(*refs):
        terms = [ref[...].astype(f32) for ref in refs[:RING]]
        master, moment1, moment2 = refs[RING : RING + 3]
        outs = refs[-4:]
        grad = ((terms[0] + terms[1]) + (terms[2] + terms[3])).T
        master_new, new_first, new_second = adam_update(grad, master[...], moment1[...], moment2[...])
        outs[0][...] = master_new
        outs[1][...] = new_first
        outs[2][...] = new_second
        outs[3][...] = master_new.astype(bf16)

    whole = jax.ShapeDtypeStruct((rows, width), f32)
    mine = pl.BlockSpec((part, width), lambda i: (chunk, 0))
    return pl.pallas_call(
        kernel,
        grid=(1,),
        in_specs=[VMEM] * RING + [mine] * 3 + [ANY] * len(earlier),
        out_specs=[mine] * 3 + [VMEM],
        out_shape=[whole] * 3 + [jax.ShapeDtypeStruct((part, width), bf16)],
        input_output_aliases={RING + 3 + i: i for i in range(len(earlier))},
        compiler_params=params(16, "arbitrary"),
        cost_estimate=pl.CostEstimate(flops=2_000_000, bytes_accessed=4_000_000, transcendentals=rows * width),
        name="adam",
    )(*pieces, *state, *earlier)


def by_slot(next_map, pieces):
    def kernel(map_ref, *refs):
        ins, outs = refs[:RING], refs[RING:]
        y, z, core = my_place()
        for distance in range(RING):
            wanted = turned(map_ref[RING * y + (z ^ turned(distance, core))] ^ y, core)
            for step in range(RING):

                @pl.when(wanted == step)
                def _(step=step, distance=distance):
                    outs[distance][...] = ins[step][...]

    shape = pieces[0].shape
    return pl.pallas_call(
        kernel,
        in_specs=[SMEM] + [VMEM] * RING,
        out_specs=[VMEM] * RING,
        out_shape=[jax.ShapeDtypeStruct(shape, bf16)] * RING,
        compiler_params=params(16),
        cost_estimate=pl.CostEstimate(flops=0, bytes_accessed=2_000_000, transcendentals=0),
        name="by_slot",
    )(next_map, *pieces)


def put_rows(chunk, pieces, ff, earlier):
    part, width = pieces[0].shape

    def kernel(*refs):
        ins, out, sems = refs[:RING], refs[-2], refs[-1]
        _, z, core = my_place()
        copies = []
        for distance in range(RING):
            start = (z ^ turned(distance, core)) * (part * CHUNKS) + chunk * part
            target = out.at[pl.ds(pl.multiple_of(start, part), part), :]
            copies.append(pltpu.make_async_copy(ins[distance], target, sems.at[distance]))
        for copy in copies:
            copy.start()
        for copy in copies:
            copy.wait()

    return pl.pallas_call(
        kernel,
        in_specs=[VMEM] * RING + [ANY] * len(earlier),
        out_specs=ANY,
        out_shape=jax.ShapeDtypeStruct((ff, width), bf16),
        scratch_shapes=[pltpu.SemaphoreType.DMA((RING,))],
        input_output_aliases={RING: 0} if earlier else {},
        compiler_params=params(16),
        cost_estimate=pl.CostEstimate(flops=0, bytes_accessed=2_000_000, transcendentals=0),
        name="put_rows",
    )(*pieces, *earlier)


def local(acts, out_grads, counts, replica_map, next_map, slot_weights, master, moment1, moment2):
    hidden, grads, weight = acts[0], out_grads[0], slot_weights[0]
    ff = hidden.shape[1]
    scale = ff**-0.5

    by_chunk = slot_grads(counts, hidden, grads, scale)
    along_z = [exchange(move_z, by_chunk[0])]
    terms, after = act_terms(counts, grads, weight, scale, by_chunk[0][0])
    terms, later, _ = lax.optimization_barrier((terms, by_chunk[1], along_z[0][1:]))
    act_grads = lax.psum_scatter(terms, "shard", scatter_dimension=0, tiled=False)
    along_z.append(exchange(move_z, later))
    along_y = [exchange(move_y, by_expert(replica_map, pieces, after)) for pieces in along_z]

    state = ()
    fresh = []
    for chunk, pieces in enumerate(along_y):
        *state, rows = adam(chunk, pieces, (master, moment1, moment2), tuple(state))
        fresh.append(exchange(move_y, [rows] * RING))
    wanted = [exchange(move_z, by_slot(next_map, pieces)) for pieces in fresh]
    new_weight = ()
    for chunk, pieces in enumerate(wanted):
        new_weight = (put_rows(chunk, pieces, ff, new_weight),)
    return (new_weight[0][None], *state, act_grads[None])


def solution(mesh):
    placed = (
        P("slot", None, None),
        P("slot", None, "shard"),
        P("slot"),
        P(),
        P(),
        P("slot", None, "shard"),
        P("slot", "shard"),
        P("slot", "shard"),
        P("slot", "shard"),
    )
    return jax.shard_map(
        local,
        mesh=mesh,
        in_specs=placed,
        out_specs=(
            P("slot", None, "shard"),
            P("slot", "shard"),
            P("slot", "shard"),
            P("slot", "shard"),
            P("slot", None, "shard"),
        ),
        check_vma=False,
    )
```

time: 243 us -> 115 us (0.47)
  waiting for transfers between devices: 172 us -> 26.9 us
  starting transfers between devices: 0.12 us -> 39 us
  Pallas kernels: 0 us -> 30 us
  matrix products: 23.3 us -> 0 us
  local copies, waits for them, and re-layouts: 21 us -> 4.22 us
  other arithmetic: 10.3 us -> 0 us
    all_gather x1 -> x0, waiting for transfers between devices: 66.7 us -> none  [local(): gathered = lax.all_gather(fresh_rows, 'slot', axis=0, tiled=True)]
    reduce_scatter x1, waiting for transfers between devices: 65.7 us -> 0.02 us  [local(): lax.psum_scatter(terms, 'shard', scatter_dimension=0, tiled=False)]
    unnamed x4 -> x1, waiting for transfers between devices: 39.3 us -> 0.02 us
    ppermute x0 -> x24, starting transfers between devices: none -> 39 us  [move(): return lax.ppermute(value, ('slot', 'shard'), pairs)]
    pallas_call x0 -> x10, Pallas kernels: none -> 30 us  [the longest x1 10.6 us: act_terms(): pl.pallas_call(kernel, grid_spec=pltpu.PrefetchScalarGridSpec(num_scalar_...]
    ppermute x0 -> x24, waiting for transfers between devices: none -> 26.9 us  [move(): return lax.ppermute(value, ('slot', 'shard'), pairs)]
    dot_general x2 -> x0, matrix products: 23.3 us -> none  [the longest x1 12.2 us: local(): jnp.einsum('tf,td->fd', hidden, masked, preferred_element_type=jnp.float32)]
    convert_element_type x3 -> x0, other arithmetic: 10.3 us -> none  [the longest x1 5.95 us: local(): dense_term.astype(jnp.bfloat16)]
  transfers between devices with their start and end apart: 3 -> 25, of which waited for: 3 -> 10; matrix products, arithmetic and copies ran while one was open for 11% -> 0% of each run, Pallas kernels for 0% -> 18%
where the time goes in v2:
time: 115 us
  starting transfers between devices  39 us (34%)
  Pallas kernels  30 us (26%)
  waiting for transfers between devices  26.9 us (23%)
  between operations  14.9 us (13%)
  local copies, waits for them, and re-layouts  4.22 us (4%)
    ppermute x24, starting transfers between devices, move(): return lax.ppermute(value, ('slot', 'shard'), pairs)  39 us
    ppermute x24, waiting for transfers between devices, move(): return lax.ppermute(value, ('slot', 'shard'), pairs)  26.9 us
    pallas_call x1, Pallas kernels, act_terms(): pl.pallas_call(kernel, grid_spec=pltpu.PrefetchScalarGridSpec(num_scalar_...  10.6 us
    pallas_call x1, Pallas kernels, slot_grads(): pl.pallas_call(kernel, in_specs=[SMEM, HBM, HBM], out_specs=[VMEM] * (CHU...  9.43 us
    unnamed x26, local copies, waits for them, and re-layouts  4.22 us
    pallas_call x2, Pallas kernels, by_expert(): pl.pallas_call(kernel, in_specs=[SMEM, SMEM] + [VMEM] * RING, out_specs=[...  3.52 us
    pallas_call x2, Pallas kernels, adam(): pl.pallas_call(kernel, grid=(1,), in_specs=[VMEM] * RING + [mine] * 3 + [...  3.05 us
  transfers between devices with their start and end apart: 25, of which 10 were waited for; matrix products, arithmetic and copies ran while one was open for 0% of the time, Pallas kernels for 18%

profile of v2, /device:TPU:0, one launch (start us, length us, event | category | flops | bytes accessed | tf_op | source)
XLA Modules:
  0.0 115.0 jit_solution(7986012560318824709)
XLA Ops:
  7.9 9.4 %slot_grads.1 = (bf16[896,128]{1,0:T(8,128)(2,1)}, bf16[896,128]{1,0:T(8,128)(2,1)}, bf16[896,128]{1,0:T(8,128)(2,1)}, bf16[896,128]{1,0:T(8,128)(2,1)}, bf16[89...) custom-call(s32[1]{0:T(128)S(6)} %copy.22.count_ref, ...), custom_call_target="tpu_custom_call" | custom-call | flops 5637144576 | bytes 14000000 | tf_op jit(solution)/shard_map/slot_grads/pallas_call | solution.py:102
  17.3 2.1 %collective-permute-start = (bf16[896,128]{1,0:T(8,128)(2,1)}, bf16[896,128]{1,0:T(8,128)(2,1)S(1)}, u32[]{:S(2)}, u32[]{:S(2)}) collective-permute-start(bf16[896,128]{1,0:T(8,128)(2,1)} %get-tuple-element.51), channel_id=1, source_target_pairs={{0,8},{1,25},{2,10},{3,27},{4,12},{5,29},{6,14},{7,31},{8,0},{9,17... | collective-permute-start | bytes 688136 | tf_op jit(solution)/shard_map/ppermute | solution.py:44
  19.4 3.6 %collective-permute-start.1 = (bf16[896,128]{1,0:T(8,128)(2,1)}, bf16[896,128]{1,0:T(8,128)(2,1)S(1)}, u32[]{:S(2)}, u32[]{:S(2)}) collective-permute-start(bf16[896,128]{1,0:T(8,128)(2,1)} %get-tuple-element.52), channel_id=1, source_target_pairs={{0,16},{1,17},{2,18},{3,19},{4,20},{5,21},{6,22},{7,23},{8,24},{9,... | collective-permute-start | bytes 688136 | tf_op jit(solution)/shard_map/ppermute | solution.py:44
  23.9 10.6 %act_terms.1 = (bf16[8,3072,128]{2,1,0:T(8,128)(2,1)}, s32[1]{0:T(128)}) custom-call(s32[1]{0:T(128)S(6)} %copy.22.count_ref, bf16[3072,896]{1,0:T(8,128)(2,1)} %bitcast.8, bf16[1024,896]{1,0:T(8,128)(2,1)S(1)} %bitcast.4, bf16[896,128]{1,0:T(8,128)(2,1)S(1)} %copy-done.4), custom_call_target="tpu_custom_call" | custom-call | flops 5637144576 | bytes 14000000 | tf_op jit(solution)/shard_map/act_terms/pallas_call | solution.py:136
  36.1 4.7 %collective-permute-start.4 = (bf16[896,128]{1,0:T(8,128)(2,1)}, bf16[896,128]{1,0:T(8,128)(2,1)S(1)}, u32[]{:S(2)}, u32[]{:S(2)}) collective-permute-start(bf16[896,128]{1,0:T(8,128)(2,1)} %get-tuple-element.56), channel_id=1, source_target_pairs={{0,16},{1,17},{2,18},{3,19},{4,20},{5,21},{6,22},{7,23},{8,24},{9,... | collective-permute-start | bytes 688136 | tf_op jit(solution)/shard_map/ppermute | solution.py:44
  42.7 1.8 %by_expert.3 = (bf16[896,128]{1,0:T(8,128)(2,1)S(1)}, bf16[896,128]{1,0:T(8,128)(2,1)S(1)}, bf16[896,128]{1,0:T(8,128)(2,1)S(1)}, bf16[896,128]{1,0:T(8,128)(2,1)S(1)}) custom-call(s32[16]{0:T(128)S(1)} %copy-done.10, s32[1]{0:T(128)} %get-tuple-element.45.after_ref, bf16[896,128]{1,0:T(8,128)(2,1)S(1)} %copy-done.5, ...), custom_call_target="tpu_custom_call" | custom-call | flops 1000000 | bytes 2000000 | tf_op jit(solution)/shard_map/by_expert/pallas_call | solution.py:172
  44.4 1.7 %collective-permute-start.9 = (bf16[896,128]{1,0:T(8,128)(2,1)S(1)}, bf16[896,128]{1,0:T(8,128)(2,1)S(1)}, u32[]{:S(2)}, u32[]{:S(2)}) collective-permute-start(bf16[896,128]{1,0:T(8,128)(2,1)S(1)} %get-tuple-element.63), channel_id=1, source_target_pairs={{0,32},{1,97},{2,34},{3,99},{4,36},{5,101},{6,38},{7,103},{8,40},{... | collective-permute-start | bytes 688136 | tf_op jit(solution)/shard_map/ppermute | solution.py:44
  46.1 2.9 %collective-permute-start.10 = (bf16[896,128]{1,0:T(8,128)(2,1)S(1)}, bf16[896,128]{1,0:T(8,128)(2,1)S(1)}, u32[]{:S(2)}, u32[]{:S(2)}) collective-permute-start(bf16[896,128]{1,0:T(8,128)(2,1)S(1)} %get-tuple-element.64), channel_id=1, source_target_pairs={{0,64},{1,65},{2,66},{3,67},{4,68},{5,69},{6,70},{7,71},{8,72},{9,... | collective-permute-start | bytes 688136 | tf_op jit(solution)/shard_map/ppermute | solution.py:44
  49.2 2.3 %collective-permute-done.4.refs_2_ = bf16[896,128]{1,0:T(8,128)(2,1)S(1)} collective-permute-done((bf16[896,128]{1,0:T(8,128)(2,1)}, bf16[896,128]{1,0:T(8,128)(2,1)S(1)}, u32[]{:S(2)}, u32[]{:S(2)}) %collective-permute-start.4) | collective-permute-done | bytes 229408 | tf_op jit(solution)/shard_map/ppermute | solution.py:44
  51.6 1.8 %by_expert.2 = (bf16[896,128]{1,0:T(8,128)(2,1)S(1)}, bf16[896,128]{1,0:T(8,128)(2,1)S(1)}, bf16[896,128]{1,0:T(8,128)(2,1)S(1)}, bf16[896,128]{1,0:T(8,128)(2,1)S(1)}) custom-call(s32[16]{0:T(128)S(1)} %copy-done.10, s32[1]{0:T(128)} %get-tuple-element.45.after_ref, bf16[896,128]{1,0:T(8,128)(2,1)S(1)} %copy-done.3, ...), custom_call_target="tpu_custom_call" | custom-call | flops 1000000 | bytes 2000000 | tf_op jit(solution)/shard_map/by_expert/pallas_call | solution.py:172
  53.3 1.7 %collective-permute-start.6 = (bf16[896,128]{1,0:T(8,128)(2,1)S(1)}, bf16[896,128]{1,0:T(8,128)(2,1)S(1)}, u32[]{:S(2)}, u32[]{:S(2)}) collective-permute-start(bf16[896,128]{1,0:T(8,128)(2,1)S(1)} %get-tuple-element.59), channel_id=1, source_target_pairs={{0,32},{1,97},{2,34},{3,99},{4,36},{5,101},{6,38},{7,103},{8,40},{... | collective-permute-start | bytes 688136 | tf_op jit(solution)/shard_map/ppermute | solution.py:44
  55.0 2.9 %collective-permute-start.7 = (bf16[896,128]{1,0:T(8,128)(2,1)S(1)}, bf16[896,128]{1,0:T(8,128)(2,1)S(1)}, u32[]{:S(2)}, u32[]{:S(2)}) collective-permute-start(bf16[896,128]{1,0:T(8,128)(2,1)S(1)} %get-tuple-element.60), channel_id=1, source_target_pairs={{0,64},{1,65},{2,66},{3,67},{4,68},{5,69},{6,70},{7,71},{8,72},{9,... | collective-permute-start | bytes 688136 | tf_op jit(solution)/shard_map/ppermute | solution.py:44
  59.3 3.3 %collective-permute-done.11.refs_3_ = bf16[896,128]{1,0:T(8,128)(2,1)S(1)} collective-permute-done((bf16[896,128]{1,0:T(8,128)(2,1)S(1)}, bf16[896,128]{1,0:T(8,128)(2,1)S(1)}, u32[]{:S(2)}, u32[]{:S(2)}) %collective-permute-start.11) | collective-permute-done | bytes 229408 | tf_op jit(solution)/shard_map/ppermute | solution.py:44
  62.7 1.5 %adam.2 = (f32[256,896]{1,0:T(8,128)}, f32[256,896]{1,0:T(8,128)}, f32[256,896]{1,0:T(8,128)}, bf16[128,896]{1,0:T(8,128)(2,1)S(1)}) custom-call(bf16[896,128]{1,0:T(8,128)(2,1)S(1)} %get-tuple-element.62.refs_0_, bf16[896,128]{1,0:T(8,128)(2,1)S(1)} %collective-permute-done.9.refs_1_, bf16[896,128]{1,0:T(8,128)(2,1)S(1)} %collective-permute-done.10.refs_2_, ...), custom_call_target="tpu_custom_call" | custom-call | flops 2000000 | bytes 4000000 | tf_op jit(solution)/shard_map/adam/pallas_call | solution.py:210
  64.2 4.1 %collective-permute-start.18 = (bf16[128,896]{1,0:T(8,128)(2,1)S(1)}, bf16[128,896]{1,0:T(8,128)(2,1)S(1)}, u32[]{:S(2)}, u32[]{:S(2)}) collective-permute-start(bf16[128,896]{1,0:T(8,128)(2,1)S(1)} %get-tuple-element.74.refs_0_), channel_id=1, source_target_pairs={{0,32},{1,97},{2,34},{3,99},{4,36},{5,101},{6,38},{7,103},{8,40},{... | collective-permute-start | bytes 688136 | tf_op jit(solution)/shard_map/ppermute | solution.py:44
  71.1 2.0 %collective-permute-start.13 = (bf16[128,896]{1,0:T(8,128)(2,1)S(1)}, bf16[128,896]{1,0:T(8,128)(2,1)S(1)}, u32[]{:S(2)}, u32[]{:S(2)}) collective-permute-start(bf16[128,896]{1,0:T(8,128)(2,1)S(1)} %get-tuple-element.69.refs_0_), channel_id=1, source_target_pairs={{0,64},{1,65},{2,66},{3,67},{4,68},{5,69},{6,70},{7,71},{8,72},{9,... | collective-permute-start | bytes 688136 | tf_op jit(solution)/shard_map/ppermute | solution.py:44
  73.1 5.9 %collective-permute-done.20.refs_3_ = bf16[128,896]{1,0:T(8,128)(2,1)S(1)} collective-permute-done((bf16[128,896]{1,0:T(8,128)(2,1)S(1)}, bf16[128,896]{1,0:T(8,128)(2,1)S(1)}, u32[]{:S(2)}, u32[]{:S(2)}) %collective-permute-start.20) | collective-permute-done | bytes 229408 | tf_op jit(solution)/shard_map/ppermute | solution.py:44
  80.5 4.7 %collective-permute-start.22 = (bf16[128,896]{1,0:T(8,128)(2,1)S(1)}, bf16[128,896]{1,0:T(8,128)(2,1)S(1)}, u32[]{:S(2)}, u32[]{:S(2)}) collective-permute-start(bf16[128,896]{1,0:T(8,128)(2,1)S(1)} %get-tuple-element.77), channel_id=1, source_target_pairs={{0,16},{1,17},{2,18},{3,19},{4,20},{5,21},{6,22},{7,23},{8,24},{9,... | collective-permute-start | bytes 688136 | tf_op jit(solution)/shard_map/ppermute | solution.py:44
  85.3 3.3 %collective-permute-done.14.refs_3_ = bf16[128,896]{1,0:T(8,128)(2,1)S(1)} collective-permute-done((bf16[128,896]{1,0:T(8,128)(2,1)S(1)}, bf16[128,896]{1,0:T(8,128)(2,1)S(1)}, u32[]{:S(2)}, u32[]{:S(2)}) %collective-permute-start.14) | collective-permute-done | bytes 229408 | tf_op jit(solution)/shard_map/ppermute | solution.py:44
  88.6 3.1 %collective-permute-start.23 = (bf16[128,896]{1,0:T(8,128)(2,1)S(1)}, bf16[128,896]{1,0:T(8,128)(2,1)S(1)}, u32[]{:S(2)}, u32[]{:S(2)}) collective-permute-start(bf16[128,896]{1,0:T(8,128)(2,1)S(1)} %get-tuple-element.78), channel_id=1, source_target_pairs={{0,24},{1,9},{2,26},{3,11},{4,28},{5,13},{6,30},{7,15},{8,16},{9,1... | collective-permute-start | bytes 688136 | tf_op jit(solution)/shard_map/ppermute | solution.py:44
  92.6 1.6 %collective-permute-start.16 = (bf16[128,896]{1,0:T(8,128)(2,1)S(1)}, bf16[128,896]{1,0:T(8,128)(2,1)S(1)}, u32[]{:S(2)}, u32[]{:S(2)}) collective-permute-start(bf16[128,896]{1,0:T(8,128)(2,1)S(1)} %get-tuple-element.72), channel_id=1, source_target_pairs={{0,16},{1,17},{2,18},{3,19},{4,20},{5,21},{6,22},{7,23},{8,24},{9,... | collective-permute-start | bytes 688136 | tf_op jit(solution)/shard_map/ppermute | solution.py:44
  94.1 3.1 %collective-permute-start.17 = (bf16[128,896]{1,0:T(8,128)(2,1)S(1)}, bf16[128,896]{1,0:T(8,128)(2,1)S(1)}, u32[]{:S(2)}, u32[]{:S(2)}) collective-permute-start(bf16[128,896]{1,0:T(8,128)(2,1)S(1)} %get-tuple-element.73), channel_id=1, source_target_pairs={{0,24},{1,9},{2,26},{3,11},{4,28},{5,13},{6,30},{7,15},{8,16},{9,1... | collective-permute-start | bytes 688136 | tf_op jit(solution)/shard_map/ppermute | solution.py:44
  97.3 5.7 %collective-permute-done.23.refs_3_ = bf16[128,896]{1,0:T(8,128)(2,1)S(1)} collective-permute-done((bf16[128,896]{1,0:T(8,128)(2,1)S(1)}, bf16[128,896]{1,0:T(8,128)(2,1)S(1)}, u32[]{:S(2)}, u32[]{:S(2)}) %collective-permute-start.23) | collective-permute-done | bytes 229408 | tf_op jit(solution)/shard_map/ppermute | solution.py:44
  103.9 2.2 %collective-permute-done.16.refs_2_ = bf16[128,896]{1,0:T(8,128)(2,1)S(1)} collective-permute-done((bf16[128,896]{1,0:T(8,128)(2,1)S(1)}, bf16[128,896]{1,0:T(8,128)(2,1)S(1)}, u32[]{:S(2)}, u32[]{:S(2)}) %collective-permute-start.16) | collective-permute-done | bytes 229408 | tf_op jit(solution)/shard_map/ppermute | solution.py:44
  (63 shorter events, 14.1 us)
Async XLA Ops:
  7.2 101.0 %reduce-scatter.2.cloned.1.call-start = ((), (), s32[]{:S(2)}) async-start(), calls=%async_computation.1 | async-start | bytes 7077888 | tf_op jit(solution)/shard_map/reduce_scatter | solution.py:285
  17.3 17.3 %collective-permute-start = (bf16[896,128]{1,0:T(8,128)(2,1)}, bf16[896,128]{1,0:T(8,128)(2,1)S(1)}, u32[]{:S(2)}, u32[]{:S(2)}) collective-permute-start(bf16[896,128]{1,0:T(8,128)(2,1)} %get-tuple-element.51), channel_id=1, source_target_pairs={{0,8},{1,25},{2,10},{3,27},{4,12},{5,29},{6,14},{7,31},{8,0},{9,17... | collective-permute-start | bytes 688136 | tf_op jit(solution)/shard_map/ppermute | solution.py:44
  19.4 15.2 %collective-permute-start.1 = (bf16[896,128]{1,0:T(8,128)(2,1)}, bf16[896,128]{1,0:T(8,128)(2,1)S(1)}, u32[]{:S(2)}, u32[]{:S(2)}) collective-permute-start(bf16[896,128]{1,0:T(8,128)(2,1)} %get-tuple-element.52), channel_id=1, source_target_pairs={{0,16},{1,17},{2,18},{3,19},{4,20},{5,21},{6,22},{7,23},{8,24},{9,... | collective-permute-start | bytes 688136 | tf_op jit(solution)/shard_map/ppermute | solution.py:44
  23.0 12.3 %collective-permute-start.2 = (bf16[896,128]{1,0:T(8,128)(2,1)}, bf16[896,128]{1,0:T(8,128)(2,1)S(1)}, u32[]{:S(2)}, u32[]{:S(2)}) collective-permute-start(bf16[896,128]{1,0:T(8,128)(2,1)} %get-tuple-element.53), channel_id=1, source_target_pairs={{0,24},{1,9},{2,26},{3,11},{4,28},{5,13},{6,30},{7,15},{8,16},{9,1... | collective-permute-start | bytes 688136 | tf_op jit(solution)/shard_map/ppermute | solution.py:44
  36.0 13.0 %collective-permute-start.3 = (bf16[896,128]{1,0:T(8,128)(2,1)}, bf16[896,128]{1,0:T(8,128)(2,1)S(1)}, u32[]{:S(2)}, u32[]{:S(2)}) collective-permute-start(bf16[896,128]{1,0:T(8,128)(2,1)} %get-tuple-element.55), channel_id=1, source_target_pairs={{0,8},{1,25},{2,10},{3,27},{4,12},{5,29},{6,14},{7,31},{8,0},{9,17... | collective-permute-start | bytes 688136 | tf_op jit(solution)/shard_map/ppermute | solution.py:44
  36.1 15.5 %collective-permute-start.4 = (bf16[896,128]{1,0:T(8,128)(2,1)}, bf16[896,128]{1,0:T(8,128)(2,1)S(1)}, u32[]{:S(2)}, u32[]{:S(2)}) collective-permute-start(bf16[896,128]{1,0:T(8,128)(2,1)} %get-tuple-element.56), channel_id=1, source_target_pairs={{0,16},{1,17},{2,18},{3,19},{4,20},{5,21},{6,22},{7,23},{8,24},{9,... | collective-permute-start | bytes 688136 | tf_op jit(solution)/shard_map/ppermute | solution.py:44
  44.4 13.5 %collective-permute-start.9 = (bf16[896,128]{1,0:T(8,128)(2,1)S(1)}, bf16[896,128]{1,0:T(8,128)(2,1)S(1)}, u32[]{:S(2)}, u32[]{:S(2)}) collective-permute-start(bf16[896,128]{1,0:T(8,128)(2,1)S(1)} %get-tuple-element.63), channel_id=1, source_target_pairs={{0,32},{1,97},{2,34},{3,99},{4,36},{5,101},{6,38},{7,103},{8,40},{... | collective-permute-start | bytes 688136 | tf_op jit(solution)/shard_map/ppermute | solution.py:44
  46.1 13.2 %collective-permute-start.10 = (bf16[896,128]{1,0:T(8,128)(2,1)S(1)}, bf16[896,128]{1,0:T(8,128)(2,1)S(1)}, u32[]{:S(2)}, u32[]{:S(2)}) collective-permute-start(bf16[896,128]{1,0:T(8,128)(2,1)S(1)} %get-tuple-element.64), channel_id=1, source_target_pairs={{0,64},{1,65},{2,66},{3,67},{4,68},{5,69},{6,70},{7,71},{8,72},{9,... | collective-permute-start | bytes 688136 | tf_op jit(solution)/shard_map/ppermute | solution.py:44
  49.0 13.6 %collective-permute-start.11 = (bf16[896,128]{1,0:T(8,128)(2,1)S(1)}, bf16[896,128]{1,0:T(8,128)(2,1)S(1)}, u32[]{:S(2)}, u32[]{:S(2)}) collective-permute-start(bf16[896,128]{1,0:T(8,128)(2,1)S(1)} %get-tuple-element.65), channel_id=1, source_target_pairs={{0,96},{1,33},{2,98},{3,35},{4,100},{5,37},{6,102},{7,39},{8,104},... | collective-permute-start | bytes 688136 | tf_op jit(solution)/shard_map/ppermute | solution.py:44
  53.3 10.9 %collective-permute-start.6 = (bf16[896,128]{1,0:T(8,128)(2,1)S(1)}, bf16[896,128]{1,0:T(8,128)(2,1)S(1)}, u32[]{:S(2)}, u32[]{:S(2)}) collective-permute-start(bf16[896,128]{1,0:T(8,128)(2,1)S(1)} %get-tuple-element.59), channel_id=1, source_target_pairs={{0,32},{1,97},{2,34},{3,99},{4,36},{5,101},{6,38},{7,103},{8,40},{... | collective-permute-start | bytes 688136 | tf_op jit(solution)/shard_map/ppermute | solution.py:44
  55.0 14.3 %collective-permute-start.7 = (bf16[896,128]{1,0:T(8,128)(2,1)S(1)}, bf16[896,128]{1,0:T(8,128)(2,1)S(1)}, u32[]{:S(2)}, u32[]{:S(2)}) collective-permute-start(bf16[896,128]{1,0:T(8,128)(2,1)S(1)} %get-tuple-element.60), channel_id=1, source_target_pairs={{0,64},{1,65},{2,66},{3,67},{4,68},{5,69},{6,70},{7,71},{8,72},{9,... | collective-permute-start | bytes 688136 | tf_op jit(solution)/shard_map/ppermute | solution.py:44
  57.9 11.4 %collective-permute-start.8 = (bf16[896,128]{1,0:T(8,128)(2,1)S(1)}, bf16[896,128]{1,0:T(8,128)(2,1)S(1)}, u32[]{:S(2)}, u32[]{:S(2)}) collective-permute-start(bf16[896,128]{1,0:T(8,128)(2,1)S(1)} %get-tuple-element.61), channel_id=1, source_target_pairs={{0,96},{1,33},{2,98},{3,35},{4,100},{5,37},{6,102},{7,39},{8,104},... | collective-permute-start | bytes 688136 | tf_op jit(solution)/shard_map/ppermute | solution.py:44
  64.2 14.8 %collective-permute-start.20 = (bf16[128,896]{1,0:T(8,128)(2,1)S(1)}, bf16[128,896]{1,0:T(8,128)(2,1)S(1)}, u32[]{:S(2)}, u32[]{:S(2)}) collective-permute-start(bf16[128,896]{1,0:T(8,128)(2,1)S(1)} %get-tuple-element.74.refs_0_), channel_id=1, source_target_pairs={{0,96},{1,33},{2,98},{3,35},{4,100},{5,37},{6,102},{7,39},{8,104},... | collective-permute-start | bytes 688136 | tf_op jit(solution)/shard_map/ppermute | solution.py:44
  64.2 14.8 %collective-permute-start.19 = (bf16[128,896]{1,0:T(8,128)(2,1)S(1)}, bf16[128,896]{1,0:T(8,128)(2,1)S(1)}, u32[]{:S(2)}, u32[]{:S(2)}) collective-permute-start(bf16[128,896]{1,0:T(8,128)(2,1)S(1)} %get-tuple-element.74.refs_0_), channel_id=1, source_target_pairs={{0,64},{1,65},{2,66},{3,67},{4,68},{5,69},{6,70},{7,71},{8,72},{9,... | collective-permute-start | bytes 688136 | tf_op jit(solution)/shard_map/ppermute | solution.py:44
  64.2 15.5 %collective-permute-start.18 = (bf16[128,896]{1,0:T(8,128)(2,1)S(1)}, bf16[128,896]{1,0:T(8,128)(2,1)S(1)}, u32[]{:S(2)}, u32[]{:S(2)}) collective-permute-start(bf16[128,896]{1,0:T(8,128)(2,1)S(1)} %get-tuple-element.74.refs_0_), channel_id=1, source_target_pairs={{0,32},{1,97},{2,34},{3,99},{4,36},{5,101},{6,38},{7,103},{8,40},{... | collective-permute-start | bytes 688136 | tf_op jit(solution)/shard_map/ppermute | solution.py:44
  70.9 17.8 %collective-permute-start.14 = (bf16[128,896]{1,0:T(8,128)(2,1)S(1)}, bf16[128,896]{1,0:T(8,128)(2,1)S(1)}, u32[]{:S(2)}, u32[]{:S(2)}) collective-permute-start(bf16[128,896]{1,0:T(8,128)(2,1)S(1)} %get-tuple-element.69.refs_0_), channel_id=1, source_target_pairs={{0,96},{1,33},{2,98},{3,35},{4,100},{5,37},{6,102},{7,39},{8,104},... | collective-permute-start | bytes 688136 | tf_op jit(solution)/shard_map/ppermute | solution.py:44
  71.1 20.7 %collective-permute-start.13 = (bf16[128,896]{1,0:T(8,128)(2,1)S(1)}, bf16[128,896]{1,0:T(8,128)(2,1)S(1)}, u32[]{:S(2)}, u32[]{:S(2)}) collective-permute-start(bf16[128,896]{1,0:T(8,128)(2,1)S(1)} %get-tuple-element.69.refs_0_), channel_id=1, source_target_pairs={{0,64},{1,65},{2,66},{3,67},{4,68},{5,69},{6,70},{7,71},{8,72},{9,... | collective-permute-start | bytes 688136 | tf_op jit(solution)/shard_map/ppermute | solution.py:44
  79.0 12.8 %collective-permute-start.12 = (bf16[128,896]{1,0:T(8,128)(2,1)S(1)}, bf16[128,896]{1,0:T(8,128)(2,1)S(1)}, u32[]{:S(2)}, u32[]{:S(2)}) collective-permute-start(bf16[128,896]{1,0:T(8,128)(2,1)S(1)} %get-tuple-element.69.refs_0_), channel_id=1, source_target_pairs={{0,32},{1,97},{2,34},{3,99},{4,36},{5,101},{6,38},{7,103},{8,40},{... | collective-permute-start | bytes 688136 | tf_op jit(solution)/shard_map/ppermute | solution.py:44
  80.4 13.7 %collective-permute-start.21 = (bf16[128,896]{1,0:T(8,128)(2,1)S(1)}, bf16[128,896]{1,0:T(8,128)(2,1)S(1)}, u32[]{:S(2)}, u32[]{:S(2)}) collective-permute-start(bf16[128,896]{1,0:T(8,128)(2,1)S(1)} %get-tuple-element.76), channel_id=1, source_target_pairs={{0,8},{1,25},{2,10},{3,27},{4,12},{5,29},{6,14},{7,31},{8,0},{9,17... | collective-permute-start | bytes 688136 | tf_op jit(solution)/shard_map/ppermute | solution.py:44
  80.5 16.7 %collective-permute-start.22 = (bf16[128,896]{1,0:T(8,128)(2,1)S(1)}, bf16[128,896]{1,0:T(8,128)(2,1)S(1)}, u32[]{:S(2)}, u32[]{:S(2)}) collective-permute-start(bf16[128,896]{1,0:T(8,128)(2,1)S(1)} %get-tuple-element.77), channel_id=1, source_target_pairs={{0,16},{1,17},{2,18},{3,19},{4,20},{5,21},{6,22},{7,23},{8,24},{9,... | collective-permute-start | bytes 688136 | tf_op jit(solution)/shard_map/ppermute | solution.py:44
  88.6 14.4 %collective-permute-start.23 = (bf16[128,896]{1,0:T(8,128)(2,1)S(1)}, bf16[128,896]{1,0:T(8,128)(2,1)S(1)}, u32[]{:S(2)}, u32[]{:S(2)}) collective-permute-start(bf16[128,896]{1,0:T(8,128)(2,1)S(1)} %get-tuple-element.78), channel_id=1, source_target_pairs={{0,24},{1,9},{2,26},{3,11},{4,28},{5,13},{6,30},{7,15},{8,16},{9,1... | collective-permute-start | bytes 688136 | tf_op jit(solution)/shard_map/ppermute | solution.py:44
  92.5 11.5 %collective-permute-start.15 = (bf16[128,896]{1,0:T(8,128)(2,1)S(1)}, bf16[128,896]{1,0:T(8,128)(2,1)S(1)}, u32[]{:S(2)}, u32[]{:S(2)}) collective-permute-start(bf16[128,896]{1,0:T(8,128)(2,1)S(1)} %get-tuple-element.71), channel_id=1, source_target_pairs={{0,8},{1,25},{2,10},{3,27},{4,12},{5,29},{6,14},{7,31},{8,0},{9,17... | collective-permute-start | bytes 688136 | tf_op jit(solution)/shard_map/ppermute | solution.py:44
  92.6 13.6 %collective-permute-start.16 = (bf16[128,896]{1,0:T(8,128)(2,1)S(1)}, bf16[128,896]{1,0:T(8,128)(2,1)S(1)}, u32[]{:S(2)}, u32[]{:S(2)}) collective-permute-start(bf16[128,896]{1,0:T(8,128)(2,1)S(1)} %get-tuple-element.72), channel_id=1, source_target_pairs={{0,16},{1,17},{2,18},{3,19},{4,20},{5,21},{6,22},{7,23},{8,24},{9,... | collective-permute-start | bytes 688136 | tf_op jit(solution)/shard_map/ppermute | solution.py:44
  94.1 13.0 %collective-permute-start.17 = (bf16[128,896]{1,0:T(8,128)(2,1)S(1)}, bf16[128,896]{1,0:T(8,128)(2,1)S(1)}, u32[]{:S(2)}, u32[]{:S(2)}) collective-permute-start(bf16[128,896]{1,0:T(8,128)(2,1)S(1)} %get-tuple-element.73), channel_id=1, source_target_pairs={{0,24},{1,9},{2,26},{3,11},{4,28},{5,13},{6,30},{7,15},{8,16},{9,1... | collective-permute-start | bytes 688136 | tf_op jit(solution)/shard_map/ppermute | solution.py:44
  (14 other events, 174.7 us)
Sparse Core Ops, SparseCore 0:
  36.1 44.0 reduce-scatter.1

commit v3 on v2

v3 whole, which is shorter than its diff:
```python
import functools

import jax
import jax.numpy as jnp
from jax import lax
from jax.experimental import pallas as pl
from jax.experimental.pallas import tpu as pltpu
from jax.sharding import PartitionSpec as P

beta_one = 0.9
beta_two = 0.95
learn_rate = 0.5
weight_decay = 0.1
epsilon = 1e-08
adam_step = 20

RING = 4
CHUNKS = 2
bf16 = jnp.bfloat16
f32 = jnp.float32


def params(limit, *semantics):
    return pltpu.CompilerParams(vmem_limit_bytes=int(limit * 2**20), dimension_semantics=semantics or None)


BUSY = pl.CostEstimate(flops=10_000_000_000, bytes_accessed=14_000_000, transcendentals=0)
BRIEF = pl.CostEstimate(flops=0, bytes_accessed=1024, transcendentals=0)
TURN = jax.ShapeDtypeStruct((1,), jnp.int32)
VMEM = pl.BlockSpec(memory_space=pltpu.VMEM)
SMEM = pl.BlockSpec(memory_space=pltpu.SMEM)
ANY = pl.BlockSpec(memory_space=pl.ANY)
HBM = pl.BlockSpec(memory_space=pltpu.HBM)


def turned(distance, core):
    return distance ^ ((distance & 1) * 2 * core)


def along(stride):
    def move(value, distance):
        pairs = [
            (slot * 2 * RING + shard, (slot ^ (turned(distance, shard % 2) * stride)) * 2 * RING + shard)
            for slot in range(RING * RING)
            for shard in range(2 * RING)
        ]
        return lax.ppermute(value, ("slot", "shard"), pairs)

    return move


move_z = along(1)
move_y = along(RING)


def exchange(move, pieces):
    return [pieces[0]] + [move(pieces[distance], distance) for distance in range(1, RING)]


def my_place():
    slot = lax.axis_index("slot")
    return slot // RING, slot % RING, lax.axis_index("shard") % 2


def slot_grads(chunk, counts, acts, out_grads, scale, after):
    tokens, ff = acts.shape
    width = out_grads.shape[1]
    quarter = ff // RING
    part = quarter // CHUNKS
    blocks = [256, 512, 768, 768, 768]
    starts = [sum(blocks[:i]) for i in range(len(blocks))]
    assert sum(blocks) == tokens

    def kernel(count_ref, acts_hbm, grads_hbm, *rest):
        outs, (acts_ref, grads_ref, total, sems) = rest[-4 - RING : -4], rest[-4:]
        _, z, core = my_place()
        copies = []
        for i, (start, block) in enumerate(zip(starts, blocks)):
            rows = pl.ds(start, block)
            group = [pltpu.make_async_copy(grads_hbm.at[rows, :], grads_ref.at[rows, :], sems.at[i, RING])]
            for distance in range(RING):
                column = pl.multiple_of((z ^ turned(distance, core)) * quarter + chunk * part, part)
                source = acts_hbm.at[rows, pl.ds(column, part)]
                target = acts_ref.at[rows, pl.ds(distance * part, part)]
                group.append(pltpu.make_async_copy(source, target, sems.at[i, distance]))
            copies.append(group)
        for group in copies:
            for copy in group:
                copy.start()
        for i, (start, block) in enumerate(zip(starts, blocks)):
            for copy in copies[i]:
                copy.wait()
            rows = lax.broadcasted_iota(jnp.int32, (block, width), 0)
            grads = grads_ref[start : start + block, :]
            masked = jnp.where(rows < count_ref[0] - start, grads, jnp.zeros_like(grads))
            term = lax.dot_general(
                acts_ref[start : start + block, :], masked, (((0,), (0,)), ((), ())), preferred_element_type=f32
            )
            if i < len(blocks) - 1:
                total[...] = term if i == 0 else total[...] + term
            else:
                term = ((total[...] + term) * scale).astype(bf16)
                for distance in range(RING):
                    outs[distance][...] = term[distance * part : (distance + 1) * part, :]

    return pl.pallas_call(
        kernel,
        in_specs=[SMEM, HBM, HBM] + [ANY] * len(after),
        out_specs=[VMEM] * RING,
        out_shape=[jax.ShapeDtypeStruct((part, width), bf16)] * RING,
        scratch_shapes=[
            pltpu.VMEM((tokens, RING * part), bf16),
            pltpu.VMEM((tokens, width), bf16),
            pltpu.VMEM((RING * part, width), f32),
            pltpu.SemaphoreType.DMA((len(blocks), RING + 1)),
        ],
        compiler_params=params(57.25),
        cost_estimate=BUSY,
        name="slot_grads",
    )(counts, acts, out_grads, *after)


def act_terms(counts, out_grads, weight, scale, after):
    tokens, width = out_grads.shape
    ff = weight.shape[0]
    block = 1024
    steps = tokens // block
    columns = ff // (2 * RING)

    def kernel(count_ref, grads_ref, weight_ref, *rest):
        out_ref, turn_ref = rest[-2:]
        turn_ref[0] = 0
        live = count_ref[0] - pl.program_id(0) * block
        term = lax.dot_general(grads_ref[...], weight_ref[...], (((1,), (1,)), ((), ())), preferred_element_type=f32)
        rows = lax.broadcasted_iota(jnp.int32, term.shape, 0)
        term = jnp.where(rows < live, term * scale, 0.0).astype(bf16)
        for piece in range(2 * RING):
            out_ref[piece] = term[:, piece * columns : (piece + 1) * columns]

    return pl.pallas_call(
        kernel,
        grid_spec=pltpu.PrefetchScalarGridSpec(
            num_scalar_prefetch=1,
            grid=(steps,),
            in_specs=[
                pl.BlockSpec((block, width), lambda i, c: (i, 0)),
                pl.BlockSpec((ff, width), lambda i, c: (0, 0)),
            ]
            + [ANY] * len(after),
            out_specs=[pl.BlockSpec((2 * RING, block, columns), lambda i, c: (0, i, 0)), SMEM],
        ),
        out_shape=[jax.ShapeDtypeStruct((2 * RING, tokens, columns), bf16), TURN],
        compiler_params=params(50, "arbitrary"),
        cost_estimate=BUSY,
        name="act_terms",
    )(counts, out_grads, weight, *after)


def by_expert(replica_map, pieces, after=(), behind=()):
    shape = pieces[0].shape

    def kernel(map_ref, *refs):
        ins, outs = refs[:RING], refs[-RING:]
        y, z, core = my_place()
        values = [ref[...].astype(f32) for ref in ins]
        held = [map_ref[RING * y + (z ^ turned(distance, core))] for distance in range(RING)]
        for step in range(RING):
            expert = y ^ turned(step, core)
            total = jnp.where(held[0] == expert, values[0], 0.0)
            for value, one in zip(values[1:], held[1:]):
                total = total + jnp.where(one == expert, value, 0.0)
            outs[step][...] = total.astype(bf16)

    return pl.pallas_call(
        kernel,
        in_specs=[SMEM] + [VMEM] * RING + [SMEM] * len(after) + [ANY] * len(behind),
        out_specs=[VMEM] * RING,
        out_shape=[jax.ShapeDtypeStruct(shape, bf16)] * RING,
        compiler_params=params(16),
        cost_estimate=BRIEF,
        name="by_expert",
    )(replica_map, *pieces, *after, *behind)


def adam_update(grad_total, master, moment1, moment2):
    new_first = beta_one * moment1 + (1.0 - beta_one) * grad_total
    new_second = beta_two * moment2 + (1.0 - beta_two) * grad_total * grad_total
    first_hat = new_first / (1.0 - beta_one**adam_step)
    second_hat = new_second / (1.0 - beta_two**adam_step)
    update = first_hat / (jnp.sqrt(second_hat) + epsilon)
    master_new = master - learn_rate * (update + weight_decay * master)
    return (master_new, new_first, new_second)


def adam(chunk, pieces, state, earlier, turns=0, behind=()):
    rows, width = state[0].shape
    part = rows // CHUNKS

    def kernel(*refs):
        terms = [ref[...].astype(f32) for ref in refs[:RING]]
        master, moment1, moment2 = refs[RING : RING + 3]
        outs = refs[-4 - turns :]
        if turns:
            outs[4][0] = 0
        grad = (terms[0] + terms[1]) + (terms[2] + terms[3])
        master_new, new_first, new_second = adam_update(grad, master[...], moment1[...], moment2[...])
        outs[0][...] = master_new
        outs[1][...] = new_first
        outs[2][...] = new_second
        outs[3][...] = master_new.astype(bf16)

    whole = jax.ShapeDtypeStruct((rows, width), f32)
    mine = pl.BlockSpec((part, width), lambda i: (chunk, 0))
    return pl.pallas_call(
        kernel,
        grid=(1,),
        in_specs=[pl.BlockSpec((part, width), lambda i: (0, 0))] + [VMEM] * (RING - 1) + [mine] * 3 + [ANY] * (len(earlier) + len(behind)),
        out_specs=[mine] * 3 + [VMEM] + [SMEM] * turns,
        out_shape=[whole] * 3 + [jax.ShapeDtypeStruct((part, width), bf16)] + [TURN] * turns,
        input_output_aliases={RING + 3 + i: i for i in range(len(earlier))},
        compiler_params=params(16, "arbitrary"),
        cost_estimate=BRIEF,
        name="adam",
    )(*pieces, *state, *earlier, *behind)


def by_slot(next_map, pieces):
    def kernel(map_ref, *refs):
        ins, outs = refs[:RING], refs[RING:]
        y, z, core = my_place()
        for distance in range(RING):
            wanted = turned(map_ref[RING * y + (z ^ turned(distance, core))] ^ y, core)
            for step in range(RING):

                @pl.when(wanted == step)
                def _(step=step, distance=distance):
                    outs[distance][...] = ins[step][...]

    shape = pieces[0].shape
    return pl.pallas_call(
        kernel,
        in_specs=[SMEM] + [VMEM] * RING,
        out_specs=[VMEM] * RING,
        out_shape=[jax.ShapeDtypeStruct(shape, bf16)] * RING,
        compiler_params=params(16),
        cost_estimate=BRIEF,
        name="by_slot",
    )(next_map, *pieces)


def put_rows(chunk, pieces, ff, earlier, after=()):
    part, width = pieces[0].shape

    def kernel(*refs):
        ins, out, sems = refs[:RING], refs[-2], refs[-1]
        _, z, core = my_place()
        copies = []
        for distance in range(RING):
            start = (z ^ turned(distance, core)) * (part * CHUNKS) + chunk * part
            target = out.at[pl.ds(pl.multiple_of(start, part), part), :]
            copies.append(pltpu.make_async_copy(ins[distance], target, sems.at[distance]))
        for copy in copies:
            copy.start()
        for copy in copies:
            copy.wait()

    return pl.pallas_call(
        kernel,
        in_specs=[VMEM] * RING + [ANY] * len(earlier) + [SMEM] * len(after),
        out_specs=ANY,
        out_shape=jax.ShapeDtypeStruct((ff, width), bf16),
        scratch_shapes=[pltpu.SemaphoreType.DMA((RING,))],
        input_output_aliases={RING: 0} if earlier else {},
        compiler_params=params(16),
        cost_estimate=BRIEF,
        name="put_rows",
    )(*pieces, *earlier, *after)


def local(acts, out_grads, counts, replica_map, next_map, slot_weights, master, moment1, moment2):
    hidden, grads, weight = acts[0], out_grads[0], slot_weights[0]
    ff = hidden.shape[1]
    scale = ff**-0.5

    first = slot_grads(0, counts, hidden, grads, scale, ())
    second = slot_grads(1, counts, hidden, grads, scale, first[:1])
    along_z = [exchange(move_z, first), exchange(move_z, second)]
    sums = by_expert(replica_map, along_z[0])
    early = exchange(move_y, sums)
    terms, turn = act_terms(counts, grads, weight, scale, (sums[0], second[0]))
    sums = by_expert(replica_map, along_z[1], (turn,), early[1:])
    late = exchange(move_y, sums)
    *state, rows, turn = adam(0, early, (master, moment1, moment2), (), 1, sums[:1])
    terms, turn = lax.optimization_barrier((terms, turn))
    act_grads = lax.psum_scatter(terms, "shard", scatter_dimension=0, tiled=False)
    fresh = [exchange(move_y, [rows] * RING)]
    *state, rows = adam(1, late, (master, moment1, moment2), tuple(state))
    fresh.append(exchange(move_y, [rows] * RING))
    wanted = [exchange(move_z, by_slot(next_map, pieces)) for pieces in fresh]
    new_weight = put_rows(0, wanted[0], ff, (), (turn,))
    new_weight = put_rows(1, wanted[1], ff, (new_weight,))
    return (new_weight[None], *state, act_grads[None])


def solution(mesh):
    placed = (
        P("slot", None, None),
        P("slot", None, "shard"),
        P("slot"),
        P(),
        P(),
        P("slot", None, "shard"),
        P("slot", "shard"),
        P("slot", "shard"),
        P("slot", "shard"),
    )
    return jax.shard_map(
        local,
        mesh=mesh,
        in_specs=placed,
        out_specs=(
            P("slot", None, "shard"),
            P("slot", "shard"),
            P("slot", "shard"),
            P("slot", "shard"),
            P("slot", None, "shard"),
        ),
        check_vma=False,
    )
```

time: 115 us -> 112 us (0.974)
  local copies, waits for them, and re-layouts: 4.22 us -> 0.98 us
  starting transfers between devices: 39 us -> 36.5 us
  Pallas kernels: 30 us -> 32.2 us
    unnamed x26 -> x20, local copies, waits for them, and re-layouts: 4.22 us -> 0.98 us
    pallas_call x7 -> x8, Pallas kernels: 17.9 us -> 20.6 us  [the longest x2 12.3 us: slot_grads(): pl.pallas_call(kernel, in_specs=[SMEM, HBM, HBM] + [ANY] * len(after), ou...]
    ppermute x24, starting transfers between devices: 39 us -> 36.5 us  [move(): return lax.ppermute(value, ('slot', 'shard'), pairs)]
  transfers between devices with their start and end apart: 25 -> 25, of which waited for: 10 -> 8; matrix products, arithmetic and copies ran while one was open for 0% -> 0% of each run, Pallas kernels for 18% -> 20%
where the time goes in v3:
time: 112 us
  starting transfers between devices  36.5 us (33%)
  Pallas kernels  32.2 us (29%)
  waiting for transfers between devices  27.1 us (24%)
  between operations  14.9 us (13%)
    ppermute x24, starting transfers between devices, move(): return lax.ppermute(value, ('slot', 'shard'), pairs)  36.5 us
    ppermute x24, waiting for transfers between devices, move(): return lax.ppermute(value, ('slot', 'shard'), pairs)  27.1 us
    pallas_call x2, Pallas kernels, slot_grads(): pl.pallas_call(kernel, in_specs=[SMEM, HBM, HBM] + [ANY] * len(after), ou...  12.3 us
    pallas_call x1, Pallas kernels, act_terms(): pl.pallas_call(kernel, grid_spec=pltpu.PrefetchScalarGridSpec(num_scalar_...  10.1 us
    pallas_call x2, Pallas kernels, adam(): pl.pallas_call(kernel, grid=(1,), in_specs=[pl.BlockSpec((part, width), l...  3.01 us
    pallas_call x2, Pallas kernels, by_expert(): pl.pallas_call(kernel, in_specs=[SMEM] + [VMEM] * RING + [SMEM] * len(aft...  2.79 us
    pallas_call x2, Pallas kernels, put_rows(): pl.pallas_call(kernel, in_specs=[VMEM] * RING + [ANY] * len(earlier) + [S...  2.52 us
  transfers between devices with their start and end apart: 25, of which 8 were waited for; matrix products, arithmetic and copies ran while one was open for 0% of the time, Pallas kernels for 20%

profile of v3, /device:TPU:0, one launch (start us, length us, event | category | flops | bytes accessed | tf_op | source)
XLA Modules:
  0.0 111.7 jit_solution(6272541587454711698)
XLA Ops:
  7.9 6.1 %slot_grads.2 = (bf16[128,896]{1,0:T(8,128)(2,1)}, bf16[128,896]{1,0:T(8,128)(2,1)}, bf16[128,896]{1,0:T(8,128)(2,1)}, bf16[128,896]{1,0:T(8,128)(2,1)}) custom-call(s32[1]{0:T(128)S(6)} %copy.22.count_ref, bf16[3072,1024]{1,0:T(8,128)(2,1)} %bitcast.6, bf16[3072,896]{1,0:T(8,128)(2,1)} %bitcast.8), custom_call_target="tpu_custom_call" | custom-call | flops 10000000000 | bytes 14000000 | tf_op jit(solution)/shard_map/slot_grads/pallas_call | solution.py:106
  13.9 2.1 %collective-permute-start.3 = (bf16[128,896]{1,0:T(8,128)(2,1)}, bf16[128,896]{1,0:T(8,128)(2,1)S(1)}, u32[]{:S(2)}, u32[]{:S(2)}) collective-permute-start(bf16[128,896]{1,0:T(8,128)(2,1)} %get-tuple-element.47), channel_id=1, source_target_pairs={{0,8},{1,25},{2,10},{3,27},{4,12},{5,29},{6,14},{7,31},{8,0},{9,17... | collective-permute-start | bytes 688136 | tf_op jit(solution)/shard_map/ppermute | solution.py:47
  16.0 3.6 %collective-permute-start.4 = (bf16[128,896]{1,0:T(8,128)(2,1)}, bf16[128,896]{1,0:T(8,128)(2,1)S(1)}, u32[]{:S(2)}, u32[]{:S(2)}) collective-permute-start(bf16[128,896]{1,0:T(8,128)(2,1)} %get-tuple-element.48), channel_id=1, source_target_pairs={{0,16},{1,17},{2,18},{3,19},{4,20},{5,21},{6,22},{7,23},{8,24},{9,... | collective-permute-start | bytes 688136 | tf_op jit(solution)/shard_map/ppermute | solution.py:47
  19.6 6.2 %slot_grads.3 = (bf16[128,896]{1,0:T(8,128)(2,1)}, bf16[128,896]{1,0:T(8,128)(2,1)}, bf16[128,896]{1,0:T(8,128)(2,1)}, bf16[128,896]{1,0:T(8,128)(2,1)}) custom-call(s32[1]{0:T(128)S(6)} %copy.22.count_ref, bf16[3072,1024]{1,0:T(8,128)(2,1)} %bitcast.7, bf16[3072,896]{1,0:T(8,128)(2,1)} %bitcast.9, bf16[128,896]{1,0:T(8,128)(2,1)} %get-tuple-element.42.rest_0_.refs_0_), custom_call_target="tpu_custom_call" | custom-call | flops 10000000000 | bytes 14000000 | tf_op jit(solution)/shard_map/slot_grads/pallas_call | solution.py:106
  25.9 4.7 %collective-permute-start.1 = (bf16[128,896]{1,0:T(8,128)(2,1)}, bf16[128,896]{1,0:T(8,128)(2,1)S(1)}, u32[]{:S(2)}, u32[]{:S(2)}) collective-permute-start(bf16[128,896]{1,0:T(8,128)(2,1)} %get-tuple-element.45), channel_id=1, source_target_pairs={{0,16},{1,17},{2,18},{3,19},{4,20},{5,21},{6,22},{7,23},{8,24},{9,... | collective-permute-start | bytes 688136 | tf_op jit(solution)/shard_map/ppermute | solution.py:47
  32.6 1.7 %collective-permute-start.6 = (bf16[128,896]{1,0:T(8,128)(2,1)S(1)}, bf16[128,896]{1,0:T(8,128)(2,1)S(1)}, u32[]{:S(2)}, u32[]{:S(2)}) collective-permute-start(bf16[128,896]{1,0:T(8,128)(2,1)S(1)} %get-tuple-element.52), channel_id=1, source_target_pairs={{0,32},{1,97},{2,34},{3,99},{4,36},{5,101},{6,38},{7,103},{8,40},{... | collective-permute-start | bytes 688136 | tf_op jit(solution)/shard_map/ppermute | solution.py:47
  34.3 2.9 %collective-permute-start.7 = (bf16[128,896]{1,0:T(8,128)(2,1)S(1)}, bf16[128,896]{1,0:T(8,128)(2,1)S(1)}, u32[]{:S(2)}, u32[]{:S(2)}) collective-permute-start(bf16[128,896]{1,0:T(8,128)(2,1)S(1)} %get-tuple-element.53), channel_id=1, source_target_pairs={{0,64},{1,65},{2,66},{3,67},{4,68},{5,69},{6,70},{7,71},{8,72},{9,... | collective-permute-start | bytes 688136 | tf_op jit(solution)/shard_map/ppermute | solution.py:47
  38.5 10.1 %act_terms.1 = (bf16[8,3072,128]{2,1,0:T(8,128)(2,1)}, s32[1]{0:T(128)}) custom-call(s32[1]{0:T(128)S(6)} %copy.22.count_ref, bf16[3072,896]{1,0:T(8,128)(2,1)} %bitcast.10, bf16[1024,896]{1,0:T(8,128)(2,1)S(1)} %bitcast.4, bf16[128,896]{1,0:T(8,128)(2,1)S(1)} %get-tuple-element.50.rest_0_.refs_0_, bf16[128,896]{1,0:T(8,128)(2,1)S(1)} %copy-done.4), custom_call_target="tpu_custom_call" | custom-call | flops 10000000000 | bytes 14000000 | tf_op jit(solution)/shard_map/act_terms/pallas_call | solution.py:140
  48.6 1.7 %by_expert.3 = (bf16[128,896]{1,0:T(8,128)(2,1)S(1)}, bf16[128,896]{1,0:T(8,128)(2,1)S(1)}, bf16[128,896]{1,0:T(8,128)(2,1)S(1)}, bf16[128,896]{1,0:T(8,128)(2,1)S(1)}) custom-call(s32[16]{0:T(128)S(1)} %copy-done.5, bf16[128,896]{1,0:T(8,128)(2,1)S(1)} %copy-done.4, bf16[128,896]{1,0:T(8,128)(2,1)S(1)} %collective-permute-done.refs_1_, ...), custom_call_target="tpu_custom_call" | custom-call | bytes 1024 | tf_op jit(solution)/shard_map/by_expert/pallas_call | solution.py:174
  50.4 1.5 %adam.2 = (f32[256,896]{1,0:T(8,128)}, f32[256,896]{1,0:T(8,128)}, f32[256,896]{1,0:T(8,128)}, bf16[128,896]{1,0:T(8,128)(2,1)S(1)}, s32[1]{0:T(128)}) custom-call(bf16[128,896]{1,0:T(8,128)(2,1)S(1)} %get-tuple-element.50.rest_0_.refs_0_, bf16[128,896]{1,0:T(8,128)(2,1)S(1)} %collective-permute-done.6.refs_5_.refs_1_, ...), custom_call_target="tpu_custom_call" | custom-call | bytes 1024 | tf_op jit(solution)/shard_map/adam/pallas_call | solution.py:214
  52.3 4.1 %collective-permute-start.10 = (bf16[128,896]{1,0:T(8,128)(2,1)}, bf16[128,896]{1,0:T(8,128)(2,1)S(1)}, u32[]{:S(2)}, u32[]{:S(2)}) collective-permute-start(bf16[128,896]{1,0:T(8,128)(2,1)} %copy-done.8), channel_id=1, source_target_pairs={{0,64},{1,65},{2,66},{3,67},{4,68},{5,69},{6,70},{7,71},{8,72},{9,... | collective-permute-start | bytes 688136 | tf_op jit(solution)/shard_map/ppermute | solution.py:47
  56.8 2.9 %collective-permute-start.20 = (bf16[128,896]{1,0:T(8,128)(2,1)S(1)}, bf16[128,896]{1,0:T(8,128)(2,1)S(1)}, u32[]{:S(2)}, u32[]{:S(2)}) collective-permute-start(bf16[128,896]{1,0:T(8,128)(2,1)S(1)} %get-tuple-element.67.refs_0_), channel_id=1, source_target_pairs={{0,96},{1,33},{2,98},{3,35},{4,100},{5,37},{6,102},{7,39},{8,104},... | collective-permute-start | bytes 688136 | tf_op jit(solution)/shard_map/ppermute | solution.py:47
  60.9 7.1 %collective-permute-done.10.refs_2_ = bf16[128,896]{1,0:T(8,128)(2,1)S(1)} collective-permute-done((bf16[128,896]{1,0:T(8,128)(2,1)}, bf16[128,896]{1,0:T(8,128)(2,1)S(1)}, u32[]{:S(2)}, u32[]{:S(2)}) %collective-permute-start.10) | collective-permute-done | bytes 229408 | tf_op jit(solution)/shard_map/ppermute | solution.py:47
  68.0 1.5 %adam.3 = (f32[256,896]{1,0:T(8,128)}, f32[256,896]{1,0:T(8,128)}, f32[256,896]{1,0:T(8,128)}, bf16[128,896]{1,0:T(8,128)(2,1)S(1)}) custom-call(bf16[128,896]{1,0:T(8,128)(2,1)S(1)} %get-tuple-element.55.refs_7_.refs_0_, bf16[128,896]{1,0:T(8,128)(2,1)S(1)} %collective-permute-done.9.refs_1_, ...), custom_call_target="tpu_custom_call", output_to_operand_aliasing={{0}: (7, {}), {1}: (8, {}), {2}: (9, {})} | custom-call | bytes 1024 | tf_op jit(solution)/shard_map/adam/pallas_call | solution.py:214
  69.9 2.0 %collective-permute-start.13 = (bf16[128,896]{1,0:T(8,128)(2,1)S(1)}, bf16[128,896]{1,0:T(8,128)(2,1)S(1)}, u32[]{:S(2)}, u32[]{:S(2)}) collective-permute-start(bf16[128,896]{1,0:T(8,128)(2,1)S(1)} %get-tuple-element.62.refs_0_), channel_id=1, source_target_pairs={{0,64},{1,65},{2,66},{3,67},{4,68},{5,69},{6,70},{7,71},{8,72},{9,... | collective-permute-start | bytes 688136 | tf_op jit(solution)/shard_map/ppermute | solution.py:47
  71.9 4.9 %collective-permute-done.20.refs_3_ = bf16[128,896]{1,0:T(8,128)(2,1)S(1)} collective-permute-done((bf16[128,896]{1,0:T(8,128)(2,1)S(1)}, bf16[128,896]{1,0:T(8,128)(2,1)S(1)}, u32[]{:S(2)}, u32[]{:S(2)}) %collective-permute-start.20) | collective-permute-done | bytes 229408 | tf_op jit(solution)/shard_map/ppermute | solution.py:47
  77.6 3.8 %collective-permute-start.22 = (bf16[128,896]{1,0:T(8,128)(2,1)S(1)}, bf16[128,896]{1,0:T(8,128)(2,1)S(1)}, u32[]{:S(2)}, u32[]{:S(2)}) collective-permute-start(bf16[128,896]{1,0:T(8,128)(2,1)S(1)} %get-tuple-element.70), channel_id=1, source_target_pairs={{0,16},{1,17},{2,18},{3,19},{4,20},{5,21},{6,22},{7,23},{8,24},{9,... | collective-permute-start | bytes 688136 | tf_op jit(solution)/shard_map/ppermute | solution.py:47
  81.4 4.3 %collective-permute-done.14.refs_3_ = bf16[128,896]{1,0:T(8,128)(2,1)S(1)} collective-permute-done((bf16[128,896]{1,0:T(8,128)(2,1)S(1)}, bf16[128,896]{1,0:T(8,128)(2,1)S(1)}, u32[]{:S(2)}, u32[]{:S(2)}) %collective-permute-start.14) | collective-permute-done | bytes 229408 | tf_op jit(solution)/shard_map/ppermute | solution.py:47
  85.7 2.3 %collective-permute-start.23 = (bf16[128,896]{1,0:T(8,128)(2,1)S(1)}, bf16[128,896]{1,0:T(8,128)(2,1)S(1)}, u32[]{:S(2)}, u32[]{:S(2)}) collective-permute-start(bf16[128,896]{1,0:T(8,128)(2,1)S(1)} %get-tuple-element.71), channel_id=1, source_target_pairs={{0,24},{1,9},{2,26},{3,11},{4,28},{5,13},{6,30},{7,15},{8,16},{9,1... | collective-permute-start | bytes 688136 | tf_op jit(solution)/shard_map/ppermute | solution.py:47
  88.9 2.4 %collective-permute-start.16 = (bf16[128,896]{1,0:T(8,128)(2,1)S(1)}, bf16[128,896]{1,0:T(8,128)(2,1)S(1)}, u32[]{:S(2)}, u32[]{:S(2)}) collective-permute-start(bf16[128,896]{1,0:T(8,128)(2,1)S(1)} %get-tuple-element.65), channel_id=1, source_target_pairs={{0,16},{1,17},{2,18},{3,19},{4,20},{5,21},{6,22},{7,23},{8,24},{9,... | collective-permute-start | bytes 688136 | tf_op jit(solution)/shard_map/ppermute | solution.py:47
  91.2 2.3 %collective-permute-start.17 = (bf16[128,896]{1,0:T(8,128)(2,1)S(1)}, bf16[128,896]{1,0:T(8,128)(2,1)S(1)}, u32[]{:S(2)}, u32[]{:S(2)}) collective-permute-start(bf16[128,896]{1,0:T(8,128)(2,1)S(1)} %get-tuple-element.66), channel_id=1, source_target_pairs={{0,24},{1,9},{2,26},{3,11},{4,28},{5,13},{6,30},{7,15},{8,16},{9,1... | collective-permute-start | bytes 688136 | tf_op jit(solution)/shard_map/ppermute | solution.py:47
  93.6 6.7 %collective-permute-done.23.refs_3_ = bf16[128,896]{1,0:T(8,128)(2,1)S(1)} collective-permute-done((bf16[128,896]{1,0:T(8,128)(2,1)S(1)}, bf16[128,896]{1,0:T(8,128)(2,1)S(1)}, u32[]{:S(2)}, u32[]{:S(2)}) %collective-permute-start.23) | collective-permute-done | bytes 229408 | tf_op jit(solution)/shard_map/ppermute | solution.py:47
  100.2 1.6 %put_rows.2.refs_4_ = bf16[1024,896]{1,0:T(8,128)(2,1)} custom-call(bf16[128,896]{1,0:T(8,128)(2,1)S(1)} %get-tuple-element.68.refs_0_, bf16[128,896]{1,0:T(8,128)(2,1)S(1)} %collective-permute-done.21.refs_1_, bf16[128,896]{1,0:T(8,128)(2,1)S(1)} %collective-permute-done.22.refs_2_, bf16[128,896]{1,0:T(8,128)(2,1)S(1)} %collective-permute-done.23.refs_3_, ...), custom_call_target="tpu_custom_call" | custom-call | bytes 1024 | tf_op jit(solution)/shard_map/put_rows/pallas_call | solution.py:267
  102.6 1.3 %collective-permute-done.17.refs_3_ = bf16[128,896]{1,0:T(8,128)(2,1)S(1)} collective-permute-done((bf16[128,896]{1,0:T(8,128)(2,1)S(1)}, bf16[128,896]{1,0:T(8,128)(2,1)S(1)}, u32[]{:S(2)}, u32[]{:S(2)}) %collective-permute-start.17) | collective-permute-done | bytes 229408 | tf_op jit(solution)/shard_map/ppermute | solution.py:47
  (58 shorter events, 9.1 us)
Async XLA Ops:
  7.2 97.7 %reduce-scatter.2.cloned.1.call-start = ((), (), s32[]{:S(2)}) async-start(), calls=%async_computation.1 | async-start | bytes 7077888 | tf_op jit(solution)/shard_map/reduce_scatter | solution.py:295
  13.9 16.7 %collective-permute-start.3 = (bf16[128,896]{1,0:T(8,128)(2,1)}, bf16[128,896]{1,0:T(8,128)(2,1)S(1)}, u32[]{:S(2)}, u32[]{:S(2)}) collective-permute-start(bf16[128,896]{1,0:T(8,128)(2,1)} %get-tuple-element.47), channel_id=1, source_target_pairs={{0,8},{1,25},{2,10},{3,27},{4,12},{5,29},{6,14},{7,31},{8,0},{9,17... | collective-permute-start | bytes 688136 | tf_op jit(solution)/shard_map/ppermute | solution.py:47
  16.0 14.6 %collective-permute-start.4 = (bf16[128,896]{1,0:T(8,128)(2,1)}, bf16[128,896]{1,0:T(8,128)(2,1)S(1)}, u32[]{:S(2)}, u32[]{:S(2)}) collective-permute-start(bf16[128,896]{1,0:T(8,128)(2,1)} %get-tuple-element.48), channel_id=1, source_target_pairs={{0,16},{1,17},{2,18},{3,19},{4,20},{5,21},{6,22},{7,23},{8,24},{9,... | collective-permute-start | bytes 688136 | tf_op jit(solution)/shard_map/ppermute | solution.py:47
  19.6 12.0 %collective-permute-start.5 = (bf16[128,896]{1,0:T(8,128)(2,1)}, bf16[128,896]{1,0:T(8,128)(2,1)S(1)}, u32[]{:S(2)}, u32[]{:S(2)}) collective-permute-start(bf16[128,896]{1,0:T(8,128)(2,1)} %get-tuple-element.49), channel_id=1, source_target_pairs={{0,24},{1,9},{2,26},{3,11},{4,28},{5,13},{6,30},{7,15},{8,16},{9,1... | collective-permute-start | bytes 688136 | tf_op jit(solution)/shard_map/ppermute | solution.py:47
  25.8 11.4 %collective-permute-start = (bf16[128,896]{1,0:T(8,128)(2,1)}, bf16[128,896]{1,0:T(8,128)(2,1)S(1)}, u32[]{:S(2)}, u32[]{:S(2)}) collective-permute-start(bf16[128,896]{1,0:T(8,128)(2,1)} %get-tuple-element.44), channel_id=1, source_target_pairs={{0,8},{1,25},{2,10},{3,27},{4,12},{5,29},{6,14},{7,31},{8,0},{9,17... | collective-permute-start | bytes 688136 | tf_op jit(solution)/shard_map/ppermute | solution.py:47
  25.9 22.7 %collective-permute-start.1 = (bf16[128,896]{1,0:T(8,128)(2,1)}, bf16[128,896]{1,0:T(8,128)(2,1)S(1)}, u32[]{:S(2)}, u32[]{:S(2)}) collective-permute-start(bf16[128,896]{1,0:T(8,128)(2,1)} %get-tuple-element.45), channel_id=1, source_target_pairs={{0,16},{1,17},{2,18},{3,19},{4,20},{5,21},{6,22},{7,23},{8,24},{9,... | collective-permute-start | bytes 688136 | tf_op jit(solution)/shard_map/ppermute | solution.py:47
  30.6 18.0 %collective-permute-start.2 = (bf16[128,896]{1,0:T(8,128)(2,1)}, bf16[128,896]{1,0:T(8,128)(2,1)S(1)}, u32[]{:S(2)}, u32[]{:S(2)}) collective-permute-start(bf16[128,896]{1,0:T(8,128)(2,1)} %get-tuple-element.46), channel_id=1, source_target_pairs={{0,24},{1,9},{2,26},{3,11},{4,28},{5,13},{6,30},{7,15},{8,16},{9,1... | collective-permute-start | bytes 688136 | tf_op jit(solution)/shard_map/ppermute | solution.py:47
  32.6 16.0 %collective-permute-start.6 = (bf16[128,896]{1,0:T(8,128)(2,1)S(1)}, bf16[128,896]{1,0:T(8,128)(2,1)S(1)}, u32[]{:S(2)}, u32[]{:S(2)}) collective-permute-start(bf16[128,896]{1,0:T(8,128)(2,1)S(1)} %get-tuple-element.52), channel_id=1, source_target_pairs={{0,32},{1,97},{2,34},{3,99},{4,36},{5,101},{6,38},{7,103},{8,40},{... | collective-permute-start | bytes 688136 | tf_op jit(solution)/shard_map/ppermute | solution.py:47
  34.3 14.3 %collective-permute-start.7 = (bf16[128,896]{1,0:T(8,128)(2,1)S(1)}, bf16[128,896]{1,0:T(8,128)(2,1)S(1)}, u32[]{:S(2)}, u32[]{:S(2)}) collective-permute-start(bf16[128,896]{1,0:T(8,128)(2,1)S(1)} %get-tuple-element.53), channel_id=1, source_target_pairs={{0,64},{1,65},{2,66},{3,67},{4,68},{5,69},{6,70},{7,71},{8,72},{9,... | collective-permute-start | bytes 688136 | tf_op jit(solution)/shard_map/ppermute | solution.py:47
  37.2 11.4 %collective-permute-start.8 = (bf16[128,896]{1,0:T(8,128)(2,1)S(1)}, bf16[128,896]{1,0:T(8,128)(2,1)S(1)}, u32[]{:S(2)}, u32[]{:S(2)}) collective-permute-start(bf16[128,896]{1,0:T(8,128)(2,1)S(1)} %get-tuple-element.54), channel_id=1, source_target_pairs={{0,96},{1,33},{2,98},{3,35},{4,100},{5,37},{6,102},{7,39},{8,104},... | collective-permute-start | bytes 688136 | tf_op jit(solution)/shard_map/ppermute | solution.py:47
  52.3 15.7 %collective-permute-start.10 = (bf16[128,896]{1,0:T(8,128)(2,1)}, bf16[128,896]{1,0:T(8,128)(2,1)S(1)}, u32[]{:S(2)}, u32[]{:S(2)}) collective-permute-start(bf16[128,896]{1,0:T(8,128)(2,1)} %copy-done.8), channel_id=1, source_target_pairs={{0,64},{1,65},{2,66},{3,67},{4,68},{5,69},{6,70},{7,71},{8,72},{9,... | collective-permute-start | bytes 688136 | tf_op jit(solution)/shard_map/ppermute | solution.py:47
  56.4 11.6 %collective-permute-start.11 = (bf16[128,896]{1,0:T(8,128)(2,1)S(1)}, bf16[128,896]{1,0:T(8,128)(2,1)S(1)}, u32[]{:S(2)}, u32[]{:S(2)}) collective-permute-start(bf16[128,896]{1,0:T(8,128)(2,1)S(1)} %get-tuple-element.58), channel_id=1, source_target_pairs={{0,96},{1,33},{2,98},{3,35},{4,100},{5,37},{6,102},{7,39},{8,104},... | collective-permute-start | bytes 688136 | tf_op jit(solution)/shard_map/ppermute | solution.py:47
  56.8 20.0 %collective-permute-start.20 = (bf16[128,896]{1,0:T(8,128)(2,1)S(1)}, bf16[128,896]{1,0:T(8,128)(2,1)S(1)}, u32[]{:S(2)}, u32[]{:S(2)}) collective-permute-start(bf16[128,896]{1,0:T(8,128)(2,1)S(1)} %get-tuple-element.67.refs_0_), channel_id=1, source_target_pairs={{0,96},{1,33},{2,98},{3,35},{4,100},{5,37},{6,102},{7,39},{8,104},... | collective-permute-start | bytes 688136 | tf_op jit(solution)/shard_map/ppermute | solution.py:47
  59.7 17.1 %collective-permute-start.19 = (bf16[128,896]{1,0:T(8,128)(2,1)S(1)}, bf16[128,896]{1,0:T(8,128)(2,1)S(1)}, u32[]{:S(2)}, u32[]{:S(2)}) collective-permute-start(bf16[128,896]{1,0:T(8,128)(2,1)S(1)} %get-tuple-element.67.refs_0_), channel_id=1, source_target_pairs={{0,64},{1,65},{2,66},{3,67},{4,68},{5,69},{6,70},{7,71},{8,72},{9,... | collective-permute-start | bytes 688136 | tf_op jit(solution)/shard_map/ppermute | solution.py:47
  60.8 16.0 %collective-permute-start.18 = (bf16[128,896]{1,0:T(8,128)(2,1)S(1)}, bf16[128,896]{1,0:T(8,128)(2,1)S(1)}, u32[]{:S(2)}, u32[]{:S(2)}) collective-permute-start(bf16[128,896]{1,0:T(8,128)(2,1)S(1)} %get-tuple-element.67.refs_0_), channel_id=1, source_target_pairs={{0,32},{1,97},{2,34},{3,99},{4,36},{5,101},{6,38},{7,103},{8,40},{... | collective-permute-start | bytes 688136 | tf_op jit(solution)/shard_map/ppermute | solution.py:47
  69.5 16.2 %collective-permute-start.14 = (bf16[128,896]{1,0:T(8,128)(2,1)S(1)}, bf16[128,896]{1,0:T(8,128)(2,1)S(1)}, u32[]{:S(2)}, u32[]{:S(2)}) collective-permute-start(bf16[128,896]{1,0:T(8,128)(2,1)S(1)} %get-tuple-element.62.refs_0_), channel_id=1, source_target_pairs={{0,96},{1,33},{2,98},{3,35},{4,100},{5,37},{6,102},{7,39},{8,104},... | collective-permute-start | bytes 688136 | tf_op jit(solution)/shard_map/ppermute | solution.py:47
  69.9 18.2 %collective-permute-start.13 = (bf16[128,896]{1,0:T(8,128)(2,1)S(1)}, bf16[128,896]{1,0:T(8,128)(2,1)S(1)}, u32[]{:S(2)}, u32[]{:S(2)}) collective-permute-start(bf16[128,896]{1,0:T(8,128)(2,1)S(1)} %get-tuple-element.62.refs_0_), channel_id=1, source_target_pairs={{0,64},{1,65},{2,66},{3,67},{4,68},{5,69},{6,70},{7,71},{8,72},{9,... | collective-permute-start | bytes 688136 | tf_op jit(solution)/shard_map/ppermute | solution.py:47
  76.8 11.3 %collective-permute-start.12 = (bf16[128,896]{1,0:T(8,128)(2,1)S(1)}, bf16[128,896]{1,0:T(8,128)(2,1)S(1)}, u32[]{:S(2)}, u32[]{:S(2)}) collective-permute-start(bf16[128,896]{1,0:T(8,128)(2,1)S(1)} %get-tuple-element.62.refs_0_), channel_id=1, source_target_pairs={{0,32},{1,97},{2,34},{3,99},{4,36},{5,101},{6,38},{7,103},{8,40},{... | collective-permute-start | bytes 688136 | tf_op jit(solution)/shard_map/ppermute | solution.py:47
  77.5 13.7 %collective-permute-start.21 = (bf16[128,896]{1,0:T(8,128)(2,1)S(1)}, bf16[128,896]{1,0:T(8,128)(2,1)S(1)}, u32[]{:S(2)}, u32[]{:S(2)}) collective-permute-start(bf16[128,896]{1,0:T(8,128)(2,1)S(1)} %get-tuple-element.69), channel_id=1, source_target_pairs={{0,8},{1,25},{2,10},{3,27},{4,12},{5,29},{6,14},{7,31},{8,0},{9,17... | collective-permute-start | bytes 688136 | tf_op jit(solution)/shard_map/ppermute | solution.py:47
  77.6 15.9 %collective-permute-start.22 = (bf16[128,896]{1,0:T(8,128)(2,1)S(1)}, bf16[128,896]{1,0:T(8,128)(2,1)S(1)}, u32[]{:S(2)}, u32[]{:S(2)}) collective-permute-start(bf16[128,896]{1,0:T(8,128)(2,1)S(1)} %get-tuple-element.70), channel_id=1, source_target_pairs={{0,16},{1,17},{2,18},{3,19},{4,20},{5,21},{6,22},{7,23},{8,24},{9,... | collective-permute-start | bytes 688136 | tf_op jit(solution)/shard_map/ppermute | solution.py:47
  85.7 14.5 %collective-permute-start.23 = (bf16[128,896]{1,0:T(8,128)(2,1)S(1)}, bf16[128,896]{1,0:T(8,128)(2,1)S(1)}, u32[]{:S(2)}, u32[]{:S(2)}) collective-permute-start(bf16[128,896]{1,0:T(8,128)(2,1)S(1)} %get-tuple-element.71), channel_id=1, source_target_pairs={{0,24},{1,9},{2,26},{3,11},{4,28},{5,13},{6,30},{7,15},{8,16},{9,1... | collective-permute-start | bytes 688136 | tf_op jit(solution)/shard_map/ppermute | solution.py:47
  88.8 13.0 %collective-permute-start.15 = (bf16[128,896]{1,0:T(8,128)(2,1)S(1)}, bf16[128,896]{1,0:T(8,128)(2,1)S(1)}, u32[]{:S(2)}, u32[]{:S(2)}) collective-permute-start(bf16[128,896]{1,0:T(8,128)(2,1)S(1)} %get-tuple-element.64), channel_id=1, source_target_pairs={{0,8},{1,25},{2,10},{3,27},{4,12},{5,29},{6,14},{7,31},{8,0},{9,17... | collective-permute-start | bytes 688136 | tf_op jit(solution)/shard_map/ppermute | solution.py:47
  88.9 13.7 %collective-permute-start.16 = (bf16[128,896]{1,0:T(8,128)(2,1)S(1)}, bf16[128,896]{1,0:T(8,128)(2,1)S(1)}, u32[]{:S(2)}, u32[]{:S(2)}) collective-permute-start(bf16[128,896]{1,0:T(8,128)(2,1)S(1)} %get-tuple-element.65), channel_id=1, source_target_pairs={{0,16},{1,17},{2,18},{3,19},{4,20},{5,21},{6,22},{7,23},{8,24},{9,... | collective-permute-start | bytes 688136 | tf_op jit(solution)/shard_map/ppermute | solution.py:47
  91.2 12.6 %collective-permute-start.17 = (bf16[128,896]{1,0:T(8,128)(2,1)S(1)}, bf16[128,896]{1,0:T(8,128)(2,1)S(1)}, u32[]{:S(2)}, u32[]{:S(2)}) collective-permute-start(bf16[128,896]{1,0:T(8,128)(2,1)S(1)} %get-tuple-element.66), channel_id=1, source_target_pairs={{0,24},{1,9},{2,26},{3,11},{4,28},{5,13},{6,30},{7,15},{8,16},{9,1... | collective-permute-start | bytes 688136 | tf_op jit(solution)/shard_map/ppermute | solution.py:47
  (11 other events, 115.3 us)
Sparse Core Ops, SparseCore 0:
  52.1 42.9 reduce-scatter.1

commit v4 on v3

--- a/solution.py
+++ b/solution.py
@@ -287,7 +287,7 @@
     along_z = [exchange(move_z, first), exchange(move_z, second)]
     sums = by_expert(replica_map, along_z[0])
     early = exchange(move_y, sums)
-    terms, turn = act_terms(counts, grads, weight, scale, (sums[0], second[0]))
+    terms, turn = act_terms(counts, grads, weight, scale, (sums[0], along_z[1][1]))
     sums = by_expert(replica_map, along_z[1], (turn,), early[1:])
     late = exchange(move_y, sums)
     *state, rows, turn = adam(0, early, (master, moment1, moment2), (), 1, sums[:1])

time: 112 us -> 111 us (level)
  transfers between devices with their start and end apart: 25 -> 25, of which waited for: 8 -> 8; matrix products, arithmetic and copies ran while one was open for 0% -> 0% of each run, Pallas kernels for 20% -> 21%
where the time goes in v4:
time: 111 us
  starting transfers between devices  36.5 us (33%)
  Pallas kernels  32.2 us (29%)
  waiting for transfers between devices  27.1 us (24%)
  between operations  14.9 us (13%)
    ppermute x24, starting transfers between devices, move(): return lax.ppermute(value, ('slot', 'shard'), pairs)  36.5 us
    ppermute x24, waiting for transfers between devices, move(): return lax.ppermute(value, ('slot', 'shard'), pairs)  27.1 us
    pallas_call x2, Pallas kernels, slot_grads(): pl.pallas_call(kernel, in_specs=[SMEM, HBM, HBM] + [ANY] * len(after), ou...  12.3 us
    pallas_call x1, Pallas kernels, act_terms(): pl.pallas_call(kernel, grid_spec=pltpu.PrefetchScalarGridSpec(num_scalar_...  10.1 us
    pallas_call x2, Pallas kernels, adam(): pl.pallas_call(kernel, grid=(1,), in_specs=[pl.BlockSpec((part, width), l...  3.01 us
    pallas_call x2, Pallas kernels, by_expert(): pl.pallas_call(kernel, in_specs=[SMEM] + [VMEM] * RING + [SMEM] * len(aft...  2.79 us
    pallas_call x2, Pallas kernels, put_rows(): pl.pallas_call(kernel, in_specs=[VMEM] * RING + [ANY] * len(earlier) + [S...  2.52 us
  transfers between devices with their start and end apart: 25, of which 8 were waited for; matrix products, arithmetic and copies ran while one was open for 0% of the time, Pallas kernels for 21%

profile of v4, /device:TPU:0, one launch (start us, length us, event | category | flops | bytes accessed | tf_op | source)
XLA Modules:
  0.0 110.8 jit_solution(11388075693880216857)
XLA Ops:
  7.9 6.1 %slot_grads.2 = (bf16[128,896]{1,0:T(8,128)(2,1)}, bf16[128,896]{1,0:T(8,128)(2,1)}, bf16[128,896]{1,0:T(8,128)(2,1)}, bf16[128,896]{1,0:T(8,128)(2,1)}) custom-call(s32[1]{0:T(128)S(6)} %copy.22.count_ref, bf16[3072,1024]{1,0:T(8,128)(2,1)} %bitcast.6, bf16[3072,896]{1,0:T(8,128)(2,1)} %bitcast.8), custom_call_target="tpu_custom_call" | custom-call | flops 10000000000 | bytes 14000000 | tf_op jit(solution)/shard_map/slot_grads/pallas_call | solution.py:106
  13.9 2.1 %collective-permute-start.3 = (bf16[128,896]{1,0:T(8,128)(2,1)}, bf16[128,896]{1,0:T(8,128)(2,1)S(1)}, u32[]{:S(2)}, u32[]{:S(2)}) collective-permute-start(bf16[128,896]{1,0:T(8,128)(2,1)} %get-tuple-element.47), channel_id=1, source_target_pairs={{0,8},{1,25},{2,10},{3,27},{4,12},{5,29},{6,14},{7,31},{8,0},{9,17... | collective-permute-start | bytes 688136 | tf_op jit(solution)/shard_map/ppermute | solution.py:47
  16.0 3.6 %collective-permute-start.4 = (bf16[128,896]{1,0:T(8,128)(2,1)}, bf16[128,896]{1,0:T(8,128)(2,1)S(1)}, u32[]{:S(2)}, u32[]{:S(2)}) collective-permute-start(bf16[128,896]{1,0:T(8,128)(2,1)} %get-tuple-element.48), channel_id=1, source_target_pairs={{0,16},{1,17},{2,18},{3,19},{4,20},{5,21},{6,22},{7,23},{8,24},{9,... | collective-permute-start | bytes 688136 | tf_op jit(solution)/shard_map/ppermute | solution.py:47
  19.6 6.2 %slot_grads.3 = (bf16[128,896]{1,0:T(8,128)(2,1)}, bf16[128,896]{1,0:T(8,128)(2,1)}, bf16[128,896]{1,0:T(8,128)(2,1)}, bf16[128,896]{1,0:T(8,128)(2,1)}) custom-call(s32[1]{0:T(128)S(6)} %copy.22.count_ref, bf16[3072,1024]{1,0:T(8,128)(2,1)} %bitcast.7, bf16[3072,896]{1,0:T(8,128)(2,1)} %bitcast.9, bf16[128,896]{1,0:T(8,128)(2,1)} %get-tuple-element.42.rest_0_.refs_0_), custom_call_target="tpu_custom_call" | custom-call | flops 10000000000 | bytes 14000000 | tf_op jit(solution)/shard_map/slot_grads/pallas_call | solution.py:106
  25.9 4.7 %collective-permute-start.1 = (bf16[128,896]{1,0:T(8,128)(2,1)}, bf16[128,896]{1,0:T(8,128)(2,1)S(1)}, u32[]{:S(2)}, u32[]{:S(2)}) collective-permute-start(bf16[128,896]{1,0:T(8,128)(2,1)} %get-tuple-element.45), channel_id=1, source_target_pairs={{0,16},{1,17},{2,18},{3,19},{4,20},{5,21},{6,22},{7,23},{8,24},{9,... | collective-permute-start | bytes 688136 | tf_op jit(solution)/shard_map/ppermute | solution.py:47
  32.6 1.7 %collective-permute-start.6 = (bf16[128,896]{1,0:T(8,128)(2,1)S(1)}, bf16[128,896]{1,0:T(8,128)(2,1)S(1)}, u32[]{:S(2)}, u32[]{:S(2)}) collective-permute-start(bf16[128,896]{1,0:T(8,128)(2,1)S(1)} %get-tuple-element.52), channel_id=1, source_target_pairs={{0,32},{1,97},{2,34},{3,99},{4,36},{5,101},{6,38},{7,103},{8,40},{... | collective-permute-start | bytes 688136 | tf_op jit(solution)/shard_map/ppermute | solution.py:47
  34.3 2.9 %collective-permute-start.7 = (bf16[128,896]{1,0:T(8,128)(2,1)S(1)}, bf16[128,896]{1,0:T(8,128)(2,1)S(1)}, u32[]{:S(2)}, u32[]{:S(2)}) collective-permute-start(bf16[128,896]{1,0:T(8,128)(2,1)S(1)} %get-tuple-element.53), channel_id=1, source_target_pairs={{0,64},{1,65},{2,66},{3,67},{4,68},{5,69},{6,70},{7,71},{8,72},{9,... | collective-permute-start | bytes 688136 | tf_op jit(solution)/shard_map/ppermute | solution.py:47
  37.6 10.1 %act_terms.1 = (bf16[8,3072,128]{2,1,0:T(8,128)(2,1)}, s32[1]{0:T(128)}) custom-call(s32[1]{0:T(128)S(6)} %copy.22.count_ref, bf16[3072,896]{1,0:T(8,128)(2,1)} %bitcast.10, bf16[1024,896]{1,0:T(8,128)(2,1)S(1)} %bitcast.4, bf16[128,896]{1,0:T(8,128)(2,1)S(1)} %get-tuple-element.50.rest_0_.refs_0_, bf16[128,896]{1,0:T(8,128)(2,1)S(1)} %collective-permute-done.rest_1_.refs_1_), custom_call_target="tpu_custom_call" | custom-call | flops 10000000000 | bytes 14000000 | tf_op jit(solution)/shard_map/act_terms/pallas_call | solution.py:140
  47.7 1.7 %by_expert.3 = (bf16[128,896]{1,0:T(8,128)(2,1)S(1)}, bf16[128,896]{1,0:T(8,128)(2,1)S(1)}, bf16[128,896]{1,0:T(8,128)(2,1)S(1)}, bf16[128,896]{1,0:T(8,128)(2,1)S(1)}) custom-call(s32[16]{0:T(128)S(1)} %copy-done.5, bf16[128,896]{1,0:T(8,128)(2,1)S(1)} %copy-done.4, bf16[128,896]{1,0:T(8,128)(2,1)S(1)} %collective-permute-done.rest_1_.refs_1_, ...), custom_call_target="tpu_custom_call" | custom-call | bytes 1024 | tf_op jit(solution)/shard_map/by_expert/pallas_call | solution.py:174
  49.5 1.5 %adam.2 = (f32[256,896]{1,0:T(8,128)}, f32[256,896]{1,0:T(8,128)}, f32[256,896]{1,0:T(8,128)}, bf16[128,896]{1,0:T(8,128)(2,1)S(1)}, s32[1]{0:T(128)}) custom-call(bf16[128,896]{1,0:T(8,128)(2,1)S(1)} %get-tuple-element.50.rest_0_.refs_0_, bf16[128,896]{1,0:T(8,128)(2,1)S(1)} %collective-permute-done.6.refs_5_.refs_1_, ...), custom_call_target="tpu_custom_call" | custom-call | bytes 1024 | tf_op jit(solution)/shard_map/adam/pallas_call | solution.py:214
  51.4 4.1 %collective-permute-start.10 = (bf16[128,896]{1,0:T(8,128)(2,1)}, bf16[128,896]{1,0:T(8,128)(2,1)S(1)}, u32[]{:S(2)}, u32[]{:S(2)}) collective-permute-start(bf16[128,896]{1,0:T(8,128)(2,1)} %copy-done.8), channel_id=1, source_target_pairs={{0,64},{1,65},{2,66},{3,67},{4,68},{5,69},{6,70},{7,71},{8,72},{9,... | collective-permute-start | bytes 688136 | tf_op jit(solution)/shard_map/ppermute | solution.py:47
  55.9 2.9 %collective-permute-start.20 = (bf16[128,896]{1,0:T(8,128)(2,1)S(1)}, bf16[128,896]{1,0:T(8,128)(2,1)S(1)}, u32[]{:S(2)}, u32[]{:S(2)}) collective-permute-start(bf16[128,896]{1,0:T(8,128)(2,1)S(1)} %get-tuple-element.67.refs_0_), channel_id=1, source_target_pairs={{0,96},{1,33},{2,98},{3,35},{4,100},{5,37},{6,102},{7,39},{8,104},... | collective-permute-start | bytes 688136 | tf_op jit(solution)/shard_map/ppermute | solution.py:47
  60.0 7.1 %collective-permute-done.10.refs_2_ = bf16[128,896]{1,0:T(8,128)(2,1)S(1)} collective-permute-done((bf16[128,896]{1,0:T(8,128)(2,1)}, bf16[128,896]{1,0:T(8,128)(2,1)S(1)}, u32[]{:S(2)}, u32[]{:S(2)}) %collective-permute-start.10) | collective-permute-done | bytes 229408 | tf_op jit(solution)/shard_map/ppermute | solution.py:47
  67.1 1.5 %adam.3 = (f32[256,896]{1,0:T(8,128)}, f32[256,896]{1,0:T(8,128)}, f32[256,896]{1,0:T(8,128)}, bf16[128,896]{1,0:T(8,128)(2,1)S(1)}) custom-call(bf16[128,896]{1,0:T(8,128)(2,1)S(1)} %get-tuple-element.55.refs_7_.refs_0_, bf16[128,896]{1,0:T(8,128)(2,1)S(1)} %collective-permute-done.9.refs_1_, ...), custom_call_target="tpu_custom_call", output_to_operand_aliasing={{0}: (7, {}), {1}: (8, {}), {2}: (9, {})} | custom-call | bytes 1024 | tf_op jit(solution)/shard_map/adam/pallas_call | solution.py:214
  69.0 2.0 %collective-permute-start.13 = (bf16[128,896]{1,0:T(8,128)(2,1)S(1)}, bf16[128,896]{1,0:T(8,128)(2,1)S(1)}, u32[]{:S(2)}, u32[]{:S(2)}) collective-permute-start(bf16[128,896]{1,0:T(8,128)(2,1)S(1)} %get-tuple-element.62.refs_0_), channel_id=1, source_target_pairs={{0,64},{1,65},{2,66},{3,67},{4,68},{5,69},{6,70},{7,71},{8,72},{9,... | collective-permute-start | bytes 688136 | tf_op jit(solution)/shard_map/ppermute | solution.py:47
  71.0 4.9 %collective-permute-done.20.refs_3_ = bf16[128,896]{1,0:T(8,128)(2,1)S(1)} collective-permute-done((bf16[128,896]{1,0:T(8,128)(2,1)S(1)}, bf16[128,896]{1,0:T(8,128)(2,1)S(1)}, u32[]{:S(2)}, u32[]{:S(2)}) %collective-permute-start.20) | collective-permute-done | bytes 229408 | tf_op jit(solution)/shard_map/ppermute | solution.py:47
  76.7 3.8 %collective-permute-start.22 = (bf16[128,896]{1,0:T(8,128)(2,1)S(1)}, bf16[128,896]{1,0:T(8,128)(2,1)S(1)}, u32[]{:S(2)}, u32[]{:S(2)}) collective-permute-start(bf16[128,896]{1,0:T(8,128)(2,1)S(1)} %get-tuple-element.70), channel_id=1, source_target_pairs={{0,16},{1,17},{2,18},{3,19},{4,20},{5,21},{6,22},{7,23},{8,24},{9,... | collective-permute-start | bytes 688136 | tf_op jit(solution)/shard_map/ppermute | solution.py:47
  80.5 4.3 %collective-permute-done.14.refs_3_ = bf16[128,896]{1,0:T(8,128)(2,1)S(1)} collective-permute-done((bf16[128,896]{1,0:T(8,128)(2,1)S(1)}, bf16[128,896]{1,0:T(8,128)(2,1)S(1)}, u32[]{:S(2)}, u32[]{:S(2)}) %collective-permute-start.14) | collective-permute-done | bytes 229408 | tf_op jit(solution)/shard_map/ppermute | solution.py:47
  84.8 2.3 %collective-permute-start.23 = (bf16[128,896]{1,0:T(8,128)(2,1)S(1)}, bf16[128,896]{1,0:T(8,128)(2,1)S(1)}, u32[]{:S(2)}, u32[]{:S(2)}) collective-permute-start(bf16[128,896]{1,0:T(8,128)(2,1)S(1)} %get-tuple-element.71), channel_id=1, source_target_pairs={{0,24},{1,9},{2,26},{3,11},{4,28},{5,13},{6,30},{7,15},{8,16},{9,1... | collective-permute-start | bytes 688136 | tf_op jit(solution)/shard_map/ppermute | solution.py:47
  88.0 2.3 %collective-permute-start.16 = (bf16[128,896]{1,0:T(8,128)(2,1)S(1)}, bf16[128,896]{1,0:T(8,128)(2,1)S(1)}, u32[]{:S(2)}, u32[]{:S(2)}) collective-permute-start(bf16[128,896]{1,0:T(8,128)(2,1)S(1)} %get-tuple-element.65), channel_id=1, source_target_pairs={{0,16},{1,17},{2,18},{3,19},{4,20},{5,21},{6,22},{7,23},{8,24},{9,... | collective-permute-start | bytes 688136 | tf_op jit(solution)/shard_map/ppermute | solution.py:47
  90.3 2.3 %collective-permute-start.17 = (bf16[128,896]{1,0:T(8,128)(2,1)S(1)}, bf16[128,896]{1,0:T(8,128)(2,1)S(1)}, u32[]{:S(2)}, u32[]{:S(2)}) collective-permute-start(bf16[128,896]{1,0:T(8,128)(2,1)S(1)} %get-tuple-element.66), channel_id=1, source_target_pairs={{0,24},{1,9},{2,26},{3,11},{4,28},{5,13},{6,30},{7,15},{8,16},{9,1... | collective-permute-start | bytes 688136 | tf_op jit(solution)/shard_map/ppermute | solution.py:47
  92.7 6.6 %collective-permute-done.23.refs_3_ = bf16[128,896]{1,0:T(8,128)(2,1)S(1)} collective-permute-done((bf16[128,896]{1,0:T(8,128)(2,1)S(1)}, bf16[128,896]{1,0:T(8,128)(2,1)S(1)}, u32[]{:S(2)}, u32[]{:S(2)}) %collective-permute-start.23) | collective-permute-done | bytes 229408 | tf_op jit(solution)/shard_map/ppermute | solution.py:47
  99.3 1.6 %put_rows.2.refs_4_ = bf16[1024,896]{1,0:T(8,128)(2,1)} custom-call(bf16[128,896]{1,0:T(8,128)(2,1)S(1)} %get-tuple-element.68.refs_0_, bf16[128,896]{1,0:T(8,128)(2,1)S(1)} %collective-permute-done.21.refs_1_, bf16[128,896]{1,0:T(8,128)(2,1)S(1)} %collective-permute-done.22.refs_2_, bf16[128,896]{1,0:T(8,128)(2,1)S(1)} %collective-permute-done.23.refs_3_, ...), custom_call_target="tpu_custom_call" | custom-call | bytes 1024 | tf_op jit(solution)/shard_map/put_rows/pallas_call | solution.py:267
  101.6 1.3 %collective-permute-done.17.refs_3_ = bf16[128,896]{1,0:T(8,128)(2,1)S(1)} collective-permute-done((bf16[128,896]{1,0:T(8,128)(2,1)S(1)}, bf16[128,896]{1,0:T(8,128)(2,1)S(1)}, u32[]{:S(2)}, u32[]{:S(2)}) %collective-permute-start.17) | collective-permute-done | bytes 229408 | tf_op jit(solution)/shard_map/ppermute | solution.py:47
  (58 shorter events, 8.2 us)
Async XLA Ops:
  7.2 96.8 %reduce-scatter.2.cloned.1.call-start = ((), (), s32[]{:S(2)}) async-start(), calls=%async_computation.1 | async-start | bytes 7077888 | tf_op jit(solution)/shard_map/reduce_scatter | solution.py:295
  13.9 16.7 %collective-permute-start.3 = (bf16[128,896]{1,0:T(8,128)(2,1)}, bf16[128,896]{1,0:T(8,128)(2,1)S(1)}, u32[]{:S(2)}, u32[]{:S(2)}) collective-permute-start(bf16[128,896]{1,0:T(8,128)(2,1)} %get-tuple-element.47), channel_id=1, source_target_pairs={{0,8},{1,25},{2,10},{3,27},{4,12},{5,29},{6,14},{7,31},{8,0},{9,17... | collective-permute-start | bytes 688136 | tf_op jit(solution)/shard_map/ppermute | solution.py:47
  16.0 14.6 %collective-permute-start.4 = (bf16[128,896]{1,0:T(8,128)(2,1)}, bf16[128,896]{1,0:T(8,128)(2,1)S(1)}, u32[]{:S(2)}, u32[]{:S(2)}) collective-permute-start(bf16[128,896]{1,0:T(8,128)(2,1)} %get-tuple-element.48), channel_id=1, source_target_pairs={{0,16},{1,17},{2,18},{3,19},{4,20},{5,21},{6,22},{7,23},{8,24},{9,... | collective-permute-start | bytes 688136 | tf_op jit(solution)/shard_map/ppermute | solution.py:47
  19.6 12.0 %collective-permute-start.5 = (bf16[128,896]{1,0:T(8,128)(2,1)}, bf16[128,896]{1,0:T(8,128)(2,1)S(1)}, u32[]{:S(2)}, u32[]{:S(2)}) collective-permute-start(bf16[128,896]{1,0:T(8,128)(2,1)} %get-tuple-element.49), channel_id=1, source_target_pairs={{0,24},{1,9},{2,26},{3,11},{4,28},{5,13},{6,30},{7,15},{8,16},{9,1... | collective-permute-start | bytes 688136 | tf_op jit(solution)/shard_map/ppermute | solution.py:47
  25.8 11.4 %collective-permute-start = (bf16[128,896]{1,0:T(8,128)(2,1)}, bf16[128,896]{1,0:T(8,128)(2,1)S(1)}, u32[]{:S(2)}, u32[]{:S(2)}) collective-permute-start(bf16[128,896]{1,0:T(8,128)(2,1)} %get-tuple-element.44), channel_id=1, source_target_pairs={{0,8},{1,25},{2,10},{3,27},{4,12},{5,29},{6,14},{7,31},{8,0},{9,17... | collective-permute-start | bytes 688136 | tf_op jit(solution)/shard_map/ppermute | solution.py:47
  25.9 21.8 %collective-permute-start.1 = (bf16[128,896]{1,0:T(8,128)(2,1)}, bf16[128,896]{1,0:T(8,128)(2,1)S(1)}, u32[]{:S(2)}, u32[]{:S(2)}) collective-permute-start(bf16[128,896]{1,0:T(8,128)(2,1)} %get-tuple-element.45), channel_id=1, source_target_pairs={{0,16},{1,17},{2,18},{3,19},{4,20},{5,21},{6,22},{7,23},{8,24},{9,... | collective-permute-start | bytes 688136 | tf_op jit(solution)/shard_map/ppermute | solution.py:47
  30.6 17.1 %collective-permute-start.2 = (bf16[128,896]{1,0:T(8,128)(2,1)}, bf16[128,896]{1,0:T(8,128)(2,1)S(1)}, u32[]{:S(2)}, u32[]{:S(2)}) collective-permute-start(bf16[128,896]{1,0:T(8,128)(2,1)} %get-tuple-element.46), channel_id=1, source_target_pairs={{0,24},{1,9},{2,26},{3,11},{4,28},{5,13},{6,30},{7,15},{8,16},{9,1... | collective-permute-start | bytes 688136 | tf_op jit(solution)/shard_map/ppermute | solution.py:47
  32.6 15.1 %collective-permute-start.6 = (bf16[128,896]{1,0:T(8,128)(2,1)S(1)}, bf16[128,896]{1,0:T(8,128)(2,1)S(1)}, u32[]{:S(2)}, u32[]{:S(2)}) collective-permute-start(bf16[128,896]{1,0:T(8,128)(2,1)S(1)} %get-tuple-element.52), channel_id=1, source_target_pairs={{0,32},{1,97},{2,34},{3,99},{4,36},{5,101},{6,38},{7,103},{8,40},{... | collective-permute-start | bytes 688136 | tf_op jit(solution)/shard_map/ppermute | solution.py:47
  34.3 13.4 %collective-permute-start.7 = (bf16[128,896]{1,0:T(8,128)(2,1)S(1)}, bf16[128,896]{1,0:T(8,128)(2,1)S(1)}, u32[]{:S(2)}, u32[]{:S(2)}) collective-permute-start(bf16[128,896]{1,0:T(8,128)(2,1)S(1)} %get-tuple-element.53), channel_id=1, source_target_pairs={{0,64},{1,65},{2,66},{3,67},{4,68},{5,69},{6,70},{7,71},{8,72},{9,... | collective-permute-start | bytes 688136 | tf_op jit(solution)/shard_map/ppermute | solution.py:47
  37.2 10.5 %collective-permute-start.8 = (bf16[128,896]{1,0:T(8,128)(2,1)S(1)}, bf16[128,896]{1,0:T(8,128)(2,1)S(1)}, u32[]{:S(2)}, u32[]{:S(2)}) collective-permute-start(bf16[128,896]{1,0:T(8,128)(2,1)S(1)} %get-tuple-element.54), channel_id=1, source_target_pairs={{0,96},{1,33},{2,98},{3,35},{4,100},{5,37},{6,102},{7,39},{8,104},... | collective-permute-start | bytes 688136 | tf_op jit(solution)/shard_map/ppermute | solution.py:47
  51.4 15.7 %collective-permute-start.10 = (bf16[128,896]{1,0:T(8,128)(2,1)}, bf16[128,896]{1,0:T(8,128)(2,1)S(1)}, u32[]{:S(2)}, u32[]{:S(2)}) collective-permute-start(bf16[128,896]{1,0:T(8,128)(2,1)} %copy-done.8), channel_id=1, source_target_pairs={{0,64},{1,65},{2,66},{3,67},{4,68},{5,69},{6,70},{7,71},{8,72},{9,... | collective-permute-start | bytes 688136 | tf_op jit(solution)/shard_map/ppermute | solution.py:47
  55.5 11.6 %collective-permute-start.11 = (bf16[128,896]{1,0:T(8,128)(2,1)S(1)}, bf16[128,896]{1,0:T(8,128)(2,1)S(1)}, u32[]{:S(2)}, u32[]{:S(2)}) collective-permute-start(bf16[128,896]{1,0:T(8,128)(2,1)S(1)} %get-tuple-element.58), channel_id=1, source_target_pairs={{0,96},{1,33},{2,98},{3,35},{4,100},{5,37},{6,102},{7,39},{8,104},... | collective-permute-start | bytes 688136 | tf_op jit(solution)/shard_map/ppermute | solution.py:47
  55.9 20.0 %collective-permute-start.20 = (bf16[128,896]{1,0:T(8,128)(2,1)S(1)}, bf16[128,896]{1,0:T(8,128)(2,1)S(1)}, u32[]{:S(2)}, u32[]{:S(2)}) collective-permute-start(bf16[128,896]{1,0:T(8,128)(2,1)S(1)} %get-tuple-element.67.refs_0_), channel_id=1, source_target_pairs={{0,96},{1,33},{2,98},{3,35},{4,100},{5,37},{6,102},{7,39},{8,104},... | collective-permute-start | bytes 688136 | tf_op jit(solution)/shard_map/ppermute | solution.py:47
  58.8 17.1 %collective-permute-start.19 = (bf16[128,896]{1,0:T(8,128)(2,1)S(1)}, bf16[128,896]{1,0:T(8,128)(2,1)S(1)}, u32[]{:S(2)}, u32[]{:S(2)}) collective-permute-start(bf16[128,896]{1,0:T(8,128)(2,1)S(1)} %get-tuple-element.67.refs_0_), channel_id=1, source_target_pairs={{0,64},{1,65},{2,66},{3,67},{4,68},{5,69},{6,70},{7,71},{8,72},{9,... | collective-permute-start | bytes 688136 | tf_op jit(solution)/shard_map/ppermute | solution.py:47
  59.9 16.0 %collective-permute-start.18 = (bf16[128,896]{1,0:T(8,128)(2,1)S(1)}, bf16[128,896]{1,0:T(8,128)(2,1)S(1)}, u32[]{:S(2)}, u32[]{:S(2)}) collective-permute-start(bf16[128,896]{1,0:T(8,128)(2,1)S(1)} %get-tuple-element.67.refs_0_), channel_id=1, source_target_pairs={{0,32},{1,97},{2,34},{3,99},{4,36},{5,101},{6,38},{7,103},{8,40},{... | collective-permute-start | bytes 688136 | tf_op jit(solution)/shard_map/ppermute | solution.py:47
  68.6 16.2 %collective-permute-start.14 = (bf16[128,896]{1,0:T(8,128)(2,1)S(1)}, bf16[128,896]{1,0:T(8,128)(2,1)S(1)}, u32[]{:S(2)}, u32[]{:S(2)}) collective-permute-start(bf16[128,896]{1,0:T(8,128)(2,1)S(1)} %get-tuple-element.62.refs_0_), channel_id=1, source_target_pairs={{0,96},{1,33},{2,98},{3,35},{4,100},{5,37},{6,102},{7,39},{8,104},... | collective-permute-start | bytes 688136 | tf_op jit(solution)/shard_map/ppermute | solution.py:47
  69.0 18.2 %collective-permute-start.13 = (bf16[128,896]{1,0:T(8,128)(2,1)S(1)}, bf16[128,896]{1,0:T(8,128)(2,1)S(1)}, u32[]{:S(2)}, u32[]{:S(2)}) collective-permute-start(bf16[128,896]{1,0:T(8,128)(2,1)S(1)} %get-tuple-element.62.refs_0_), channel_id=1, source_target_pairs={{0,64},{1,65},{2,66},{3,67},{4,68},{5,69},{6,70},{7,71},{8,72},{9,... | collective-permute-start | bytes 688136 | tf_op jit(solution)/shard_map/ppermute | solution.py:47
  75.9 11.3 %collective-permute-start.12 = (bf16[128,896]{1,0:T(8,128)(2,1)S(1)}, bf16[128,896]{1,0:T(8,128)(2,1)S(1)}, u32[]{:S(2)}, u32[]{:S(2)}) collective-permute-start(bf16[128,896]{1,0:T(8,128)(2,1)S(1)} %get-tuple-element.62.refs_0_), channel_id=1, source_target_pairs={{0,32},{1,97},{2,34},{3,99},{4,36},{5,101},{6,38},{7,103},{8,40},{... | collective-permute-start | bytes 688136 | tf_op jit(solution)/shard_map/ppermute | solution.py:47
  76.6 13.7 %collective-permute-start.21 = (bf16[128,896]{1,0:T(8,128)(2,1)S(1)}, bf16[128,896]{1,0:T(8,128)(2,1)S(1)}, u32[]{:S(2)}, u32[]{:S(2)}) collective-permute-start(bf16[128,896]{1,0:T(8,128)(2,1)S(1)} %get-tuple-element.69), channel_id=1, source_target_pairs={{0,8},{1,25},{2,10},{3,27},{4,12},{5,29},{6,14},{7,31},{8,0},{9,17... | collective-permute-start | bytes 688136 | tf_op jit(solution)/shard_map/ppermute | solution.py:47
  76.7 15.9 %collective-permute-start.22 = (bf16[128,896]{1,0:T(8,128)(2,1)S(1)}, bf16[128,896]{1,0:T(8,128)(2,1)S(1)}, u32[]{:S(2)}, u32[]{:S(2)}) collective-permute-start(bf16[128,896]{1,0:T(8,128)(2,1)S(1)} %get-tuple-element.70), channel_id=1, source_target_pairs={{0,16},{1,17},{2,18},{3,19},{4,20},{5,21},{6,22},{7,23},{8,24},{9,... | collective-permute-start | bytes 688136 | tf_op jit(solution)/shard_map/ppermute | solution.py:47
  84.8 14.5 %collective-permute-start.23 = (bf16[128,896]{1,0:T(8,128)(2,1)S(1)}, bf16[128,896]{1,0:T(8,128)(2,1)S(1)}, u32[]{:S(2)}, u32[]{:S(2)}) collective-permute-start(bf16[128,896]{1,0:T(8,128)(2,1)S(1)} %get-tuple-element.71), channel_id=1, source_target_pairs={{0,24},{1,9},{2,26},{3,11},{4,28},{5,13},{6,30},{7,15},{8,16},{9,1... | collective-permute-start | bytes 688136 | tf_op jit(solution)/shard_map/ppermute | solution.py:47
  87.9 13.0 %collective-permute-start.15 = (bf16[128,896]{1,0:T(8,128)(2,1)S(1)}, bf16[128,896]{1,0:T(8,128)(2,1)S(1)}, u32[]{:S(2)}, u32[]{:S(2)}) collective-permute-start(bf16[128,896]{1,0:T(8,128)(2,1)S(1)} %get-tuple-element.64), channel_id=1, source_target_pairs={{0,8},{1,25},{2,10},{3,27},{4,12},{5,29},{6,14},{7,31},{8,0},{9,17... | collective-permute-start | bytes 688136 | tf_op jit(solution)/shard_map/ppermute | solution.py:47
  88.0 13.7 %collective-permute-start.16 = (bf16[128,896]{1,0:T(8,128)(2,1)S(1)}, bf16[128,896]{1,0:T(8,128)(2,1)S(1)}, u32[]{:S(2)}, u32[]{:S(2)}) collective-permute-start(bf16[128,896]{1,0:T(8,128)(2,1)S(1)} %get-tuple-element.65), channel_id=1, source_target_pairs={{0,16},{1,17},{2,18},{3,19},{4,20},{5,21},{6,22},{7,23},{8,24},{9,... | collective-permute-start | bytes 688136 | tf_op jit(solution)/shard_map/ppermute | solution.py:47
  90.3 12.6 %collective-permute-start.17 = (bf16[128,896]{1,0:T(8,128)(2,1)S(1)}, bf16[128,896]{1,0:T(8,128)(2,1)S(1)}, u32[]{:S(2)}, u32[]{:S(2)}) collective-permute-start(bf16[128,896]{1,0:T(8,128)(2,1)S(1)} %get-tuple-element.66), channel_id=1, source_target_pairs={{0,24},{1,9},{2,26},{3,11},{4,28},{5,13},{6,30},{7,15},{8,16},{9,1... | collective-permute-start | bytes 688136 | tf_op jit(solution)/shard_map/ppermute | solution.py:47
  (11 other events, 124.6 us)
Sparse Core Ops, SparseCore 0:
  51.2 42.9 reduce-scatter.1

commit v5 on v4

--- a/solution.py
+++ b/solution.py
@@ -33,8 +33,17 @@
 HBM = pl.BlockSpec(memory_space=pltpu.HBM)
 
 
-def turned(distance, core):
+def swapped(bits):
+    return ((bits & 1) << 1) | (bits >> 1)
+
+
+def turned(index, core):
+    distance = swapped(index)
     return distance ^ ((distance & 1) * 2 * core)
+
+
+def index_of(distance, core):
+    return swapped(distance ^ ((distance & 1) * 2 * core))
 
 
 def along(stride):
@@ -229,7 +238,7 @@
         ins, outs = refs[:RING], refs[RING:]
         y, z, core = my_place()
         for distance in range(RING):
-            wanted = turned(map_ref[RING * y + (z ^ turned(distance, core))] ^ y, core)
+            wanted = index_of(map_ref[RING * y + (z ^ turned(distance, core))] ^ y, core)
             for step in range(RING):
 
                 @pl.when(wanted == step)

time: 111 us -> 107 us (0.964)
  waiting for transfers between devices: 27.1 us -> 19.4 us
  starting transfers between devices: 36.5 us -> 40 us
    ppermute x24, waiting for transfers between devices: 27.1 us -> 19.4 us  [move(): return lax.ppermute(value, ('slot', 'shard'), pairs)]
    ppermute x24, starting transfers between devices: 36.5 us -> 39.9 us  [move(): return lax.ppermute(value, ('slot', 'shard'), pairs)]
  transfers between devices with their start and end apart: 25 -> 25, of which waited for: 8 -> 10; matrix products, arithmetic and copies ran while one was open for 0% -> 0% of each run, Pallas kernels for 21% -> 21%
where the time goes in v5:
time: 107 us; the launch traced here: 106 us
  starting transfers between devices  40 us (37%)
  Pallas kernels  32.2 us (30%)
  waiting for transfers between devices  19.4 us (18%)
  between operations  14.9 us (14%)
    ppermute x24, starting transfers between devices, move(): return lax.ppermute(value, ('slot', 'shard'), pairs)  39.9 us
    ppermute x24, waiting for transfers between devices, move(): return lax.ppermute(value, ('slot', 'shard'), pairs)  19.4 us
    pallas_call x2, Pallas kernels, slot_grads(): pl.pallas_call(kernel, in_specs=[SMEM, HBM, HBM] + [ANY] * len(after), ou...  12.3 us
    pallas_call x1, Pallas kernels, act_terms(): pl.pallas_call(kernel, grid_spec=pltpu.PrefetchScalarGridSpec(num_scalar_...  10.1 us
    pallas_call x2, Pallas kernels, adam(): pl.pallas_call(kernel, grid=(1,), in_specs=[pl.BlockSpec((part, width), l...  3.01 us
    pallas_call x2, Pallas kernels, by_expert(): pl.pallas_call(kernel, in_specs=[SMEM] + [VMEM] * RING + [SMEM] * len(aft...  2.8 us
    pallas_call x2, Pallas kernels, put_rows(): pl.pallas_call(kernel, in_specs=[VMEM] * RING + [ANY] * len(earlier) + [S...  2.52 us
  transfers between devices with their start and end apart: 25, of which 10 were waited for; matrix products, arithmetic and copies ran while one was open for 0% of the time, Pallas kernels for 21%

profile of v5, /device:TPU:0, one launch (start us, length us, event | category | flops | bytes accessed | tf_op | source)
XLA Modules:
  0.0 106.5 jit_solution(16889260162460650362)
XLA Ops:
  7.9 6.1 %slot_grads.2 = (bf16[128,896]{1,0:T(8,128)(2,1)}, bf16[128,896]{1,0:T(8,128)(2,1)}, bf16[128,896]{1,0:T(8,128)(2,1)}, bf16[128,896]{1,0:T(8,128)(2,1)}) custom-call(s32[1]{0:T(128)S(6)} %copy.22.count_ref, bf16[3072,1024]{1,0:T(8,128)(2,1)} %bitcast.6, bf16[3072,896]{1,0:T(8,128)(2,1)} %bitcast.8), custom_call_target="tpu_custom_call" | custom-call | flops 10000000000 | bytes 14000000 | tf_op jit(solution)/shard_map/slot_grads/pallas_call | solution.py:115
  13.9 4.0 %collective-permute-start.3 = (bf16[128,896]{1,0:T(8,128)(2,1)}, bf16[128,896]{1,0:T(8,128)(2,1)S(1)}, u32[]{:S(2)}, u32[]{:S(2)}) collective-permute-start(bf16[128,896]{1,0:T(8,128)(2,1)} %get-tuple-element.47), channel_id=1, source_target_pairs={{0,16},{1,17},{2,18},{3,19},{4,20},{5,21},{6,22},{7,23},{8,24},{9,... | collective-permute-start | bytes 688136 | tf_op jit(solution)/shard_map/ppermute | solution.py:56
  19.0 6.2 %slot_grads.3 = (bf16[128,896]{1,0:T(8,128)(2,1)}, bf16[128,896]{1,0:T(8,128)(2,1)}, bf16[128,896]{1,0:T(8,128)(2,1)}, bf16[128,896]{1,0:T(8,128)(2,1)}) custom-call(s32[1]{0:T(128)S(6)} %copy.22.count_ref, bf16[3072,1024]{1,0:T(8,128)(2,1)} %bitcast.7, bf16[3072,896]{1,0:T(8,128)(2,1)} %bitcast.9, bf16[128,896]{1,0:T(8,128)(2,1)} %get-tuple-element.42.rest_0_.refs_0_), custom_call_target="tpu_custom_call" | custom-call | flops 10000000000 | bytes 14000000 | tf_op jit(solution)/shard_map/slot_grads/pallas_call | solution.py:115
  25.2 3.1 %collective-permute-start = (bf16[128,896]{1,0:T(8,128)(2,1)}, bf16[128,896]{1,0:T(8,128)(2,1)S(1)}, u32[]{:S(2)}, u32[]{:S(2)}) collective-permute-start(bf16[128,896]{1,0:T(8,128)(2,1)} %get-tuple-element.44), channel_id=1, source_target_pairs={{0,16},{1,17},{2,18},{3,19},{4,20},{5,21},{6,22},{7,23},{8,24},{9,... | collective-permute-start | bytes 688136 | tf_op jit(solution)/shard_map/ppermute | solution.py:56
  31.4 3.3 %collective-permute-start.6 = (bf16[128,896]{1,0:T(8,128)(2,1)S(1)}, bf16[128,896]{1,0:T(8,128)(2,1)S(1)}, u32[]{:S(2)}, u32[]{:S(2)}) collective-permute-start(bf16[128,896]{1,0:T(8,128)(2,1)S(1)} %get-tuple-element.52), channel_id=1, source_target_pairs={{0,64},{1,65},{2,66},{3,67},{4,68},{5,69},{6,70},{7,71},{8,72},{9,... | collective-permute-start | bytes 688136 | tf_op jit(solution)/shard_map/ppermute | solution.py:56
  35.4 2.6 %collective-permute-start.8 = (bf16[128,896]{1,0:T(8,128)(2,1)S(1)}, bf16[128,896]{1,0:T(8,128)(2,1)S(1)}, u32[]{:S(2)}, u32[]{:S(2)}) collective-permute-start(bf16[128,896]{1,0:T(8,128)(2,1)S(1)} %get-tuple-element.54), channel_id=1, source_target_pairs={{0,96},{1,33},{2,98},{3,35},{4,100},{5,37},{6,102},{7,39},{8,104},... | collective-permute-start | bytes 688136 | tf_op jit(solution)/shard_map/ppermute | solution.py:56
  38.0 10.1 %act_terms.1 = (bf16[8,3072,128]{2,1,0:T(8,128)(2,1)}, s32[1]{0:T(128)}) custom-call(s32[1]{0:T(128)S(6)} %copy.22.count_ref, bf16[3072,896]{1,0:T(8,128)(2,1)} %bitcast.10, bf16[1024,896]{1,0:T(8,128)(2,1)S(1)} %bitcast.4, bf16[128,896]{1,0:T(8,128)(2,1)S(1)} %get-tuple-element.50.rest_0_.refs_0_, bf16[128,896]{1,0:T(8,128)(2,1)S(1)} %collective-permute-done.rest_1_.refs_1_), custom_call_target="tpu_custom_call" | custom-call | flops 10000000000 | bytes 14000000 | tf_op jit(solution)/shard_map/act_terms/pallas_call | solution.py:149
  48.2 1.7 %by_expert.3 = (bf16[128,896]{1,0:T(8,128)(2,1)S(1)}, bf16[128,896]{1,0:T(8,128)(2,1)S(1)}, bf16[128,896]{1,0:T(8,128)(2,1)S(1)}, bf16[128,896]{1,0:T(8,128)(2,1)S(1)}) custom-call(s32[16]{0:T(128)S(1)} %copy-done.5, bf16[128,896]{1,0:T(8,128)(2,1)S(1)} %copy-done.4, bf16[128,896]{1,0:T(8,128)(2,1)S(1)} %collective-permute-done.rest_1_.refs_1_, ...), custom_call_target="tpu_custom_call" | custom-call | bytes 1024 | tf_op jit(solution)/shard_map/by_expert/pallas_call | solution.py:183
  49.9 1.5 %adam.2 = (f32[256,896]{1,0:T(8,128)}, f32[256,896]{1,0:T(8,128)}, f32[256,896]{1,0:T(8,128)}, bf16[128,896]{1,0:T(8,128)(2,1)S(1)}, s32[1]{0:T(128)}) custom-call(bf16[128,896]{1,0:T(8,128)(2,1)S(1)} %get-tuple-element.50.rest_0_.refs_0_, bf16[128,896]{1,0:T(8,128)(2,1)S(1)} %collective-permute-done.6.refs_5_.refs_1_, ...), custom_call_target="tpu_custom_call" | custom-call | bytes 1024 | tf_op jit(solution)/shard_map/adam/pallas_call | solution.py:223
  53.1 2.6 %collective-permute-start.11 = (bf16[128,896]{1,0:T(8,128)(2,1)S(1)}, bf16[128,896]{1,0:T(8,128)(2,1)S(1)}, u32[]{:S(2)}, u32[]{:S(2)}) collective-permute-start(bf16[128,896]{1,0:T(8,128)(2,1)S(1)} %get-tuple-element.58), channel_id=1, source_target_pairs={{0,96},{1,33},{2,98},{3,35},{4,100},{5,37},{6,102},{7,39},{8,104},... | collective-permute-start | bytes 688136 | tf_op jit(solution)/shard_map/ppermute | solution.py:56
  56.5 5.4 %collective-permute-done.9.refs_1_ = bf16[128,896]{1,0:T(8,128)(2,1)S(1)} collective-permute-done((bf16[128,896]{1,0:T(8,128)(2,1)}, bf16[128,896]{1,0:T(8,128)(2,1)S(1)}, u32[]{:S(2)}, u32[]{:S(2)}) %collective-permute-start.9) | collective-permute-done | bytes 229408 | tf_op jit(solution)/shard_map/ppermute | solution.py:56
  62.7 2.1 %collective-permute-done.10.refs_2_ = bf16[128,896]{1,0:T(8,128)(2,1)S(1)} collective-permute-done((bf16[128,896]{1,0:T(8,128)(2,1)}, bf16[128,896]{1,0:T(8,128)(2,1)S(1)}, u32[]{:S(2)}, u32[]{:S(2)}) %collective-permute-start.10) | collective-permute-done | bytes 229408 | tf_op jit(solution)/shard_map/ppermute | solution.py:56
  64.8 1.5 %adam.3 = (f32[256,896]{1,0:T(8,128)}, f32[256,896]{1,0:T(8,128)}, f32[256,896]{1,0:T(8,128)}, bf16[128,896]{1,0:T(8,128)(2,1)S(1)}) custom-call(bf16[128,896]{1,0:T(8,128)(2,1)S(1)} %get-tuple-element.55.refs_7_.refs_0_, bf16[128,896]{1,0:T(8,128)(2,1)S(1)} %collective-permute-done.9.refs_1_, ...), custom_call_target="tpu_custom_call", output_to_operand_aliasing={{0}: (7, {}), {1}: (8, {}), {2}: (9, {})} | custom-call | bytes 1024 | tf_op jit(solution)/shard_map/adam/pallas_call | solution.py:223
  66.3 3.1 %collective-permute-start.14 = (bf16[128,896]{1,0:T(8,128)(2,1)S(1)}, bf16[128,896]{1,0:T(8,128)(2,1)S(1)}, u32[]{:S(2)}, u32[]{:S(2)}) collective-permute-start(bf16[128,896]{1,0:T(8,128)(2,1)S(1)} %get-tuple-element.62.refs_0_), channel_id=1, source_target_pairs={{0,96},{1,33},{2,98},{3,35},{4,100},{5,37},{6,102},{7,39},{8,104},... | collective-permute-start | bytes 688136 | tf_op jit(solution)/shard_map/ppermute | solution.py:56
  69.5 1.6 %collective-permute-done.20.refs_3_ = bf16[128,896]{1,0:T(8,128)(2,1)S(1)} collective-permute-done((bf16[128,896]{1,0:T(8,128)(2,1)S(1)}, bf16[128,896]{1,0:T(8,128)(2,1)S(1)}, u32[]{:S(2)}, u32[]{:S(2)}) %collective-permute-start.20) | collective-permute-done | bytes 229408 | tf_op jit(solution)/shard_map/ppermute | solution.py:56
  71.1 2.6 %collective-permute-start.12 = (bf16[128,896]{1,0:T(8,128)(2,1)S(1)}, bf16[128,896]{1,0:T(8,128)(2,1)S(1)}, u32[]{:S(2)}, u32[]{:S(2)}) collective-permute-start(bf16[128,896]{1,0:T(8,128)(2,1)S(1)} %get-tuple-element.62.refs_0_), channel_id=1, source_target_pairs={{0,64},{1,65},{2,66},{3,67},{4,68},{5,69},{6,70},{7,71},{8,72},{9,... | collective-permute-start | bytes 688136 | tf_op jit(solution)/shard_map/ppermute | solution.py:56
  73.7 3.0 %collective-permute-done.18.refs_1_ = bf16[128,896]{1,0:T(8,128)(2,1)S(1)} collective-permute-done((bf16[128,896]{1,0:T(8,128)(2,1)S(1)}, bf16[128,896]{1,0:T(8,128)(2,1)S(1)}, u32[]{:S(2)}, u32[]{:S(2)}) %collective-permute-start.18) | collective-permute-done | bytes 229408 | tf_op jit(solution)/shard_map/ppermute | solution.py:56
  77.5 3.7 %collective-permute-start.21 = (bf16[128,896]{1,0:T(8,128)(2,1)S(1)}, bf16[128,896]{1,0:T(8,128)(2,1)S(1)}, u32[]{:S(2)}, u32[]{:S(2)}) collective-permute-start(bf16[128,896]{1,0:T(8,128)(2,1)S(1)} %get-tuple-element.69), channel_id=1, source_target_pairs={{0,16},{1,17},{2,18},{3,19},{4,20},{5,21},{6,22},{7,23},{8,24},{9,... | collective-permute-start | bytes 688136 | tf_op jit(solution)/shard_map/ppermute | solution.py:56
  83.7 2.8 %collective-permute-start.15 = (bf16[128,896]{1,0:T(8,128)(2,1)S(1)}, bf16[128,896]{1,0:T(8,128)(2,1)S(1)}, u32[]{:S(2)}, u32[]{:S(2)}) collective-permute-start(bf16[128,896]{1,0:T(8,128)(2,1)S(1)} %get-tuple-element.64), channel_id=1, source_target_pairs={{0,16},{1,17},{2,18},{3,19},{4,20},{5,21},{6,22},{7,23},{8,24},{9,... | collective-permute-start | bytes 688136 | tf_op jit(solution)/shard_map/ppermute | solution.py:56
  86.5 1.6 %collective-permute-start.16 = (bf16[128,896]{1,0:T(8,128)(2,1)S(1)}, bf16[128,896]{1,0:T(8,128)(2,1)S(1)}, u32[]{:S(2)}, u32[]{:S(2)}) collective-permute-start(bf16[128,896]{1,0:T(8,128)(2,1)S(1)} %get-tuple-element.65), channel_id=1, source_target_pairs={{0,8},{1,25},{2,10},{3,27},{4,12},{5,29},{6,14},{7,31},{8,0},{9,17... | collective-permute-start | bytes 688136 | tf_op jit(solution)/shard_map/ppermute | solution.py:56
  88.1 2.8 %collective-permute-start.17 = (bf16[128,896]{1,0:T(8,128)(2,1)S(1)}, bf16[128,896]{1,0:T(8,128)(2,1)S(1)}, u32[]{:S(2)}, u32[]{:S(2)}) collective-permute-start(bf16[128,896]{1,0:T(8,128)(2,1)S(1)} %get-tuple-element.66), channel_id=1, source_target_pairs={{0,24},{1,9},{2,26},{3,11},{4,28},{5,13},{6,30},{7,15},{8,16},{9,1... | collective-permute-start | bytes 688136 | tf_op jit(solution)/shard_map/ppermute | solution.py:56
  90.9 2.2 %collective-permute-done.22.refs_2_ = bf16[128,896]{1,0:T(8,128)(2,1)S(1)} collective-permute-done((bf16[128,896]{1,0:T(8,128)(2,1)S(1)}, bf16[128,896]{1,0:T(8,128)(2,1)S(1)}, u32[]{:S(2)}, u32[]{:S(2)}) %collective-permute-start.22) | collective-permute-done | bytes 229408 | tf_op jit(solution)/shard_map/ppermute | solution.py:56
  93.1 1.6 %put_rows.2.refs_4_ = bf16[1024,896]{1,0:T(8,128)(2,1)} custom-call(bf16[128,896]{1,0:T(8,128)(2,1)S(1)} %get-tuple-element.68.refs_0_, bf16[128,896]{1,0:T(8,128)(2,1)S(1)} %collective-permute-done.21.refs_1_, bf16[128,896]{1,0:T(8,128)(2,1)S(1)} %collective-permute-done.22.refs_2_, bf16[128,896]{1,0:T(8,128)(2,1)S(1)} %collective-permute-done.23.refs_3_, ...), custom_call_target="tpu_custom_call" | custom-call | bytes 1024 | tf_op jit(solution)/shard_map/put_rows/pallas_call | solution.py:276
  95.2 3.5 %collective-permute-done.16.refs_2_ = bf16[128,896]{1,0:T(8,128)(2,1)S(1)} collective-permute-done((bf16[128,896]{1,0:T(8,128)(2,1)S(1)}, bf16[128,896]{1,0:T(8,128)(2,1)S(1)}, u32[]{:S(2)}, u32[]{:S(2)}) %collective-permute-start.16) | collective-permute-done | bytes 229408 | tf_op jit(solution)/shard_map/ppermute | solution.py:56
  (58 shorter events, 12.8 us)
Async XLA Ops:
  7.2 92.5 %reduce-scatter.2.cloned.1.call-start = ((), (), s32[]{:S(2)}) async-start(), calls=%async_computation.1 | async-start | bytes 7077888 | tf_op jit(solution)/shard_map/reduce_scatter | solution.py:304
  13.9 15.5 %collective-permute-start.3 = (bf16[128,896]{1,0:T(8,128)(2,1)}, bf16[128,896]{1,0:T(8,128)(2,1)S(1)}, u32[]{:S(2)}, u32[]{:S(2)}) collective-permute-start(bf16[128,896]{1,0:T(8,128)(2,1)} %get-tuple-element.47), channel_id=1, source_target_pairs={{0,16},{1,17},{2,18},{3,19},{4,20},{5,21},{6,22},{7,23},{8,24},{9,... | collective-permute-start | bytes 688136 | tf_op jit(solution)/shard_map/ppermute | solution.py:56
  18.0 12.3 %collective-permute-start.4 = (bf16[128,896]{1,0:T(8,128)(2,1)}, bf16[128,896]{1,0:T(8,128)(2,1)S(1)}, u32[]{:S(2)}, u32[]{:S(2)}) collective-permute-start(bf16[128,896]{1,0:T(8,128)(2,1)} %get-tuple-element.48), channel_id=1, source_target_pairs={{0,8},{1,25},{2,10},{3,27},{4,12},{5,29},{6,14},{7,31},{8,0},{9,17... | collective-permute-start | bytes 688136 | tf_op jit(solution)/shard_map/ppermute | solution.py:56
  19.0 11.3 %collective-permute-start.5 = (bf16[128,896]{1,0:T(8,128)(2,1)}, bf16[128,896]{1,0:T(8,128)(2,1)S(1)}, u32[]{:S(2)}, u32[]{:S(2)}) collective-permute-start(bf16[128,896]{1,0:T(8,128)(2,1)} %get-tuple-element.49), channel_id=1, source_target_pairs={{0,24},{1,9},{2,26},{3,11},{4,28},{5,13},{6,30},{7,15},{8,16},{9,1... | collective-permute-start | bytes 688136 | tf_op jit(solution)/shard_map/ppermute | solution.py:56
  28.4 19.7 %collective-permute-start.1 = (bf16[128,896]{1,0:T(8,128)(2,1)}, bf16[128,896]{1,0:T(8,128)(2,1)S(1)}, u32[]{:S(2)}, u32[]{:S(2)}) collective-permute-start(bf16[128,896]{1,0:T(8,128)(2,1)} %get-tuple-element.45), channel_id=1, source_target_pairs={{0,8},{1,25},{2,10},{3,27},{4,12},{5,29},{6,14},{7,31},{8,0},{9,17... | collective-permute-start | bytes 688136 | tf_op jit(solution)/shard_map/ppermute | solution.py:56
  29.4 18.7 %collective-permute-start.2 = (bf16[128,896]{1,0:T(8,128)(2,1)}, bf16[128,896]{1,0:T(8,128)(2,1)S(1)}, u32[]{:S(2)}, u32[]{:S(2)}) collective-permute-start(bf16[128,896]{1,0:T(8,128)(2,1)} %get-tuple-element.46), channel_id=1, source_target_pairs={{0,24},{1,9},{2,26},{3,11},{4,28},{5,13},{6,30},{7,15},{8,16},{9,1... | collective-permute-start | bytes 688136 | tf_op jit(solution)/shard_map/ppermute | solution.py:56
  31.4 16.7 %collective-permute-start.6 = (bf16[128,896]{1,0:T(8,128)(2,1)S(1)}, bf16[128,896]{1,0:T(8,128)(2,1)S(1)}, u32[]{:S(2)}, u32[]{:S(2)}) collective-permute-start(bf16[128,896]{1,0:T(8,128)(2,1)S(1)} %get-tuple-element.52), channel_id=1, source_target_pairs={{0,64},{1,65},{2,66},{3,67},{4,68},{5,69},{6,70},{7,71},{8,72},{9,... | collective-permute-start | bytes 688136 | tf_op jit(solution)/shard_map/ppermute | solution.py:56
  34.7 13.5 %collective-permute-start.7 = (bf16[128,896]{1,0:T(8,128)(2,1)S(1)}, bf16[128,896]{1,0:T(8,128)(2,1)S(1)}, u32[]{:S(2)}, u32[]{:S(2)}) collective-permute-start(bf16[128,896]{1,0:T(8,128)(2,1)S(1)} %get-tuple-element.53), channel_id=1, source_target_pairs={{0,32},{1,97},{2,34},{3,99},{4,36},{5,101},{6,38},{7,103},{8,40},{... | collective-permute-start | bytes 688136 | tf_op jit(solution)/shard_map/ppermute | solution.py:56
  35.4 12.8 %collective-permute-start.8 = (bf16[128,896]{1,0:T(8,128)(2,1)S(1)}, bf16[128,896]{1,0:T(8,128)(2,1)S(1)}, u32[]{:S(2)}, u32[]{:S(2)}) collective-permute-start(bf16[128,896]{1,0:T(8,128)(2,1)S(1)} %get-tuple-element.54), channel_id=1, source_target_pairs={{0,96},{1,33},{2,98},{3,35},{4,100},{5,37},{6,102},{7,39},{8,104},... | collective-permute-start | bytes 688136 | tf_op jit(solution)/shard_map/ppermute | solution.py:56
  51.5 10.3 %collective-permute-start.9 = (bf16[128,896]{1,0:T(8,128)(2,1)}, bf16[128,896]{1,0:T(8,128)(2,1)S(1)}, u32[]{:S(2)}, u32[]{:S(2)}) collective-permute-start(bf16[128,896]{1,0:T(8,128)(2,1)} %copy-done.9), channel_id=1, source_target_pairs={{0,64},{1,65},{2,66},{3,67},{4,68},{5,69},{6,70},{7,71},{8,72},{9,... | collective-permute-start | bytes 688136 | tf_op jit(solution)/shard_map/ppermute | solution.py:56
  52.4 12.3 %collective-permute-start.10 = (bf16[128,896]{1,0:T(8,128)(2,1)}, bf16[128,896]{1,0:T(8,128)(2,1)S(1)}, u32[]{:S(2)}, u32[]{:S(2)}) collective-permute-start(bf16[128,896]{1,0:T(8,128)(2,1)} %copy-done.8), channel_id=1, source_target_pairs={{0,32},{1,97},{2,34},{3,99},{4,36},{5,101},{6,38},{7,103},{8,40},{... | collective-permute-start | bytes 688136 | tf_op jit(solution)/shard_map/ppermute | solution.py:56
  53.1 11.7 %collective-permute-start.11 = (bf16[128,896]{1,0:T(8,128)(2,1)S(1)}, bf16[128,896]{1,0:T(8,128)(2,1)S(1)}, u32[]{:S(2)}, u32[]{:S(2)}) collective-permute-start(bf16[128,896]{1,0:T(8,128)(2,1)S(1)} %get-tuple-element.58), channel_id=1, source_target_pairs={{0,96},{1,33},{2,98},{3,35},{4,100},{5,37},{6,102},{7,39},{8,104},... | collective-permute-start | bytes 688136 | tf_op jit(solution)/shard_map/ppermute | solution.py:56
  55.7 15.4 %collective-permute-start.20 = (bf16[128,896]{1,0:T(8,128)(2,1)S(1)}, bf16[128,896]{1,0:T(8,128)(2,1)S(1)}, u32[]{:S(2)}, u32[]{:S(2)}) collective-permute-start(bf16[128,896]{1,0:T(8,128)(2,1)S(1)} %get-tuple-element.67.refs_0_), channel_id=1, source_target_pairs={{0,96},{1,33},{2,98},{3,35},{4,100},{5,37},{6,102},{7,39},{8,104},... | collective-permute-start | bytes 688136 | tf_op jit(solution)/shard_map/ppermute | solution.py:56
  56.3 17.4 %collective-permute-start.19 = (bf16[128,896]{1,0:T(8,128)(2,1)S(1)}, bf16[128,896]{1,0:T(8,128)(2,1)S(1)}, u32[]{:S(2)}, u32[]{:S(2)}) collective-permute-start(bf16[128,896]{1,0:T(8,128)(2,1)S(1)} %get-tuple-element.67.refs_0_), channel_id=1, source_target_pairs={{0,32},{1,97},{2,34},{3,99},{4,36},{5,101},{6,38},{7,103},{8,40},{... | collective-permute-start | bytes 688136 | tf_op jit(solution)/shard_map/ppermute | solution.py:56
  61.9 14.8 %collective-permute-start.18 = (bf16[128,896]{1,0:T(8,128)(2,1)S(1)}, bf16[128,896]{1,0:T(8,128)(2,1)S(1)}, u32[]{:S(2)}, u32[]{:S(2)}) collective-permute-start(bf16[128,896]{1,0:T(8,128)(2,1)S(1)} %get-tuple-element.67.refs_0_), channel_id=1, source_target_pairs={{0,64},{1,65},{2,66},{3,67},{4,68},{5,69},{6,70},{7,71},{8,72},{9,... | collective-permute-start | bytes 688136 | tf_op jit(solution)/shard_map/ppermute | solution.py:56
  66.3 16.0 %collective-permute-start.14 = (bf16[128,896]{1,0:T(8,128)(2,1)S(1)}, bf16[128,896]{1,0:T(8,128)(2,1)S(1)}, u32[]{:S(2)}, u32[]{:S(2)}) collective-permute-start(bf16[128,896]{1,0:T(8,128)(2,1)S(1)} %get-tuple-element.62.refs_0_), channel_id=1, source_target_pairs={{0,96},{1,33},{2,98},{3,35},{4,100},{5,37},{6,102},{7,39},{8,104},... | collective-permute-start | bytes 688136 | tf_op jit(solution)/shard_map/ppermute | solution.py:56
  69.5 13.5 %collective-permute-start.13 = (bf16[128,896]{1,0:T(8,128)(2,1)S(1)}, bf16[128,896]{1,0:T(8,128)(2,1)S(1)}, u32[]{:S(2)}, u32[]{:S(2)}) collective-permute-start(bf16[128,896]{1,0:T(8,128)(2,1)S(1)} %get-tuple-element.62.refs_0_), channel_id=1, source_target_pairs={{0,32},{1,97},{2,34},{3,99},{4,36},{5,101},{6,38},{7,103},{8,40},{... | collective-permute-start | bytes 688136 | tf_op jit(solution)/shard_map/ppermute | solution.py:56
  71.1 11.9 %collective-permute-start.12 = (bf16[128,896]{1,0:T(8,128)(2,1)S(1)}, bf16[128,896]{1,0:T(8,128)(2,1)S(1)}, u32[]{:S(2)}, u32[]{:S(2)}) collective-permute-start(bf16[128,896]{1,0:T(8,128)(2,1)S(1)} %get-tuple-element.62.refs_0_), channel_id=1, source_target_pairs={{0,64},{1,65},{2,66},{3,67},{4,68},{5,69},{6,70},{7,71},{8,72},{9,... | collective-permute-start | bytes 688136 | tf_op jit(solution)/shard_map/ppermute | solution.py:56
  77.5 10.6 %collective-permute-start.21 = (bf16[128,896]{1,0:T(8,128)(2,1)S(1)}, bf16[128,896]{1,0:T(8,128)(2,1)S(1)}, u32[]{:S(2)}, u32[]{:S(2)}) collective-permute-start(bf16[128,896]{1,0:T(8,128)(2,1)S(1)} %get-tuple-element.69), channel_id=1, source_target_pairs={{0,16},{1,17},{2,18},{3,19},{4,20},{5,21},{6,22},{7,23},{8,24},{9,... | collective-permute-start | bytes 688136 | tf_op jit(solution)/shard_map/ppermute | solution.py:56
  81.2 11.8 %collective-permute-start.22 = (bf16[128,896]{1,0:T(8,128)(2,1)S(1)}, bf16[128,896]{1,0:T(8,128)(2,1)S(1)}, u32[]{:S(2)}, u32[]{:S(2)}) collective-permute-start(bf16[128,896]{1,0:T(8,128)(2,1)S(1)} %get-tuple-element.70), channel_id=1, source_target_pairs={{0,8},{1,25},{2,10},{3,27},{4,12},{5,29},{6,14},{7,31},{8,0},{9,17... | collective-permute-start | bytes 688136 | tf_op jit(solution)/shard_map/ppermute | solution.py:56
  82.3 10.8 %collective-permute-start.23 = (bf16[128,896]{1,0:T(8,128)(2,1)S(1)}, bf16[128,896]{1,0:T(8,128)(2,1)S(1)}, u32[]{:S(2)}, u32[]{:S(2)}) collective-permute-start(bf16[128,896]{1,0:T(8,128)(2,1)S(1)} %get-tuple-element.71), channel_id=1, source_target_pairs={{0,24},{1,9},{2,26},{3,11},{4,28},{5,13},{6,30},{7,15},{8,16},{9,1... | collective-permute-start | bytes 688136 | tf_op jit(solution)/shard_map/ppermute | solution.py:56
  83.7 11.5 %collective-permute-start.15 = (bf16[128,896]{1,0:T(8,128)(2,1)S(1)}, bf16[128,896]{1,0:T(8,128)(2,1)S(1)}, u32[]{:S(2)}, u32[]{:S(2)}) collective-permute-start(bf16[128,896]{1,0:T(8,128)(2,1)S(1)} %get-tuple-element.64), channel_id=1, source_target_pairs={{0,16},{1,17},{2,18},{3,19},{4,20},{5,21},{6,22},{7,23},{8,24},{9,... | collective-permute-start | bytes 688136 | tf_op jit(solution)/shard_map/ppermute | solution.py:56
  86.5 12.2 %collective-permute-start.16 = (bf16[128,896]{1,0:T(8,128)(2,1)S(1)}, bf16[128,896]{1,0:T(8,128)(2,1)S(1)}, u32[]{:S(2)}, u32[]{:S(2)}) collective-permute-start(bf16[128,896]{1,0:T(8,128)(2,1)S(1)} %get-tuple-element.65), channel_id=1, source_target_pairs={{0,8},{1,25},{2,10},{3,27},{4,12},{5,29},{6,14},{7,31},{8,0},{9,17... | collective-permute-start | bytes 688136 | tf_op jit(solution)/shard_map/ppermute | solution.py:56
  88.1 10.6 %collective-permute-start.17 = (bf16[128,896]{1,0:T(8,128)(2,1)S(1)}, bf16[128,896]{1,0:T(8,128)(2,1)S(1)}, u32[]{:S(2)}, u32[]{:S(2)}) collective-permute-start(bf16[128,896]{1,0:T(8,128)(2,1)S(1)} %get-tuple-element.66), channel_id=1, source_target_pairs={{0,24},{1,9},{2,26},{3,11},{4,28},{5,13},{6,30},{7,15},{8,16},{9,1... | collective-permute-start | bytes 688136 | tf_op jit(solution)/shard_map/ppermute | solution.py:56
  (11 other events, 126.2 us)
Sparse Core Ops, SparseCore 0:
  51.7 42.1 reduce-scatter.1

commit v6 on v5

--- a/solution.py
+++ b/solution.py
@@ -243,7 +243,7 @@
 
                 @pl.when(wanted == step)
                 def _(step=step, distance=distance):
-                    outs[distance][...] = ins[step][...]
+                    outs[distance][...] = ins[-step][...]
 
     shape = pieces[0].shape
     return pl.pallas_call(
@@ -305,7 +305,7 @@
     fresh = [exchange(move_y, [rows] * RING)]
     *state, rows = adam(1, late, (master, moment1, moment2), tuple(state))
     fresh.append(exchange(move_y, [rows] * RING))
-    wanted = [exchange(move_z, by_slot(next_map, pieces)) for pieces in fresh]
+    wanted = [exchange(move_z, by_slot(next_map, pieces[:1] + pieces[:0:-1])) for pieces in fresh]
     new_weight = put_rows(0, wanted[0], ff, (), (turn,))
     new_weight = put_rows(1, wanted[1], ff, (new_weight,))
     return (new_weight[None], *state, act_grads[None])

time: 107 us -> 107 us (level)
  transfers between devices with their start and end apart: 25 -> 25, of which waited for: 10 -> 9; matrix products, arithmetic and copies ran while one was open for 0% -> 0% of each run, Pallas kernels for 21% -> 21%
where the time goes in v6:
time: 107 us; the launch traced here: 106 us
  starting transfers between devices  39.4 us (37%)
  Pallas kernels  32.2 us (30%)
  waiting for transfers between devices  19.9 us (19%)
  between operations  14.9 us (14%)
    ppermute x24, starting transfers between devices, move(): return lax.ppermute(value, ('slot', 'shard'), pairs)  39.3 us
    ppermute x24, waiting for transfers between devices, move(): return lax.ppermute(value, ('slot', 'shard'), pairs)  19.9 us
    pallas_call x2, Pallas kernels, slot_grads(): pl.pallas_call(kernel, in_specs=[SMEM, HBM, HBM] + [ANY] * len(after), ou...  12.3 us
    pallas_call x1, Pallas kernels, act_terms(): pl.pallas_call(kernel, grid_spec=pltpu.PrefetchScalarGridSpec(num_scalar_...  10.1 us
    pallas_call x2, Pallas kernels, adam(): pl.pallas_call(kernel, grid=(1,), in_specs=[pl.BlockSpec((part, width), l...  3.01 us
    pallas_call x2, Pallas kernels, by_expert(): pl.pallas_call(kernel, in_specs=[SMEM] + [VMEM] * RING + [SMEM] * len(aft...  2.8 us
    pallas_call x2, Pallas kernels, put_rows(): pl.pallas_call(kernel, in_specs=[VMEM] * RING + [ANY] * len(earlier) + [S...  2.52 us
  transfers between devices with their start and end apart: 25, of which 9 were waited for; matrix products, arithmetic and copies ran while one was open for 0% of the time, Pallas kernels for 21%

profile of v6, /device:TPU:0, one launch (start us, length us, event | category | flops | bytes accessed | tf_op | source)
XLA Modules:
  0.0 106.4 jit_solution(5107044505084633268)
XLA Ops:
  7.9 6.1 %slot_grads.2 = (bf16[128,896]{1,0:T(8,128)(2,1)}, bf16[128,896]{1,0:T(8,128)(2,1)}, bf16[128,896]{1,0:T(8,128)(2,1)}, bf16[128,896]{1,0:T(8,128)(2,1)}) custom-call(s32[1]{0:T(128)S(6)} %copy.22.count_ref, bf16[3072,1024]{1,0:T(8,128)(2,1)} %bitcast.6, bf16[3072,896]{1,0:T(8,128)(2,1)} %bitcast.8), custom_call_target="tpu_custom_call" | custom-call | flops 10000000000 | bytes 14000000 | tf_op jit(solution)/shard_map/slot_grads/pallas_call | solution.py:115
  13.9 4.0 %collective-permute-start.3 = (bf16[128,896]{1,0:T(8,128)(2,1)}, bf16[128,896]{1,0:T(8,128)(2,1)S(1)}, u32[]{:S(2)}, u32[]{:S(2)}) collective-permute-start(bf16[128,896]{1,0:T(8,128)(2,1)} %get-tuple-element.47), channel_id=1, source_target_pairs={{0,16},{1,17},{2,18},{3,19},{4,20},{5,21},{6,22},{7,23},{8,24},{9,... | collective-permute-start | bytes 688136 | tf_op jit(solution)/shard_map/ppermute | solution.py:56
  19.0 6.2 %slot_grads.3 = (bf16[128,896]{1,0:T(8,128)(2,1)}, bf16[128,896]{1,0:T(8,128)(2,1)}, bf16[128,896]{1,0:T(8,128)(2,1)}, bf16[128,896]{1,0:T(8,128)(2,1)}) custom-call(s32[1]{0:T(128)S(6)} %copy.22.count_ref, bf16[3072,1024]{1,0:T(8,128)(2,1)} %bitcast.7, bf16[3072,896]{1,0:T(8,128)(2,1)} %bitcast.9, bf16[128,896]{1,0:T(8,128)(2,1)} %get-tuple-element.42.rest_0_.refs_0_), custom_call_target="tpu_custom_call" | custom-call | flops 10000000000 | bytes 14000000 | tf_op jit(solution)/shard_map/slot_grads/pallas_call | solution.py:115
  25.2 3.1 %collective-permute-start = (bf16[128,896]{1,0:T(8,128)(2,1)}, bf16[128,896]{1,0:T(8,128)(2,1)S(1)}, u32[]{:S(2)}, u32[]{:S(2)}) collective-permute-start(bf16[128,896]{1,0:T(8,128)(2,1)} %get-tuple-element.44), channel_id=1, source_target_pairs={{0,16},{1,17},{2,18},{3,19},{4,20},{5,21},{6,22},{7,23},{8,24},{9,... | collective-permute-start | bytes 688136 | tf_op jit(solution)/shard_map/ppermute | solution.py:56
  31.4 3.3 %collective-permute-start.6 = (bf16[128,896]{1,0:T(8,128)(2,1)S(1)}, bf16[128,896]{1,0:T(8,128)(2,1)S(1)}, u32[]{:S(2)}, u32[]{:S(2)}) collective-permute-start(bf16[128,896]{1,0:T(8,128)(2,1)S(1)} %get-tuple-element.52), channel_id=1, source_target_pairs={{0,64},{1,65},{2,66},{3,67},{4,68},{5,69},{6,70},{7,71},{8,72},{9,... | collective-permute-start | bytes 688136 | tf_op jit(solution)/shard_map/ppermute | solution.py:56
  35.4 2.6 %collective-permute-start.8 = (bf16[128,896]{1,0:T(8,128)(2,1)S(1)}, bf16[128,896]{1,0:T(8,128)(2,1)S(1)}, u32[]{:S(2)}, u32[]{:S(2)}) collective-permute-start(bf16[128,896]{1,0:T(8,128)(2,1)S(1)} %get-tuple-element.54), channel_id=1, source_target_pairs={{0,96},{1,33},{2,98},{3,35},{4,100},{5,37},{6,102},{7,39},{8,104},... | collective-permute-start | bytes 688136 | tf_op jit(solution)/shard_map/ppermute | solution.py:56
  38.0 10.1 %act_terms.1 = (bf16[8,3072,128]{2,1,0:T(8,128)(2,1)}, s32[1]{0:T(128)}) custom-call(s32[1]{0:T(128)S(6)} %copy.22.count_ref, bf16[3072,896]{1,0:T(8,128)(2,1)} %bitcast.10, bf16[1024,896]{1,0:T(8,128)(2,1)S(1)} %bitcast.4, bf16[128,896]{1,0:T(8,128)(2,1)S(1)} %get-tuple-element.50.rest_0_.refs_0_, bf16[128,896]{1,0:T(8,128)(2,1)S(1)} %collective-permute-done.rest_1_.refs_1_), custom_call_target="tpu_custom_call" | custom-call | flops 10000000000 | bytes 14000000 | tf_op jit(solution)/shard_map/act_terms/pallas_call | solution.py:149
  48.2 1.7 %by_expert.3 = (bf16[128,896]{1,0:T(8,128)(2,1)S(1)}, bf16[128,896]{1,0:T(8,128)(2,1)S(1)}, bf16[128,896]{1,0:T(8,128)(2,1)S(1)}, bf16[128,896]{1,0:T(8,128)(2,1)S(1)}) custom-call(s32[16]{0:T(128)S(1)} %copy-done.5, bf16[128,896]{1,0:T(8,128)(2,1)S(1)} %copy-done.4, bf16[128,896]{1,0:T(8,128)(2,1)S(1)} %collective-permute-done.rest_1_.refs_1_, ...), custom_call_target="tpu_custom_call" | custom-call | bytes 1024 | tf_op jit(solution)/shard_map/by_expert/pallas_call | solution.py:183
  49.9 1.5 %adam.2 = (f32[256,896]{1,0:T(8,128)}, f32[256,896]{1,0:T(8,128)}, f32[256,896]{1,0:T(8,128)}, bf16[128,896]{1,0:T(8,128)(2,1)S(1)}, s32[1]{0:T(128)}) custom-call(bf16[128,896]{1,0:T(8,128)(2,1)S(1)} %get-tuple-element.50.rest_0_.refs_0_, bf16[128,896]{1,0:T(8,128)(2,1)S(1)} %collective-permute-done.6.refs_5_.refs_1_, ...), custom_call_target="tpu_custom_call" | custom-call | bytes 1024 | tf_op jit(solution)/shard_map/adam/pallas_call | solution.py:223
  53.1 2.6 %collective-permute-start.11 = (bf16[128,896]{1,0:T(8,128)(2,1)S(1)}, bf16[128,896]{1,0:T(8,128)(2,1)S(1)}, u32[]{:S(2)}, u32[]{:S(2)}) collective-permute-start(bf16[128,896]{1,0:T(8,128)(2,1)S(1)} %get-tuple-element.58), channel_id=1, source_target_pairs={{0,96},{1,33},{2,98},{3,35},{4,100},{5,37},{6,102},{7,39},{8,104},... | collective-permute-start | bytes 688136 | tf_op jit(solution)/shard_map/ppermute | solution.py:56
  57.2 4.8 %collective-permute-done.9.refs_1_ = bf16[128,896]{1,0:T(8,128)(2,1)S(1)} collective-permute-done((bf16[128,896]{1,0:T(8,128)(2,1)}, bf16[128,896]{1,0:T(8,128)(2,1)S(1)}, u32[]{:S(2)}, u32[]{:S(2)}) %collective-permute-start.9) | collective-permute-done | bytes 229408 | tf_op jit(solution)/shard_map/ppermute | solution.py:56
  62.6 2.2 %collective-permute-done.10.refs_2_ = bf16[128,896]{1,0:T(8,128)(2,1)S(1)} collective-permute-done((bf16[128,896]{1,0:T(8,128)(2,1)}, bf16[128,896]{1,0:T(8,128)(2,1)S(1)}, u32[]{:S(2)}, u32[]{:S(2)}) %collective-permute-start.10) | collective-permute-done | bytes 229408 | tf_op jit(solution)/shard_map/ppermute | solution.py:56
  64.8 2.8 %collective-permute-done.11.refs_3_ = bf16[128,896]{1,0:T(8,128)(2,1)S(1)} collective-permute-done((bf16[128,896]{1,0:T(8,128)(2,1)S(1)}, bf16[128,896]{1,0:T(8,128)(2,1)S(1)}, u32[]{:S(2)}, u32[]{:S(2)}) %collective-permute-start.11) | collective-permute-done | bytes 229408 | tf_op jit(solution)/shard_map/ppermute | solution.py:56
  67.6 1.5 %adam.3 = (f32[256,896]{1,0:T(8,128)}, f32[256,896]{1,0:T(8,128)}, f32[256,896]{1,0:T(8,128)}, bf16[128,896]{1,0:T(8,128)(2,1)S(1)}) custom-call(bf16[128,896]{1,0:T(8,128)(2,1)S(1)} %get-tuple-element.55.refs_7_.refs_0_, bf16[128,896]{1,0:T(8,128)(2,1)S(1)} %collective-permute-done.9.refs_1_, ...), custom_call_target="tpu_custom_call", output_to_operand_aliasing={{0}: (7, {}), {1}: (8, {}), {2}: (9, {})} | custom-call | bytes 1024 | tf_op jit(solution)/shard_map/adam/pallas_call | solution.py:223
  69.1 1.8 %collective-permute-start.14 = (bf16[128,896]{1,0:T(8,128)(2,1)S(1)}, bf16[128,896]{1,0:T(8,128)(2,1)S(1)}, u32[]{:S(2)}, u32[]{:S(2)}) collective-permute-start(bf16[128,896]{1,0:T(8,128)(2,1)S(1)} %get-tuple-element.62.refs_0_), channel_id=1, source_target_pairs={{0,64},{1,65},{2,66},{3,67},{4,68},{5,69},{6,70},{7,71},{8,72},{9,... | collective-permute-start | bytes 688136 | tf_op jit(solution)/shard_map/ppermute | solution.py:56
  70.9 4.0 %collective-permute-start.13 = (bf16[128,896]{1,0:T(8,128)(2,1)S(1)}, bf16[128,896]{1,0:T(8,128)(2,1)S(1)}, u32[]{:S(2)}, u32[]{:S(2)}) collective-permute-start(bf16[128,896]{1,0:T(8,128)(2,1)S(1)} %get-tuple-element.62.refs_0_), channel_id=1, source_target_pairs={{0,32},{1,97},{2,34},{3,99},{4,36},{5,101},{6,38},{7,103},{8,40},{... | collective-permute-start | bytes 688136 | tf_op jit(solution)/shard_map/ppermute | solution.py:56
  74.9 2.5 %collective-permute-done.18.refs_1_ = bf16[128,896]{1,0:T(8,128)(2,1)S(1)} collective-permute-done((bf16[128,896]{1,0:T(8,128)(2,1)S(1)}, bf16[128,896]{1,0:T(8,128)(2,1)S(1)}, u32[]{:S(2)}, u32[]{:S(2)}) %collective-permute-start.18) | collective-permute-done | bytes 229408 | tf_op jit(solution)/shard_map/ppermute | solution.py:56
  78.1 3.3 %collective-permute-start.21 = (bf16[128,896]{1,0:T(8,128)(2,1)S(1)}, bf16[128,896]{1,0:T(8,128)(2,1)S(1)}, u32[]{:S(2)}, u32[]{:S(2)}) collective-permute-start(bf16[128,896]{1,0:T(8,128)(2,1)S(1)} %get-tuple-element.69), channel_id=1, source_target_pairs={{0,16},{1,17},{2,18},{3,19},{4,20},{5,21},{6,22},{7,23},{8,24},{9,... | collective-permute-start | bytes 688136 | tf_op jit(solution)/shard_map/ppermute | solution.py:56
  82.2 1.9 %collective-permute-start.23 = (bf16[128,896]{1,0:T(8,128)(2,1)S(1)}, bf16[128,896]{1,0:T(8,128)(2,1)S(1)}, u32[]{:S(2)}, u32[]{:S(2)}) collective-permute-start(bf16[128,896]{1,0:T(8,128)(2,1)S(1)} %get-tuple-element.71), channel_id=1, source_target_pairs={{0,24},{1,9},{2,26},{3,11},{4,28},{5,13},{6,30},{7,15},{8,16},{9,1... | collective-permute-start | bytes 688136 | tf_op jit(solution)/shard_map/ppermute | solution.py:56
  84.9 1.5 %collective-permute-start.15 = (bf16[128,896]{1,0:T(8,128)(2,1)S(1)}, bf16[128,896]{1,0:T(8,128)(2,1)S(1)}, u32[]{:S(2)}, u32[]{:S(2)}) collective-permute-start(bf16[128,896]{1,0:T(8,128)(2,1)S(1)} %get-tuple-element.64), channel_id=1, source_target_pairs={{0,16},{1,17},{2,18},{3,19},{4,20},{5,21},{6,22},{7,23},{8,24},{9,... | collective-permute-start | bytes 688136 | tf_op jit(solution)/shard_map/ppermute | solution.py:56
  88.2 2.7 %collective-permute-start.17 = (bf16[128,896]{1,0:T(8,128)(2,1)S(1)}, bf16[128,896]{1,0:T(8,128)(2,1)S(1)}, u32[]{:S(2)}, u32[]{:S(2)}) collective-permute-start(bf16[128,896]{1,0:T(8,128)(2,1)S(1)} %get-tuple-element.66), channel_id=1, source_target_pairs={{0,24},{1,9},{2,26},{3,11},{4,28},{5,13},{6,30},{7,15},{8,16},{9,1... | collective-permute-start | bytes 688136 | tf_op jit(solution)/shard_map/ppermute | solution.py:56
  90.9 2.2 %collective-permute-done.22.refs_2_ = bf16[128,896]{1,0:T(8,128)(2,1)S(1)} collective-permute-done((bf16[128,896]{1,0:T(8,128)(2,1)S(1)}, bf16[128,896]{1,0:T(8,128)(2,1)S(1)}, u32[]{:S(2)}, u32[]{:S(2)}) %collective-permute-start.22) | collective-permute-done | bytes 229408 | tf_op jit(solution)/shard_map/ppermute | solution.py:56
  93.0 1.6 %put_rows.2.refs_4_ = bf16[1024,896]{1,0:T(8,128)(2,1)} custom-call(bf16[128,896]{1,0:T(8,128)(2,1)S(1)} %get-tuple-element.68.refs_0_, bf16[128,896]{1,0:T(8,128)(2,1)S(1)} %collective-permute-done.21.refs_1_, bf16[128,896]{1,0:T(8,128)(2,1)S(1)} %collective-permute-done.22.refs_2_, bf16[128,896]{1,0:T(8,128)(2,1)S(1)} %collective-permute-done.23.refs_3_, ...), custom_call_target="tpu_custom_call" | custom-call | bytes 1024 | tf_op jit(solution)/shard_map/put_rows/pallas_call | solution.py:276
  95.2 3.3 %collective-permute-done.16.refs_2_ = bf16[128,896]{1,0:T(8,128)(2,1)S(1)} collective-permute-done((bf16[128,896]{1,0:T(8,128)(2,1)S(1)}, bf16[128,896]{1,0:T(8,128)(2,1)S(1)}, u32[]{:S(2)}, u32[]{:S(2)}) %collective-permute-start.16) | collective-permute-done | bytes 229408 | tf_op jit(solution)/shard_map/ppermute | solution.py:56
  (58 shorter events, 14.1 us)
Async XLA Ops:
  7.2 92.4 %reduce-scatter.2.cloned.1.call-start = ((), (), s32[]{:S(2)}) async-start(), calls=%async_computation.1 | async-start | bytes 7077888 | tf_op jit(solution)/shard_map/reduce_scatter | solution.py:304
  13.9 15.5 %collective-permute-start.3 = (bf16[128,896]{1,0:T(8,128)(2,1)}, bf16[128,896]{1,0:T(8,128)(2,1)S(1)}, u32[]{:S(2)}, u32[]{:S(2)}) collective-permute-start(bf16[128,896]{1,0:T(8,128)(2,1)} %get-tuple-element.47), channel_id=1, source_target_pairs={{0,16},{1,17},{2,18},{3,19},{4,20},{5,21},{6,22},{7,23},{8,24},{9,... | collective-permute-start | bytes 688136 | tf_op jit(solution)/shard_map/ppermute | solution.py:56
  18.0 12.3 %collective-permute-start.4 = (bf16[128,896]{1,0:T(8,128)(2,1)}, bf16[128,896]{1,0:T(8,128)(2,1)S(1)}, u32[]{:S(2)}, u32[]{:S(2)}) collective-permute-start(bf16[128,896]{1,0:T(8,128)(2,1)} %get-tuple-element.48), channel_id=1, source_target_pairs={{0,8},{1,25},{2,10},{3,27},{4,12},{5,29},{6,14},{7,31},{8,0},{9,17... | collective-permute-start | bytes 688136 | tf_op jit(solution)/shard_map/ppermute | solution.py:56
  19.0 11.3 %collective-permute-start.5 = (bf16[128,896]{1,0:T(8,128)(2,1)}, bf16[128,896]{1,0:T(8,128)(2,1)S(1)}, u32[]{:S(2)}, u32[]{:S(2)}) collective-permute-start(bf16[128,896]{1,0:T(8,128)(2,1)} %get-tuple-element.49), channel_id=1, source_target_pairs={{0,24},{1,9},{2,26},{3,11},{4,28},{5,13},{6,30},{7,15},{8,16},{9,1... | collective-permute-start | bytes 688136 | tf_op jit(solution)/shard_map/ppermute | solution.py:56
  25.2 10.1 %collective-permute-start = (bf16[128,896]{1,0:T(8,128)(2,1)}, bf16[128,896]{1,0:T(8,128)(2,1)S(1)}, u32[]{:S(2)}, u32[]{:S(2)}) collective-permute-start(bf16[128,896]{1,0:T(8,128)(2,1)} %get-tuple-element.44), channel_id=1, source_target_pairs={{0,16},{1,17},{2,18},{3,19},{4,20},{5,21},{6,22},{7,23},{8,24},{9,... | collective-permute-start | bytes 688136 | tf_op jit(solution)/shard_map/ppermute | solution.py:56
  28.4 19.7 %collective-permute-start.1 = (bf16[128,896]{1,0:T(8,128)(2,1)}, bf16[128,896]{1,0:T(8,128)(2,1)S(1)}, u32[]{:S(2)}, u32[]{:S(2)}) collective-permute-start(bf16[128,896]{1,0:T(8,128)(2,1)} %get-tuple-element.45), channel_id=1, source_target_pairs={{0,8},{1,25},{2,10},{3,27},{4,12},{5,29},{6,14},{7,31},{8,0},{9,17... | collective-permute-start | bytes 688136 | tf_op jit(solution)/shard_map/ppermute | solution.py:56
  29.4 18.7 %collective-permute-start.2 = (bf16[128,896]{1,0:T(8,128)(2,1)}, bf16[128,896]{1,0:T(8,128)(2,1)S(1)}, u32[]{:S(2)}, u32[]{:S(2)}) collective-permute-start(bf16[128,896]{1,0:T(8,128)(2,1)} %get-tuple-element.46), channel_id=1, source_target_pairs={{0,24},{1,9},{2,26},{3,11},{4,28},{5,13},{6,30},{7,15},{8,16},{9,1... | collective-permute-start | bytes 688136 | tf_op jit(solution)/shard_map/ppermute | solution.py:56
  31.4 16.7 %collective-permute-start.6 = (bf16[128,896]{1,0:T(8,128)(2,1)S(1)}, bf16[128,896]{1,0:T(8,128)(2,1)S(1)}, u32[]{:S(2)}, u32[]{:S(2)}) collective-permute-start(bf16[128,896]{1,0:T(8,128)(2,1)S(1)} %get-tuple-element.52), channel_id=1, source_target_pairs={{0,64},{1,65},{2,66},{3,67},{4,68},{5,69},{6,70},{7,71},{8,72},{9,... | collective-permute-start | bytes 688136 | tf_op jit(solution)/shard_map/ppermute | solution.py:56
  34.7 13.5 %collective-permute-start.7 = (bf16[128,896]{1,0:T(8,128)(2,1)S(1)}, bf16[128,896]{1,0:T(8,128)(2,1)S(1)}, u32[]{:S(2)}, u32[]{:S(2)}) collective-permute-start(bf16[128,896]{1,0:T(8,128)(2,1)S(1)} %get-tuple-element.53), channel_id=1, source_target_pairs={{0,32},{1,97},{2,34},{3,99},{4,36},{5,101},{6,38},{7,103},{8,40},{... | collective-permute-start | bytes 688136 | tf_op jit(solution)/shard_map/ppermute | solution.py:56
  35.4 12.8 %collective-permute-start.8 = (bf16[128,896]{1,0:T(8,128)(2,1)S(1)}, bf16[128,896]{1,0:T(8,128)(2,1)S(1)}, u32[]{:S(2)}, u32[]{:S(2)}) collective-permute-start(bf16[128,896]{1,0:T(8,128)(2,1)S(1)} %get-tuple-element.54), channel_id=1, source_target_pairs={{0,96},{1,33},{2,98},{3,35},{4,100},{5,37},{6,102},{7,39},{8,104},... | collective-permute-start | bytes 688136 | tf_op jit(solution)/shard_map/ppermute | solution.py:56
  51.5 10.4 %collective-permute-start.9 = (bf16[128,896]{1,0:T(8,128)(2,1)}, bf16[128,896]{1,0:T(8,128)(2,1)S(1)}, u32[]{:S(2)}, u32[]{:S(2)}) collective-permute-start(bf16[128,896]{1,0:T(8,128)(2,1)} %copy-done.9), channel_id=1, source_target_pairs={{0,64},{1,65},{2,66},{3,67},{4,68},{5,69},{6,70},{7,71},{8,72},{9,... | collective-permute-start | bytes 688136 | tf_op jit(solution)/shard_map/ppermute | solution.py:56
  52.4 12.4 %collective-permute-start.10 = (bf16[128,896]{1,0:T(8,128)(2,1)}, bf16[128,896]{1,0:T(8,128)(2,1)S(1)}, u32[]{:S(2)}, u32[]{:S(2)}) collective-permute-start(bf16[128,896]{1,0:T(8,128)(2,1)} %copy-done.8), channel_id=1, source_target_pairs={{0,32},{1,97},{2,34},{3,99},{4,36},{5,101},{6,38},{7,103},{8,40},{... | collective-permute-start | bytes 688136 | tf_op jit(solution)/shard_map/ppermute | solution.py:56
  53.1 14.5 %collective-permute-start.11 = (bf16[128,896]{1,0:T(8,128)(2,1)S(1)}, bf16[128,896]{1,0:T(8,128)(2,1)S(1)}, u32[]{:S(2)}, u32[]{:S(2)}) collective-permute-start(bf16[128,896]{1,0:T(8,128)(2,1)S(1)} %get-tuple-element.58), channel_id=1, source_target_pairs={{0,96},{1,33},{2,98},{3,35},{4,100},{5,37},{6,102},{7,39},{8,104},... | collective-permute-start | bytes 688136 | tf_op jit(solution)/shard_map/ppermute | solution.py:56
  55.7 19.2 %collective-permute-start.20 = (bf16[128,896]{1,0:T(8,128)(2,1)S(1)}, bf16[128,896]{1,0:T(8,128)(2,1)S(1)}, u32[]{:S(2)}, u32[]{:S(2)}) collective-permute-start(bf16[128,896]{1,0:T(8,128)(2,1)S(1)} %get-tuple-element.67.refs_0_), channel_id=1, source_target_pairs={{0,64},{1,65},{2,66},{3,67},{4,68},{5,69},{6,70},{7,71},{8,72},{9,... | collective-permute-start | bytes 688136 | tf_op jit(solution)/shard_map/ppermute | solution.py:56
  56.5 18.4 %collective-permute-start.19 = (bf16[128,896]{1,0:T(8,128)(2,1)S(1)}, bf16[128,896]{1,0:T(8,128)(2,1)S(1)}, u32[]{:S(2)}, u32[]{:S(2)}) collective-permute-start(bf16[128,896]{1,0:T(8,128)(2,1)S(1)} %get-tuple-element.67.refs_0_), channel_id=1, source_target_pairs={{0,32},{1,97},{2,34},{3,99},{4,36},{5,101},{6,38},{7,103},{8,40},{... | collective-permute-start | bytes 688136 | tf_op jit(solution)/shard_map/ppermute | solution.py:56
  62.0 15.4 %collective-permute-start.18 = (bf16[128,896]{1,0:T(8,128)(2,1)S(1)}, bf16[128,896]{1,0:T(8,128)(2,1)S(1)}, u32[]{:S(2)}, u32[]{:S(2)}) collective-permute-start(bf16[128,896]{1,0:T(8,128)(2,1)S(1)} %get-tuple-element.67.refs_0_), channel_id=1, source_target_pairs={{0,96},{1,33},{2,98},{3,35},{4,100},{5,37},{6,102},{7,39},{8,104},... | collective-permute-start | bytes 688136 | tf_op jit(solution)/shard_map/ppermute | solution.py:56
  69.1 13.1 %collective-permute-start.14 = (bf16[128,896]{1,0:T(8,128)(2,1)S(1)}, bf16[128,896]{1,0:T(8,128)(2,1)S(1)}, u32[]{:S(2)}, u32[]{:S(2)}) collective-permute-start(bf16[128,896]{1,0:T(8,128)(2,1)S(1)} %get-tuple-element.62.refs_0_), channel_id=1, source_target_pairs={{0,64},{1,65},{2,66},{3,67},{4,68},{5,69},{6,70},{7,71},{8,72},{9,... | collective-permute-start | bytes 688136 | tf_op jit(solution)/shard_map/ppermute | solution.py:56
  70.9 13.2 %collective-permute-start.13 = (bf16[128,896]{1,0:T(8,128)(2,1)S(1)}, bf16[128,896]{1,0:T(8,128)(2,1)S(1)}, u32[]{:S(2)}, u32[]{:S(2)}) collective-permute-start(bf16[128,896]{1,0:T(8,128)(2,1)S(1)} %get-tuple-element.62.refs_0_), channel_id=1, source_target_pairs={{0,32},{1,97},{2,34},{3,99},{4,36},{5,101},{6,38},{7,103},{8,40},{... | collective-permute-start | bytes 688136 | tf_op jit(solution)/shard_map/ppermute | solution.py:56
  78.1 10.0 %collective-permute-start.21 = (bf16[128,896]{1,0:T(8,128)(2,1)S(1)}, bf16[128,896]{1,0:T(8,128)(2,1)S(1)}, u32[]{:S(2)}, u32[]{:S(2)}) collective-permute-start(bf16[128,896]{1,0:T(8,128)(2,1)S(1)} %get-tuple-element.69), channel_id=1, source_target_pairs={{0,16},{1,17},{2,18},{3,19},{4,20},{5,21},{6,22},{7,23},{8,24},{9,... | collective-permute-start | bytes 688136 | tf_op jit(solution)/shard_map/ppermute | solution.py:56
  81.4 11.7 %collective-permute-start.22 = (bf16[128,896]{1,0:T(8,128)(2,1)S(1)}, bf16[128,896]{1,0:T(8,128)(2,1)S(1)}, u32[]{:S(2)}, u32[]{:S(2)}) collective-permute-start(bf16[128,896]{1,0:T(8,128)(2,1)S(1)} %get-tuple-element.70), channel_id=1, source_target_pairs={{0,8},{1,25},{2,10},{3,27},{4,12},{5,29},{6,14},{7,31},{8,0},{9,17... | collective-permute-start | bytes 688136 | tf_op jit(solution)/shard_map/ppermute | solution.py:56
  82.2 10.8 %collective-permute-start.23 = (bf16[128,896]{1,0:T(8,128)(2,1)S(1)}, bf16[128,896]{1,0:T(8,128)(2,1)S(1)}, u32[]{:S(2)}, u32[]{:S(2)}) collective-permute-start(bf16[128,896]{1,0:T(8,128)(2,1)S(1)} %get-tuple-element.71), channel_id=1, source_target_pairs={{0,24},{1,9},{2,26},{3,11},{4,28},{5,13},{6,30},{7,15},{8,16},{9,1... | collective-permute-start | bytes 688136 | tf_op jit(solution)/shard_map/ppermute | solution.py:56
  84.9 10.4 %collective-permute-start.15 = (bf16[128,896]{1,0:T(8,128)(2,1)S(1)}, bf16[128,896]{1,0:T(8,128)(2,1)S(1)}, u32[]{:S(2)}, u32[]{:S(2)}) collective-permute-start(bf16[128,896]{1,0:T(8,128)(2,1)S(1)} %get-tuple-element.64), channel_id=1, source_target_pairs={{0,16},{1,17},{2,18},{3,19},{4,20},{5,21},{6,22},{7,23},{8,24},{9,... | collective-permute-start | bytes 688136 | tf_op jit(solution)/shard_map/ppermute | solution.py:56
  86.4 12.2 %collective-permute-start.16 = (bf16[128,896]{1,0:T(8,128)(2,1)S(1)}, bf16[128,896]{1,0:T(8,128)(2,1)S(1)}, u32[]{:S(2)}, u32[]{:S(2)}) collective-permute-start(bf16[128,896]{1,0:T(8,128)(2,1)S(1)} %get-tuple-element.65), channel_id=1, source_target_pairs={{0,8},{1,25},{2,10},{3,27},{4,12},{5,29},{6,14},{7,31},{8,0},{9,17... | collective-permute-start | bytes 688136 | tf_op jit(solution)/shard_map/ppermute | solution.py:56
  88.2 10.4 %collective-permute-start.17 = (bf16[128,896]{1,0:T(8,128)(2,1)S(1)}, bf16[128,896]{1,0:T(8,128)(2,1)S(1)}, u32[]{:S(2)}, u32[]{:S(2)}) collective-permute-start(bf16[128,896]{1,0:T(8,128)(2,1)S(1)} %get-tuple-element.66), channel_id=1, source_target_pairs={{0,24},{1,9},{2,26},{3,11},{4,28},{5,13},{6,30},{7,15},{8,16},{9,1... | collective-permute-start | bytes 688136 | tf_op jit(solution)/shard_map/ppermute | solution.py:56
  (11 other events, 125.9 us)
Sparse Core Ops, SparseCore 0:
  51.7 42.1 reduce-scatter.1
